TPU v7x, 1024 devices: a whole 4x8x16 slice. The times are simulated.
1024 devices in a mesh: gx: 16 (over y_lo, x, core), gy: 64 (over y_hi, z).
Axes of the slice: x: 4, y: 8 (y_hi: 4, y_lo: 2; y = y_hi * 2 + y_lo), z: 16, core: 2. Of those that a mesh axis runs over, the one named last changes fastest.
Arguments:
- features: bfloat16 [32, 512, 8, 9, 128], P('gx', 'gy'), may hold values from -6 to 6
- positions: float32 [3, 32, 512, 8], P(None, 'gx', 'gy'), may hold values from 0.5 to 4.5, as said below
- occupied: int32 [32, 512, 8], P('gx', 'gy'), may hold values 0 or 1
- neighbours: int32 [32, 512, 8, 32], P('gx', 'gy'), may hold values from 0 to 72
- radial_weight: float32 [7, 8, 128], replicated, may hold values from -0.5 to 0.5
- mix_weight: bfloat16 [128, 128], replicated, may hold values from -0.5 to 0.5
- out_weight: float32 [128], replicated, may hold values from -1 to 1
Outputs:
- forces: float32 [3, 32, 512, 8], P(None, 'gx', 'gy')
- slot_energy_values: float32 [32, 512, 8], P('gx', 'gy')
- total_energy: float32 [], replicated
Inputs may be any that keep to these rules, and one draw needn't show every extreme that they name: `positions`: any two atoms that a list pairs are 1 angstrom or more apart, also across cells.
All inputs are finite; a program needn't handle non-finite values. No bound on the sum of `occupied` on one device may be relied on, other than what follows from the above.
Results may differ from a plain program's by a relative error of at most 0.0045.
Values may be sent and summed in bfloat16 or wider, within the bound.
No kernel may reach another device: no remote copies, remote signals or barrier semaphores. Data moves between devices by JAX's collectives and lax.ppermute only.
A program may use at most 32 MiB of HBM per device.

v0:
```python
import math

import jax
import jax.numpy as jnp
import numpy as np
from jax import lax
from jax.sharding import PartitionSpec as P

CHANNEL_COUNT = 128
NB = 8
NEIGHBOUR_SLOTS = 32
CELL_ATOM_SLOTS = 8


CELL_SIDE = 5.0
CUTOFF = 5.0
LEAD_PATHS = np.array([0, 3, 3, 3, 5, 5, 5, 5, 5], dtype=np.int32)
PLAIN_PATHS = np.array([4, 4, 4, 6, 6, 6, 6, 6], dtype=np.int32)
PAIRED_PATHS = np.array([1, 1, 1, 2, 2, 2, 2, 2], dtype=np.int32)


def with_halo(array, sides, width):
    for axis, dim in sides:
        size, length = (lax.axis_size(axis), array.shape[dim])
        up = [(i, (i + 1) % size) for i in range(size)]
        down = [(j, i) for i, j in up]
        last = lax.slice_in_dim(array, length - width, length, axis=dim)
        first = lax.slice_in_dim(array, 0, width, axis=dim)
        before = lax.ppermute(last, axis, up)
        after = lax.ppermute(first, axis, down)
        array = jnp.concatenate([before, array, after], axis=dim)
    return array


def edge_terms(vectors):
    dist_sq = jnp.sum(vectors * vectors, axis=-1)
    distance = jnp.sqrt(dist_sq)
    unit_x = vectors[..., 0] / distance
    unit_y = vectors[..., 1] / distance
    unit_z = vectors[..., 2] / distance
    envelope = jnp.square(jnp.maximum(1.0 - dist_sq / (CUTOFF * CUTOFF), 0.0))
    orders = jnp.arange(1, NB + 1).astype(jnp.float32)
    radial = (
        jnp.sin(orders * (math.pi / CUTOFF) * distance[..., None])
        / distance[..., None]
        * envelope[..., None]
    )
    root3 = math.sqrt(3.0)
    root15 = math.sqrt(15.0)
    root5 = math.sqrt(5.0)
    harmonics = jnp.stack(
        [
            jnp.ones_like(unit_x),
            root3 * unit_x,
            root3 * unit_y,
            root3 * unit_z,
            root15 * unit_x * unit_y,
            root15 * unit_y * unit_z,
            0.5 * root5 * (3.0 * unit_z * unit_z - 1.0),
            root15 * unit_x * unit_z,
            0.5 * root15 * (unit_x * unit_x - unit_y * unit_y),
        ],
        axis=-1,
    )
    return radial[..., :, None] * harmonics[..., None, :]


def block_step(neigh_rows, vectors, weights, own_occupied, radial_weight, mix_weight, out_weight):
    highest = lax.Precision.HIGHEST
    single = jnp.float32

    def geometry_of(edge_vectors):
        return edge_terms(edge_vectors) * weights[..., None, None]

    geometry, pull_back = jax.vjp(geometry_of, vectors)
    rounded = geometry.astype(jnp.bfloat16)
    lead_sum = jnp.einsum(
        "akbg,akc->abgc", rounded, neigh_rows[:, :, 0], preferred_element_type=single
    )
    plain_sum = jnp.einsum(
        "akb,akmc->abmc", rounded[..., 0], neigh_rows[:, :, 1:], preferred_element_type=single
    )
    paired_sum = jnp.einsum(
        "akbm,akmc->abmc", rounded[..., 1:], neigh_rows[:, :, 1:], preferred_element_type=single
    )
    w_lead = radial_weight[LEAD_PATHS]
    w_plain = radial_weight[PLAIN_PATHS]
    w_paired = radial_weight[PAIRED_PATHS]
    part_lead = jnp.einsum("abgc,gbc->agc", lead_sum, w_lead, precision=highest)
    part_plain = jnp.einsum("abmc,mbc->amc", plain_sum, w_plain, precision=highest)
    part_paired = jnp.einsum("abmc,mbc->ac", paired_sum, w_paired, precision=highest)
    messages = part_lead + jnp.concatenate([part_paired[:, None], part_plain], axis=1)
    messages = messages.astype(jnp.bfloat16)
    mixed_out = jnp.einsum("agc,cd->agd", messages, mix_weight, preferred_element_type=single)
    pre_act = mixed_out[:, 0] + jnp.sum(mixed_out[:, 1:] * mixed_out[:, 1:], axis=1)
    gate_value = jax.nn.sigmoid(pre_act)
    energy_values = own_occupied * jnp.dot(pre_act * gate_value, out_weight, precision=highest)
    grad_z = (
        own_occupied[:, None]
        * out_weight[None, :]
        * gate_value
        * (1.0 + pre_act * (1.0 - gate_value))
    )
    grad_mixed = jnp.concatenate(
        [grad_z[:, None], 2.0 * grad_z[:, None] * mixed_out[:, 1:]], axis=1
    )
    grad_mixed = grad_mixed.astype(jnp.bfloat16)
    grad_messages = jnp.einsum("agd,cd->agc", grad_mixed, mix_weight, preferred_element_type=single)
    grad_lead = (jnp.transpose(w_lead, (1, 0, 2))[None] * grad_messages[:, None]).astype(
        jnp.bfloat16
    )
    grad_plain = (jnp.transpose(w_plain, (1, 0, 2))[None] * grad_messages[:, None, 1:]).astype(
        jnp.bfloat16
    )
    grad_paired = (
        jnp.transpose(w_paired, (1, 0, 2))[None] * grad_messages[:, None, None, 0]
    ).astype(jnp.bfloat16)
    grad_all = jnp.einsum(
        "abgc,akc->akbg", grad_lead, neigh_rows[:, :, 0], preferred_element_type=single
    )
    grad_zero = jnp.einsum(
        "abmc,akmc->akb", grad_plain, neigh_rows[:, :, 1:], preferred_element_type=single
    )
    grad_rest = jnp.einsum(
        "abmc,akmc->akbm", grad_paired, neigh_rows[:, :, 1:], preferred_element_type=single
    )
    grad_geometry = grad_all + jnp.concatenate([grad_zero[..., None], grad_rest], axis=-1)
    edge_gradient = pull_back(grad_geometry)[0]
    return (energy_values, edge_gradient)


def on_device(features, positions, occupied, neighbours, radial_weight, mix_weight, out_weight):
    cells_x, cells_y, slot_count = occupied.shape
    atom_count = cells_x * cells_y * slot_count
    wide_cols = cells_y + 2
    packed = jnp.concatenate([positions, occupied.astype(jnp.float32)[None]], axis=0)
    ghost_cycle = with_halo(packed, (("gx", 1), ("gy", 2)), 1)
    cycle_rows = ghost_cycle.reshape(4, -1)
    whole_cycle = with_halo(features, (("gx", 0), ("gy", 1)), 1)
    row_table = whole_cycle.reshape(-1, 9, CHANNEL_COUNT)
    is_used = neighbours < 9 * CELL_ATOM_SLOTS
    cell_code = neighbours // CELL_ATOM_SLOTS
    horizontal_stride = jnp.where(is_used, cell_code // 3 - 1, 0)
    step_y = jnp.where(is_used, cell_code % 3 - 1, 0)
    slot_index = jnp.where(is_used, neighbours % CELL_ATOM_SLOTS, 0)
    place_x = jnp.arange(cells_x, dtype=jnp.int32)[:, None, None, None] + 1 + horizontal_stride
    place_y = jnp.arange(cells_y, dtype=jnp.int32)[None, :, None, None] + 1 + step_y
    target_rows = ((place_x * wide_cols + place_y) * CELL_ATOM_SLOTS + slot_index).reshape(
        atom_count, NEIGHBOUR_SLOTS
    )
    gathered = jnp.take(cycle_rows, target_rows, axis=1)
    cell_steps = jnp.stack(
        [
            horizontal_stride.astype(jnp.float32) * CELL_SIDE,
            step_y.astype(jnp.float32) * CELL_SIDE,
            jnp.zeros(horizontal_stride.shape, jnp.float32),
        ],
        axis=-1,
    ).reshape(atom_count, NEIGHBOUR_SLOTS, 3)
    own_coords = jnp.transpose(positions.reshape(3, atom_count))
    raw_vectors = jnp.moveaxis(gathered[:3], 0, -1) + cell_steps - own_coords[:, None, :]
    used_flat = is_used.reshape(atom_count, NEIGHBOUR_SLOTS)
    safe_vector = jnp.array([CELL_SIDE, 0.0, 0.0], dtype=jnp.float32)
    vectors = jnp.where(used_flat[..., None], raw_vectors, safe_vector)
    weights = used_flat.astype(jnp.float32) * gathered[3]
    own_occupied = occupied.reshape(atom_count).astype(jnp.float32)
    block_size = math.gcd(atom_count, 64)
    block_count = atom_count // block_size

    def single_block_view(inputs):
        block_targets, block_vectors, block_weights, block_occupied = inputs
        neigh_rows = jnp.take(row_table, block_targets, axis=0)
        return block_step(
            neigh_rows,
            block_vectors,
            block_weights,
            block_occupied,
            radial_weight,
            mix_weight,
            out_weight,
        )

    energy_values, edge_gradient = lax.map(
        single_block_view,
        (
            target_rows.reshape(block_count, block_size, NEIGHBOUR_SLOTS),
            vectors.reshape(block_count, block_size, NEIGHBOUR_SLOTS, 3),
            weights.reshape(block_count, block_size, NEIGHBOUR_SLOTS),
            own_occupied.reshape(block_count, block_size),
        ),
    )
    edge_gradient = edge_gradient.reshape(atom_count, NEIGHBOUR_SLOTS, 3)
    self_force_term = jnp.sum(edge_gradient, axis=1)
    spread_grad = (
        jnp.zeros((cycle_rows.shape[1], 3), jnp.float32)
        .at[target_rows.reshape(-1)]
        .add(-edge_gradient.reshape(-1, 3))
    )
    spread_grad = jnp.transpose(spread_grad).reshape(3, cells_x + 2, cells_y + 2, CELL_ATOM_SLOTS)
    returned = with_halo(spread_grad, (("gx", 1), ("gy", 2)), 1)
    fold_y = returned[:, :, 1:-1]
    fold_y = fold_y.at[:, :, 1].add(returned[:, :, 0]).at[:, :, -2].add(returned[:, :, -1])
    fold_x = fold_y[:, 1:-1]
    fold_x = fold_x.at[:, 1].add(fold_y[:, 0]).at[:, -2].add(fold_y[:, -1])
    forces = fold_x[:, 1:-1, 1:-1] + jnp.transpose(self_force_term).reshape(
        3, cells_x, cells_y, CELL_ATOM_SLOTS
    )
    slot_energy_values = energy_values.reshape(cells_x, cells_y, CELL_ATOM_SLOTS)
    total_energy = lax.psum(jnp.sum(slot_energy_values), ("gx", "gy"))
    return (forces, slot_energy_values, total_energy)


def solution(mesh):
    in_specs = (
        P("gx", "gy", None, None, None),
        P(None, "gx", "gy", None),
        P("gx", "gy", None),
        P("gx", "gy", None, None),
        P(),
        P(),
        P(),
    )
    out_specs = (P(None, "gx", "gy", None), P("gx", "gy", None), P())
    return jax.shard_map(
        on_device, mesh=mesh, in_specs=in_specs, out_specs=out_specs, check_vma=False
    )
```

profile of v0, /device:TPU:1, one launch (start us, length us, event | category | flops | bytes accessed | tf_op | source)
XLA Modules:
  0.0 356.7 jit_solution(8190235171304904646)
XLA Ops:
  2.1 4.5 %collective-permute-start = (f32[4,1,8,8]{3,2,1,0:T(8,128)S(1)}, f32[4,1,8,8]{3,2,1,0:T(8,128)S(1)}, u32[]{:S(2)}, u32[]{:S(2)}) collective-permute-start(f32[4,1,8,8]{3,2,1,0:T(8,128)S(1)} %get-tuple-element.447), channel_id=1, source_target_pairs={{0,64},{64,128},{128,192},{192,256},{256,320},{320,384},{384,448},... | collective-permute-start | bytes 3080 | tf_op jit(solution)/shard_map/ppermute | solution.py:29
  6.6 13.5 %collective-permute-start.1 = (f32[4,1,8,8]{3,2,1,0:T(8,128)S(1)}, f32[4,1,8,8]{3,2,1,0:T(8,128)S(1)}, u32[]{:S(2)}, u32[]{:S(2)}) collective-permute-start(f32[4,1,8,8]{3,2,1,0:T(8,128)S(1)} %get-tuple-element.448), channel_id=1, source_target_pairs={{64,0},{128,64},{192,128},{256,192},{320,256},{384,320},{448,384},... | collective-permute-start | bytes 3080 | tf_op jit(solution)/shard_map/ppermute | solution.py:30
  20.0 1.0 fusion.110
  21.1 1.9 collective-permute-start.4
  23.0 5.8 %collective-permute-start.5 = (bf16[1,8,8,9,128]{4,2,3,1,0:T(8,128)(2,1)S(1)}, bf16[1,8,8,9,128]{4,2,3,1,0:T(8,128)(2,1)S(1)}, u32[]{:S(2)}, u32[]{:S(2)}) collective-permute-start(bf16[1,8,8,9,128]{4,2,3,1,0:T(8,128)(2,1)S(1)} %get-tuple-element.437), channel_id=1, source_target_pairs={{64,0},{128,64},{192,128},{256,192},{320,256},{384,320},{448,384},... | collective-permute-start | bytes 442376 | tf_op jit(solution)/shard_map/ppermute | solution.py:30
  30.6 1.6 fusion.97
  37.6 1.9 collective-permute-start.2
  39.5 9.0 %collective-permute-start.3 = (f32[4,4,1,8]{3,2,1,0:T(1,128)S(1)}, f32[4,4,1,8]{3,2,1,0:T(1,128)S(1)}, u32[]{:S(2)}, u32[]{:S(2)}) collective-permute-start(f32[4,4,1,8]{3,2,1,0:T(1,128)S(1)} %get-tuple-element.446), channel_id=1, source_target_pairs={{1,0},{2,1},{3,2},{4,3},{5,4},{6,5},{7,6},{8,7},{9,8},{10,9},{11,1... | collective-permute-start | bytes 1544 | tf_op jit(solution)/shard_map/ppermute | solution.py:30
  50.4 10.8 %gather_fusion.4 = f32[4096,4]{1,0:T(8,128)S(1)} fusion(f32[4,320]{0,1:T(8,128)S(1)} %bitcast.435, s32[4096]{0:T(1024)S(1)} %broadcast_clamp_fusion.1), kind=kCustom, calls=%fused_computation.4 | custom fusion | bytes 147456 | tf_op jit(solution)/shard_map/jit(_take)/gather | solution.py:151
  61.2 1.3 copy.130
  62.8 1.9 collective-permute-start.6
  64.7 7.8 %collective-permute-start.7 = (bf16[4,1,8,9,128]{4,2,3,1,0:T(8,128)(2,1)S(1)}, bf16[4,1,8,9,128]{4,2,3,1,0:T(8,128)(2,1)S(1)}, u32[]{:S(2)}, u32[]{:S(2)}) collective-permute-start(bf16[4,1,8,9,128]{4,2,3,1,0:T(8,128)(2,1)S(1)} %get-tuple-element.436), channel_id=1, source_target_pairs={{1,0},{2,1},{3,2},{4,3},{5,4},{6,5},{7,6},{8,7},{9,8},{10,9},{11,1... | collective-permute-start | bytes 221192 | tf_op jit(solution)/shard_map/ppermute | solution.py:30
  74.3 109.5 %while.20 = (s32[]{:T(128)}, f32[2,64]{1,0:T(2,128)}, f32[2,64,32,3]{2,1,3,0:T(8,128)}, f32[2,64]{1,0:T(2,128)}, f32[7,8,128]{2,1,0:T(8,128)S(1)}, /*index=5*/f3...) while((s32[]{:T(128)}, f32[2,64]{1,0:T(2,128)}, ...), condition=%wide.region_8.9_spmd.clone.clone, body=%wide.region_0.8_spmd.sunk.clone.clone.sunk | while | flops 259054688 | bytes 81258744 | solution.py:183
  74.5 1.0 constant_dynamic-slice_fusion.3
  78.1 1.4 compare_select_fusion.6
  80.3 16.2 %gather_fusion.1 = bf16[2048,9,128]{2,1,0:T(8,128)(2,1)} fusion(bf16[320,9,128]{2,1,0:T(8,128)(2,1)S(1)} %get-tuple-element.606, s32[2048]{0:T(1024)S(1)} %broadcast_clamp_fusion.3), kind=kCustom, calls=%fused_computation.1.clone.clone.1 | custom fusion | bytes 9445376 | tf_op jit(solution)/shard_map/while/body/eval_jaxpr/jit(_take)/gather | solution.py:172
  96.4 4.7 %copy.226 = bf16[2048,9,128]{2,0,1:T(8,128)(2,1)S(1)} copy(bf16[2048,9,128]{2,1,0:T(8,128)(2,1)} %gather_fusion.1) | data formatting | bytes 9437184 | tf_op jit(solution)/shard_map/while/body/eval_jaxpr/jit(_take)/gather | solution.py:172
  101.9 2.5 broadcast_select_fusion.2
  105.6 2.6 multiply_reduce_fusion.14
  108.2 1.2 gather_fusion
  109.4 2.9 multiply_reduce_fusion.13
  113.0 1.2 gather_fusion.2
  114.2 3.5 fusion.170
  119.2 3.4 convolution_bitcast_fusion.3
  122.6 2.3 fusion.175
  124.9 1.5 multiply_reduce_fusion.16
  126.4 1.6 fusion.177
  132.7 1.4 compare_select_fusion.6
  134.9 16.2 %gather_fusion.1 = bf16[2048,9,128]{2,1,0:T(8,128)(2,1)} fusion(bf16[320,9,128]{2,1,0:T(8,128)(2,1)S(1)} %get-tuple-element.606, s32[2048]{0:T(1024)S(1)} %broadcast_clamp_fusion.3), kind=kCustom, calls=%fused_computation.1.clone.clone.1 | custom fusion | bytes 9445376 | tf_op jit(solution)/shard_map/while/body/eval_jaxpr/jit(_take)/gather | solution.py:172
  151.1 4.7 %copy.226 = bf16[2048,9,128]{2,0,1:T(8,128)(2,1)S(1)} copy(bf16[2048,9,128]{2,1,0:T(8,128)(2,1)} %gather_fusion.1) | data formatting | bytes 9437184 | tf_op jit(solution)/shard_map/while/body/eval_jaxpr/jit(_take)/gather | solution.py:172
  156.5 2.5 broadcast_select_fusion.2
  160.3 2.6 multiply_reduce_fusion.14
  162.8 1.2 gather_fusion
  164.0 2.9 multiply_reduce_fusion.13
  167.7 1.2 gather_fusion.2
  168.8 3.5 fusion.170
  173.8 3.4 convolution_bitcast_fusion.3
  177.2 2.3 fusion.175
  179.5 1.5 multiply_reduce_fusion.16
  181.0 1.6 fusion.177
  183.8 1.1 fusion.111
  185.7 22.6 %scatter_custom_fusion = f32[320,3]{1,0:T(8,128)S(1)} fusion(s32[4096]{0:T(1024)} %bitcast.468, f32[4096,3]{1,0:T(8,128)S(1)} %bitcast.457, f32[]{:T(128)} %constant.304.clone.1), kind=kCustom, calls=%fused_computation.172 | custom fusion | flops 12288 | bytes 4352 | tf_op jit(solution)/shard_map/scatter-add | solution.py:197
  208.8 4.7 %collective-permute-start.8 = (f32[3,1,10,8]{3,2,1,0:T(8,128)S(1)}, f32[3,1,10,8]{3,2,1,0:T(8,128)S(1)}, u32[]{:S(2)}, u32[]{:S(2)}) collective-permute-start(f32[3,1,10,8]{3,2,1,0:T(8,128)S(1)} %get-tuple-element.443), channel_id=1, source_target_pairs={{0,64},{64,128},{128,192},{192,256},{256,320},{320,384},{384,448},... | collective-permute-start | bytes 2888 | tf_op jit(solution)/shard_map/ppermute | solution.py:29
  213.5 5.0 %collective-permute-start.9 = (f32[3,1,10,8]{3,2,1,0:T(8,128)S(1)}, f32[3,1,10,8]{3,2,1,0:T(8,128)S(1)}, u32[]{:S(2)}, u32[]{:S(2)}) collective-permute-start(f32[3,1,10,8]{3,2,1,0:T(8,128)S(1)} %get-tuple-element.444), channel_id=1, source_target_pairs={{64,0},{128,64},{192,128},{256,192},{320,256},{384,320},{448,384},... | collective-permute-start | bytes 2888 | tf_op jit(solution)/shard_map/ppermute | solution.py:30
  219.4 1.9 collective-permute-start.10
  221.9 128.7 %psum.7 = f32[]{:T(128)} all-reduce(f32[]{:T(128)} %reduce_sum.128), channel_id=1, replica_groups=mesh['gx'=16,'gy'=64] {'gx','gy'}, use_global_device_ids=true, to_apply=%region_12.13 | all-reduce | flops 1 | bytes 8 | tf_op jit(solution)/shard_map/psum | solution.py:209
  351.5 1.9 collective-permute-start.11
  353.5 2.4 collective-permute-done.11
  (242 shorter events, 35.1 us)
Async XLA Ops:
  2.1 34.7 %collective-permute-start = (f32[4,1,8,8]{3,2,1,0:T(8,128)S(1)}, f32[4,1,8,8]{3,2,1,0:T(8,128)S(1)}, u32[]{:S(2)}, u32[]{:S(2)}) collective-permute-start(f32[4,1,8,8]{3,2,1,0:T(8,128)S(1)} %get-tuple-element.447), channel_id=1, source_target_pairs={{0,64},{64,128},{128,192},{192,256},{256,320},{320,384},{384,448},... | collective-permute-start | bytes 3080 | tf_op jit(solution)/shard_map/ppermute | solution.py:29
  6.6 30.2 %collective-permute-start.1 = (f32[4,1,8,8]{3,2,1,0:T(8,128)S(1)}, f32[4,1,8,8]{3,2,1,0:T(8,128)S(1)}, u32[]{:S(2)}, u32[]{:S(2)}) collective-permute-start(f32[4,1,8,8]{3,2,1,0:T(8,128)S(1)} %get-tuple-element.448), channel_id=1, source_target_pairs={{64,0},{128,64},{192,128},{256,192},{320,256},{384,320},{448,384},... | collective-permute-start | bytes 3080 | tf_op jit(solution)/shard_map/ppermute | solution.py:30
  21.1 41.5 %collective-permute-start.4 = (bf16[1,8,8,9,128]{4,2,3,1,0:T(8,128)(2,1)S(1)}, bf16[1,8,8,9,128]{4,2,3,1,0:T(8,128)(2,1)S(1)}, u32[]{:S(2)}, u32[]{:S(2)}) collective-permute-start(bf16[1,8,8,9,128]{4,2,3,1,0:T(8,128)(2,1)S(1)} %get-tuple-element.438), channel_id=1, source_target_pairs={{0,64},{64,128},{128,192},{192,256},{256,320},{320,384},{384,448},... | collective-permute-start | bytes 442376 | tf_op jit(solution)/shard_map/ppermute | solution.py:29
  23.0 39.7 %collective-permute-start.5 = (bf16[1,8,8,9,128]{4,2,3,1,0:T(8,128)(2,1)S(1)}, bf16[1,8,8,9,128]{4,2,3,1,0:T(8,128)(2,1)S(1)}, u32[]{:S(2)}, u32[]{:S(2)}) collective-permute-start(bf16[1,8,8,9,128]{4,2,3,1,0:T(8,128)(2,1)S(1)} %get-tuple-element.437), channel_id=1, source_target_pairs={{64,0},{128,64},{192,128},{256,192},{320,256},{384,320},{448,384},... | collective-permute-start | bytes 442376 | tf_op jit(solution)/shard_map/ppermute | solution.py:30
  37.6 11.7 %collective-permute-start.2 = (f32[4,4,1,8]{3,2,1,0:T(1,128)S(1)}, f32[4,4,1,8]{3,2,1,0:T(1,128)S(1)}, u32[]{:S(2)}, u32[]{:S(2)}) collective-permute-start(f32[4,4,1,8]{3,2,1,0:T(1,128)S(1)} %get-tuple-element.445), channel_id=1, source_target_pairs={{0,1},{1,2},{2,3},{3,4},{4,5},{5,6},{6,7},{7,8},{8,9},{9,10},{10,1... | collective-permute-start | bytes 1544 | tf_op jit(solution)/shard_map/ppermute | solution.py:29
  39.5 9.8 %collective-permute-start.3 = (f32[4,4,1,8]{3,2,1,0:T(1,128)S(1)}, f32[4,4,1,8]{3,2,1,0:T(1,128)S(1)}, u32[]{:S(2)}, u32[]{:S(2)}) collective-permute-start(f32[4,4,1,8]{3,2,1,0:T(1,128)S(1)} %get-tuple-element.446), channel_id=1, source_target_pairs={{1,0},{2,1},{3,2},{4,3},{5,4},{6,5},{7,6},{8,7},{9,8},{10,9},{11,1... | collective-permute-start | bytes 1544 | tf_op jit(solution)/shard_map/ppermute | solution.py:30
  50.4 12.2 %copy-start.7 = (bf16[2,8,8,9,128]{4,2,3,1,0:T(8,128)(2,1)S(1)}, bf16[2,8,8,9,128]{4,2,3,1,0:T(8,128)(2,1)}, u32[]{:S(2)}) copy-start(bf16[2,8,8,9,128]{4,2,3,1,0:T(8,128)(2,1)} %param.24) | copy-start | bytes 884740
  61.2 11.3 %copy-start.21 = (f32[3]{0:T(128)S(1)}, f32[3]{0:T(128)}, u32[]{:S(2)}) copy-start(f32[3]{0:T(128)} %constant.318.clone) | copy-start | bytes 40
  62.6 11.7 %copy-start.1 = (f32[7,8,128]{2,1,0:T(8,128)S(1)}, f32[7,8,128]{2,1,0:T(8,128)}, u32[]{:S(2)}) copy-start(f32[7,8,128]{2,1,0:T(8,128)} %param.28) | copy-start | bytes 86020
  62.7 11.7 %copy-start.14 = (f32[128]{0:T(128)S(1)}, f32[128]{0:T(128)}, u32[]{:S(2)}) copy-start(f32[128]{0:T(128)} %param.30) | copy-start | bytes 1540
  62.8 10.6 %collective-permute-start.6 = (bf16[4,1,8,9,128]{4,2,3,1,0:T(8,128)(2,1)S(1)}, bf16[4,1,8,9,128]{4,2,3,1,0:T(8,128)(2,1)S(1)}, u32[]{:S(2)}, u32[]{:S(2)}) collective-permute-start(bf16[4,1,8,9,128]{4,2,3,1,0:T(8,128)(2,1)S(1)} %get-tuple-element.435), channel_id=1, source_target_pairs={{0,1},{1,2},{2,3},{3,4},{4,5},{5,6},{6,7},{7,8},{8,9},{9,10},{10,1... | collective-permute-start | bytes 221192 | tf_op jit(solution)/shard_map/ppermute | solution.py:29
  64.7 9.2 %collective-permute-start.7 = (bf16[4,1,8,9,128]{4,2,3,1,0:T(8,128)(2,1)S(1)}, bf16[4,1,8,9,128]{4,2,3,1,0:T(8,128)(2,1)S(1)}, u32[]{:S(2)}, u32[]{:S(2)}) collective-permute-start(bf16[4,1,8,9,128]{4,2,3,1,0:T(8,128)(2,1)S(1)} %get-tuple-element.436), channel_id=1, source_target_pairs={{1,0},{2,1},{3,2},{4,3},{5,4},{6,5},{7,6},{8,7},{9,8},{10,9},{11,1... | collective-permute-start | bytes 221192 | tf_op jit(solution)/shard_map/ppermute | solution.py:30
  74.5 3.1 copy-start.10
  77.6 1.8 copy-start.3
  105.6 2.6 copy-start.15
  105.6 2.6 copy-start.16
  114.2 3.5 copy-start
  114.2 3.5 copy-start.2
  114.2 3.5 copy-start.6
  114.2 3.8 %copy-start.20 = (f32[2,64]{1,0:T(2,128)S(1)}, f32[2,64]{1,0:T(2,128)}, u32[]{:S(2)}) copy-start(f32[2,64]{1,0:T(2,128)} %get-tuple-element.601) | copy-start | bytes 1540 | tf_op jit(solution)/shard_map/while
  117.7 4.8 %slice-start = ((s8[4718592]{0:T(1024)(128)(4,1)}), s8[4194304]{0:T(1024)(128)(4,1)S(1)}, s32[]{:S(2)}) async-start(s8[4718592]{0:T(1024)(128)(4,1)} %bitcast.433), calls=%async_computation | async-start | bytes 8388608 | tf_op jit(solution)/shard_map/while
  118.5 4.0 %slice-start.1 = ((s8[4718592]{0:T(1024)(128)(4,1)}), s8[524288]{0:T(1024)(128)(4,1)S(1)}, s32[]{:S(2)}) async-start(s8[4718592]{0:T(1024)(128)(4,1)} %bitcast.433), calls=%async_computation.1 | async-start | bytes 1048576 | tf_op jit(solution)/shard_map/while
  119.2 3.4 copy-start.9
  122.6 2.3 copy-start.4
  124.9 3.5 copy-start.12
  126.3 2.2 copy-start.17
  126.3 2.8 copy-start.11
  129.2 3.1 copy-start.10
  132.3 1.8 copy-start.3
  160.2 2.6 copy-start.15
  160.2 2.6 copy-start.16
  168.8 3.5 copy-start
  168.8 3.5 copy-start.2
  168.8 3.5 copy-start.6
  168.8 3.8 %copy-start.20 = (f32[2,64]{1,0:T(2,128)S(1)}, f32[2,64]{1,0:T(2,128)}, u32[]{:S(2)}) copy-start(f32[2,64]{1,0:T(2,128)} %get-tuple-element.601) | copy-start | bytes 1540 | tf_op jit(solution)/shard_map/while
  172.3 4.8 %slice-start = ((s8[4718592]{0:T(1024)(128)(4,1)}), s8[4194304]{0:T(1024)(128)(4,1)S(1)}, s32[]{:S(2)}) async-start(s8[4718592]{0:T(1024)(128)(4,1)} %bitcast.433), calls=%async_computation | async-start | bytes 8388608 | tf_op jit(solution)/shard_map/while
  173.2 4.0 %slice-start.1 = ((s8[4718592]{0:T(1024)(128)(4,1)}), s8[524288]{0:T(1024)(128)(4,1)S(1)}, s32[]{:S(2)}) async-start(s8[4718592]{0:T(1024)(128)(4,1)} %bitcast.433), calls=%async_computation.1 | async-start | bytes 1048576 | tf_op jit(solution)/shard_map/while
  173.8 3.4 copy-start.9
  177.2 2.3 copy-start.4
  179.5 1.5 copy-start.5
  179.5 3.5 copy-start.12
  181.0 2.2 copy-start.17
  181.0 2.8 copy-start.11
  183.8 37.5 %copy-start.19 = (f32[2,64]{1,0:T(2,128)S(1)}, f32[2,64]{1,0:T(2,128)}, u32[]{:S(2)}) copy-start(f32[2,64]{1,0:T(2,128)} %get-tuple-element.262) | copy-start | bytes 1540
  208.8 9.7 %collective-permute-start.8 = (f32[3,1,10,8]{3,2,1,0:T(8,128)S(1)}, f32[3,1,10,8]{3,2,1,0:T(8,128)S(1)}, u32[]{:S(2)}, u32[]{:S(2)}) collective-permute-start(f32[3,1,10,8]{3,2,1,0:T(8,128)S(1)} %get-tuple-element.443), channel_id=1, source_target_pairs={{0,64},{64,128},{128,192},{192,256},{256,320},{320,384},{384,448},... | collective-permute-start | bytes 2888 | tf_op jit(solution)/shard_map/ppermute | solution.py:29
  213.5 5.8 %collective-permute-start.9 = (f32[3,1,10,8]{3,2,1,0:T(8,128)S(1)}, f32[3,1,10,8]{3,2,1,0:T(8,128)S(1)}, u32[]{:S(2)}, u32[]{:S(2)}) collective-permute-start(f32[3,1,10,8]{3,2,1,0:T(8,128)S(1)} %get-tuple-element.444), channel_id=1, source_target_pairs={{64,0},{128,64},{192,128},{256,192},{320,256},{384,320},{448,384},... | collective-permute-start | bytes 2888 | tf_op jit(solution)/shard_map/ppermute | solution.py:30
  219.4 134.0 %collective-permute-start.10 = (f32[3,6,1,8]{3,2,1,0:T(1,128)S(1)}, f32[3,6,1,8]{3,2,1,0:T(1,128)S(1)}, u32[]{:S(2)}, u32[]{:S(2)}) collective-permute-start(f32[3,6,1,8]{3,2,1,0:T(1,128)S(1)} %get-tuple-element.442), channel_id=1, source_target_pairs={{0,1},{1,2},{2,3},{3,4},{4,5},{5,6},{6,7},{7,8},{8,9},{9,10},{10,1... | collective-permute-start | bytes 1736 | tf_op jit(solution)/shard_map/ppermute | solution.py:29
  351.5 4.4 %collective-permute-start.11 = (f32[3,6,1,8]{3,2,1,0:T(1,128)S(1)}, f32[3,6,1,8]{3,2,1,0:T(1,128)S(1)}, u32[]{:S(2)}, u32[]{:S(2)}) collective-permute-start(f32[3,6,1,8]{3,2,1,0:T(1,128)S(1)} %get-tuple-element.441), channel_id=1, source_target_pairs={{1,0},{2,1},{3,2},{4,3},{5,4},{6,5},{7,6},{8,7},{9,8},{10,9},{11,1... | collective-permute-start | bytes 1736 | tf_op jit(solution)/shard_map/ppermute | solution.py:30
  (7 other events, 6.1 us)
where the time goes:
time: 359 us; the launch traced here: 357 us
  blocking collectives  129 us (36%)
  local copies, waits for them, and re-layouts  74.8 us (21%)
  starting transfers between devices  59.8 us (17%)
  other arithmetic  54.2 us (15%)
  matrix products  33.2 us (9%)
  waiting for transfers between devices  3.8 us (1%)
    psum x1, blocking collectives, on_device(): total_energy = lax.psum(jnp.sum(slot_energy_values), ('gx', 'gy'))  129 us
    ppermute x6, starting transfers between devices, with_halo(): after = lax.ppermute(first, axis, down)  42.9 us
    gather x4, local copies, waits for them, and re-layouts, single_block_view(): neigh_rows = jnp.take(row_table, block_targets, axis=0)  41.7 us
    scatter-add x1, other arithmetic, on_device(): spread_grad = jnp.zeros((cycle_rows.shape[1], 3), jnp.float32).at[target_...  22.6 us
    ppermute x6, starting transfers between devices, with_halo(): before = lax.ppermute(last, axis, up)  16.8 us
    gather x2, local copies, waits for them, and re-layouts, on_device(): gathered = jnp.take(cycle_rows, target_rows, axis=1)  12 us
    select_n x4, other arithmetic, single_block_view(): neigh_rows = jnp.take(row_table, block_targets, axis=0)  7.67 us
  transfers between devices with their start and end apart: 12, of which 3 were waited for; matrix products, arithmetic and copies ran while one was open for 7% of the time, Pallas kernels for 0%

commit v1 on v0

v1 whole, which is shorter than its diff:
```python
import math

import jax
import jax.numpy as jnp
from jax import lax
from jax.experimental import pallas as pl
from jax.experimental.pallas import tpu as pltpu
from jax.sharding import Mesh, PartitionSpec as P

C = 128
NB = 8
GROUPS = 4
ROWS = 32
LEAD = (0, 3, 3, 3, 5, 5, 5, 5, 5)
PLAIN = (4, 4, 4, 6, 6, 6, 6, 6)
PAIRED = (1, 1, 1, 2, 2, 2, 2, 2)
R3 = math.sqrt(3.0)
R5 = math.sqrt(5.0)
R15 = math.sqrt(15.0)
F32 = jnp.float32
BF16 = jnp.bfloat16
NT = (((1,), (1,)), ((), ()))


def count_kernel(neighbours, counts):
    lanes = lax.broadcasted_iota(jnp.int32, (ROWS, C), 1)
    rows = lax.broadcasted_iota(jnp.int32, (ROWS, ROWS), 0)
    own_y = rows >> 4
    own_x = (rows >> 3) & 1
    for q in range(GROUPS):
        code = jnp.concatenate(
            [neighbours[x, 2 * q + y] for y in range(2) for x in range(2)], axis=0
        )
        cell = code >> 3
        step_x = (cell * 11) >> 5
        x = own_x + step_x
        y = own_y + cell - 3 * step_x
        column = jnp.where(x == 0, 2, jnp.where(x == 3, 3, x - 1))
        place = jnp.where(code < 72, (y * 4 + column) * 8 + (code & 7), -1)
        total = jnp.zeros((ROWS, C), F32)
        for k in range(32):
            total = total + jnp.where(lanes == place[:, k : k + 1], 1.0, 0.0)
        counts[q] = total


def weighted(products, weight, path):
    total = None
    for b in range(NB):
        term = weight[path, b : b + 1, :] * products[ROWS * b : ROWS * (b + 1)]
        total = term if total is None else total + term
    return total


def main_kernel(
    col_a, col_b, col_l, col_r, down, up, counts, weight, mix, out_weight,
    rows_out, near_out, send_down, send_up,
    table, geometry, edge, message, back, values, near,
):
    columns = (col_a, col_b, col_l, col_r)
    for m in range(10):
        for y in range(10):
            if y == 0:
                tiles = [down[i, m] for i in range(4)]
            elif y == 9:
                tiles = [up[i, m] for i in range(4)]
            else:
                tiles = [column[y - 1, m] for column in columns]
            rows = jnp.concatenate([tile.astype(F32) for tile in tiles], axis=0)
            table[32 * y : 32 * y + 32, C * m : C * m + C] = rows.astype(BF16)
    near[...] = jnp.zeros_like(near)

    piece = lax.broadcasted_iota(jnp.int32, (16, C), 1)
    which = lax.broadcasted_iota(jnp.int32, (16, C), 0) * 3
    pick_rows = jnp.where((piece >= which) & (piece < which + 3), 1.0, 0.0).astype(BF16)
    piece = lax.broadcasted_iota(jnp.int32, (C, 4 * C), 0)
    which = (lax.broadcasted_iota(jnp.int32, (C, 4 * C), 1) >> 7) * 3
    pick_columns = jnp.where((piece >= which) & (piece < which + 3), 1.0, 0.0).astype(BF16)
    lane = lax.broadcasted_iota(jnp.int32, (1, C), 1)
    column = (lane >> 3) & 3
    place_x = jnp.where(column == 2, 0, jnp.where(column == 3, 3, column + 1))
    shift_x = place_x.astype(F32) * 5.0
    shift_y = (lane >> 5).astype(F32) * 5.0
    row = lax.broadcasted_iota(jnp.int32, (ROWS, C), 0)
    own_shift_x = ((row >> 3) & 1).astype(F32) * 5.0 + 5.0
    own_shift_y = (row >> 4).astype(F32) * 5.0 + 5.0

    def block_of(q):
        return pl.ds(pl.multiple_of(q * 64, 64), C)

    def own_values(q):
        base = pl.multiple_of(q * 64, 64)
        own = jnp.concatenate(
            [
                table[pl.ds(base + 32, 16), 9 * C : 10 * C],
                table[pl.ds(base + 64, 16), 9 * C : 10 * C],
            ],
            axis=0,
        )
        return jnp.dot(own, pick_columns, preferred_element_type=F32)

    def forward(q, carry):
        block = block_of(q)
        around = lax.dot_general(
            pick_rows, table[block, 9 * C : 10 * C], NT, preferred_element_type=F32
        )
        own = own_values(q)
        rx = (around[0:1] + shift_x) - (own[:, 0:C] + own_shift_x)
        ry = (around[1:2] + shift_y) - (own[:, C : 2 * C] + own_shift_y)
        rz = around[2:3] - own[:, 2 * C : 3 * C]
        times = counts[q]
        dist_sq = rx * rx + ry * ry + rz * rz
        inside = (times > 0.5) & (dist_sq < 25.0)
        dist_sq = jnp.where(inside, dist_sq, 25.0)
        fall = jnp.where(inside, 1.0 - dist_sq * 0.04, 0.0)
        inv = lax.rsqrt(dist_sq)
        inv = inv * (1.5 - 0.5 * dist_sq * inv * inv)
        turn = dist_sq * inv * (math.pi / 5.0) - math.pi / 2.0
        sq = turn * turn
        cosine = jnp.full_like(sq, 1.0 / math.factorial(12))
        for order in (10, 8, 6, 4, 2, 0):
            sign = 1.0 if order % 4 == 0 else -1.0
            cosine = cosine * sq + sign / math.factorial(order)
        sine = jnp.full_like(sq, 1.0 / math.factorial(13))
        for order in (11, 9, 7, 5, 3, 1):
            sign = 1.0 if order % 4 == 1 else -1.0
            sine = sine * sq + sign / math.factorial(order)
        s_now, c_now = cosine, -sine * turn
        twice = 2.0 * c_now
        s_last, c_last = jnp.zeros_like(sq), jnp.ones_like(sq)
        amount = times * around[3:4]
        base = amount * fall * fall * inv
        slope = -(amount * fall) * (fall * inv * inv + 0.16)
        ux, uy, uz = rx * inv, ry * inv, rz * inv
        harmonics = (
            None,
            R3 * ux,
            R3 * uy,
            R3 * uz,
            R15 * ux * uy,
            R15 * uy * uz,
            (0.5 * R5) * (3.0 * uz * uz - 1.0),
            R15 * ux * uz,
            (0.5 * R15) * (ux * ux - uy * uy),
        )
        edge[q, 0] = inv
        for g in range(1, 9):
            edge[q, g] = harmonics[g]
        for b in range(NB):
            radial = s_now * base
            edge[q, 9 + b] = radial
            edge[q, 17 + b] = c_now * base * ((b + 1) * math.pi / 5.0) + s_now * slope
            spot = slice(ROWS * b, ROWS * b + ROWS)
            geometry[0, spot] = radial.astype(BF16)
            for g in range(1, 9):
                geometry[g, spot] = (radial * harmonics[g]).astype(BF16)
            s_now, s_last = twice * s_now - s_last, s_now
            c_now, c_last = twice * c_now - c_last, c_now
        messages = [None] * 9
        for m in (0, 2, 4, 6, 8):
            width = 1 if m == 8 else 2
            products = jnp.dot(
                geometry[0], table[block, C * m : C * (m + width)], preferred_element_type=F32
            )
            for j in range(width):
                path = 0 if m + j == 0 else PLAIN[m + j - 1]
                messages[m + j] = weighted(products[:, C * j : C * j + C], weight, path)
        first = table[block, 0:C]
        for g in range(1, 9):
            both = jnp.concatenate([first, table[block, C * g : C * g + C]], axis=1)
            products = jnp.dot(geometry[g], both, preferred_element_type=F32)
            messages[g] = messages[g] + weighted(products[:, :C], weight, LEAD[g])
            messages[0] = messages[0] + weighted(products[:, C:], weight, PAIRED[g - 1])
        for g in range(9):
            message[g] = messages[g].astype(BF16)
        mixed = jnp.dot(message[...].reshape(9 * ROWS, C), mix[...], preferred_element_type=F32)
        mixed = mixed.reshape(9, ROWS, C)
        z = mixed[0]
        for g in range(1, 9):
            z = z + mixed[g] * mixed[g]
        gate = 1.0 / (1.0 + jnp.exp(-z))
        scale = own[:, 3 * C : 4 * C] * out_weight[0:1]
        spot = pl.ds(pl.multiple_of(q * ROWS, ROWS), ROWS)
        values[3, spot] = scale * (z * gate)
        grad = scale * gate * (1.0 + z * (1.0 - gate))
        message[0] = grad.astype(BF16)
        grad = 2.0 * grad
        for g in range(1, 9):
            message[g] = (grad * mixed[g]).astype(BF16)
        returned = lax.dot_general(
            message[...].reshape(9 * ROWS, C), mix[...], NT, preferred_element_type=F32
        )
        back[...] = returned.reshape(9, ROWS, C)

        def spread(g, path):
            return jnp.concatenate(
                [(weight[path, b : b + 1, :] * back[g]).astype(BF16) for b in range(NB)], axis=0
            )

        wide = jnp.concatenate([spread(0, 0)] + [spread(g, PLAIN[g - 1]) for g in range(1, 9)], axis=1)
        grads = lax.dot_general(wide, table[block, 0 : 9 * C], NT, preferred_element_type=F32)
        along = [None] * NB
        sums = [None] * 9
        for b in range(NB):
            along[b] = grads[ROWS * b : ROWS * b + ROWS]
        paired = {1: spread(0, 1), 2: spread(0, 2)}
        for g in range(1, 9):
            both = jnp.concatenate([first, table[block, C * g : C * g + C]], axis=1)
            wide = jnp.concatenate([spread(g, LEAD[g]), paired[PAIRED[g - 1]]], axis=1)
            grads = lax.dot_general(wide, both, NT, preferred_element_type=F32)
            harmonic = edge[q, g]
            total = None
            for b in range(NB):
                part = grads[ROWS * b : ROWS * b + ROWS]
                along[b] = along[b] + part * harmonic
                term = part * edge[q, 9 + b]
                total = term if total is None else total + term
            sums[g] = total
        radial = None
        for b in range(NB):
            term = along[b] * edge[q, 17 + b]
            radial = term if radial is None else radial + term
        inv = edge[q, 0]
        ux, uy, uz = (edge[q, g] * (1.0 / R3) for g in (1, 2, 3))
        vx = R3 * sums[1] + R15 * (uy * sums[4] + uz * sums[7] + ux * sums[8])
        vy = R3 * sums[2] + R15 * (ux * sums[4] + uz * sums[5] - uy * sums[8])
        vz = R3 * sums[3] + R15 * (uy * sums[5] + ux * sums[7]) + (3.0 * R5) * uz * sums[6]
        inward = radial - inv * (ux * vx + uy * vy + uz * vz)
        for axis, (v, unit) in enumerate(((vx, ux), (vy, uy), (vz, uz))):
            gradient = inward * unit + inv * v
            values[axis, spot] = gradient
            near[axis, pl.ds(q, 1)] = jnp.sum(gradient, axis=0, keepdims=True)
        return carry

    lax.fori_loop(0, GROUPS, forward, 0)
    rows_out[...] = jnp.zeros_like(rows_out)
    send_down[...] = jnp.zeros_like(send_down)
    send_up[...] = jnp.zeros_like(send_up)
    for kind in range(4):
        rows_out[kind : kind + 1] = jnp.sum(values[kind].T, axis=0, keepdims=True)
    low = lax.broadcasted_iota(jnp.int32, (8, C), 1) < 64
    for axis in range(3):
        part = near[axis]
        later = pltpu.roll(pltpu.roll(part, 64, 1), 1, 0)
        pairs = jnp.where(low, part + later, 0.0)
        near_out[axis] = pairs
        send_down[axis : axis + 1] = pairs[0:1]
        send_up[axis : axis + 1] = pairs[4:5]


def main_call(*arrays):
    rows = jax.ShapeDtypeStruct((8, C), F32)
    return pl.pallas_call(
        main_kernel,
        out_shape=(rows, jax.ShapeDtypeStruct((3, 8, C), F32), rows, rows),
        in_specs=[pl.BlockSpec(memory_space=pltpu.VMEM)] * 10,
        out_specs=(pl.BlockSpec(memory_space=pltpu.VMEM),) * 4,
        scratch_shapes=[
            pltpu.VMEM((320, 10 * C), BF16),
            pltpu.VMEM((9, NB * ROWS, C), BF16),
            pltpu.VMEM((GROUPS, 25, ROWS, C), F32),
            pltpu.VMEM((9, ROWS, C), BF16),
            pltpu.VMEM((9, ROWS, C), F32),
            pltpu.VMEM((4, C, C), F32),
            pltpu.VMEM((3, 8, C), F32),
        ],
        compiler_params=pltpu.CompilerParams(vmem_limit_bytes=40 * 1024 * 1024),
        name="interact",
    )(*arrays)


def count_call(neighbours):
    return pl.pallas_call(
        count_kernel,
        out_shape=jax.ShapeDtypeStruct((GROUPS, ROWS, C), F32),
        in_specs=[pl.BlockSpec(memory_space=pltpu.VMEM)],
        out_specs=pl.BlockSpec(memory_space=pltpu.VMEM),
        compiler_params=pltpu.CompilerParams(vmem_limit_bytes=16 * 1024 * 1024),
        cost_estimate=pl.CostEstimate(flops=2_000_000, bytes_accessed=1_000_000, transcendentals=0),
        name="count",
    )(neighbours)


def ring(size, step):
    return [(i, (i + step) % size) for i in range(size)]


def packed_places(positions, occupied):
    pieces = []
    for axis in range(3):
        rest = positions[axis]
        for _ in range(3):
            piece = lax.reduce_precision(rest, 8, 7)
            pieces.append(piece)
            rest = rest - piece
    pieces.append(occupied.astype(F32))
    packed = jnp.stack(pieces, axis=-1)
    return jnp.pad(packed, ((0, 0), (0, 0), (0, 0), (0, C - 10))).astype(BF16)


def on_device(features, positions, occupied, neighbours, radial_weight, mix_weight, out_weight, *, outer, inner):
    gy = outer + inner
    size_x = lax.axis_size("gx")
    size_y = lax.axis_size(gy)
    counts = count_call(neighbours)
    own = jnp.concatenate(
        [jnp.transpose(features, (0, 1, 3, 2, 4)), packed_places(positions, occupied)[:, :, None]],
        axis=2,
    )
    col_a, col_b = own[0], own[1]
    col_l = lax.ppermute(col_b, "gx", ring(size_x, 1))
    col_r = lax.ppermute(col_a, "gx", ring(size_x, -1))
    columns = (col_a, col_b, col_l, col_r)
    down = lax.ppermute(jnp.stack([c[7] for c in columns]), gy, ring(size_y, 1))
    up = lax.ppermute(jnp.stack([c[0] for c in columns]), gy, ring(size_y, -1))
    rows, near, send_down, send_up = main_call(
        col_a, col_b, col_l, col_r, down, up, counts, radial_weight, mix_weight, out_weight[None]
    )
    from_up = lax.ppermute(send_down, gy, ring(size_y, -1))
    from_down = lax.ppermute(send_up, gy, ring(size_y, 1))
    energy = rows[3:4]
    plane = size_x * lax.axis_size(outer)
    gathered = lax.all_to_all(jnp.broadcast_to(energy[None], (plane, 1, C)), ("gx",) + outer, 0, 0)
    energy_plane = jnp.sum(gathered, axis=0)

    lane = jnp.arange(C)
    low = (lane < 32)[None, None, :]
    high = ((lane >= 32) & (lane < 64))[None, None, :]
    pair = jnp.arange(8)[None, :, None]
    near = near + jnp.where((pair == 0) & high, from_down[:3, None], 0.0)
    near = near + jnp.where((pair == 4) & low, from_up[:3, None], 0.0)
    from_left = lax.ppermute(near, "gx", ring(size_x, 1))
    from_right = lax.ppermute(near, "gx", ring(size_x, -1))
    depth = lax.axis_size(inner)
    gathered = lax.all_to_all(jnp.broadcast_to(energy_plane[None], (depth, 1, C)), inner, 0, 0)
    total_energy = jnp.sum(gathered)

    def cells(block):
        return block[:, :5, :64].reshape(3, 10, 4, 8)[:, 1:9]

    mine = cells(near)
    self_term = rows[:3].reshape(3, 8, 2, 8)
    first = self_term[:, :, 0] - mine[:, :, 0] - cells(from_left)[:, :, 3]
    second = self_term[:, :, 1] - mine[:, :, 1] - cells(from_right)[:, :, 2]
    forces = jnp.stack([first, second], axis=1)
    slot_energy_values = jnp.transpose(rows[3].reshape(8, 2, 8), (1, 0, 2))
    return forces, slot_energy_values, total_energy


def solution(mesh):
    size_x, size_y = mesh.shape["gx"], mesh.shape["gy"]
    depth = 16 if size_y % 16 == 0 else size_y // 2
    split = Mesh(mesh.devices.reshape(size_x, size_y // depth, depth), ("gx", "gya", "gyb"))
    outer, inner = ("gya",), ("gyb",)
    gy = outer + inner
    in_specs = (
        P("gx", gy, None, None, None),
        P(None, "gx", gy, None),
        P("gx", gy, None),
        P("gx", gy, None, None),
        P(),
        P(),
        P(),
    )
    out_specs = (P(None, "gx", gy, None), P("gx", gy, None), P())

    def program(*arrays):
        return on_device(*arrays, outer=outer, inner=inner)

    return jax.shard_map(
        program, mesh=split, in_specs=in_specs, out_specs=out_specs, check_vma=False
    )
```

time: 359 us -> 110 us (0.31)
  blocking collectives: 129 us -> 0 us
  local copies, waits for them, and re-layouts: 74.8 us -> 6.88 us
  other arithmetic: 54.2 us -> 1.68 us
  matrix products: 33.2 us -> 0 us
  waiting for transfers between devices: 3.8 us -> 27.6 us
  Pallas kernels: 0 us -> 8.48 us
  starting transfers between devices: 59.8 us -> 64.1 us
    psum x1 -> x0, blocking collectives: 129 us -> none  [on_device(): total_energy = lax.psum(jnp.sum(slot_energy_values), ('gx', 'gy'))]
    gather x12 -> x0, local copies, waits for them, and re-layouts: 59.4 us -> none  [the longest x4 41.7 us: single_block_view(): neigh_rows = jnp.take(row_table, block_targets, axis=0)]
    dot_general x18 -> x0, matrix products: 33.2 us -> none  [the longest x2 6.96 us: block_step(): jnp.einsum('akbm,akmc->abmc', rounded[..., 1:], neigh_rows[:, :, 1:], pre...]
    scatter-add x3 -> x0, other arithmetic: 22.6 us -> none  [the longest x1 22.6 us: on_device(): spread_grad = jnp.zeros((cycle_rows.shape[1], 3), jnp.float32).at[target_...]
    all_to_all x0 -> x2, waiting for transfers between devices: none -> 18.7 us  [the longest x1 10.7 us: on_device(): lax.all_to_all(jnp.broadcast_to(energy_plane[None], (depth, 1, C)), inner...]
    all_to_all x0 -> x2, starting transfers between devices: none -> 13.8 us  [the longest x1 8.03 us: on_device(): lax.all_to_all(jnp.broadcast_to(energy[None], (plane, 1, C)), ('gx',) + o...]
    ppermute x12 -> x8, starting transfers between devices: 59.8 us -> 50.3 us  [the longest x1 13.8 us: on_device(): up = lax.ppermute(jnp.stack([c[0] for c in columns]), gy, ring(size_y, -1))]
    select_n x8 -> x0, other arithmetic: 9.23 us -> none  [the longest x4 7.67 us: single_block_view(): neigh_rows = jnp.take(row_table, block_targets, axis=0)]
  transfers between devices with their start and end apart: 12 -> 10, of which waited for: 3 -> 5; matrix products, arithmetic and copies ran while one was open for 7% -> 2% of each run, Pallas kernels for 0% -> 1%
where the time goes in v1:
time: 110 us
  starting transfers between devices  64.1 us (58%)
  waiting for transfers between devices  27.6 us (25%)
  Pallas kernels  8.48 us (8%)
  local copies, waits for them, and re-layouts  6.88 us (6%)
  other arithmetic  1.68 us (2%)
    ppermute x1, starting transfers between devices, on_device(): up = lax.ppermute(jnp.stack([c[0] for c in columns]), gy, ring(size_y, -1))  13.8 us
    ppermute x1, starting transfers between devices, on_device(): col_r = lax.ppermute(col_a, 'gx', ring(size_x, -1))  13.5 us
    all_to_all x1, waiting for transfers between devices, on_device(): lax.all_to_all(jnp.broadcast_to(energy_plane[None], (depth, 1, C)), inner...  10.7 us
    ppermute x1, waiting for transfers between devices, on_device(): down = lax.ppermute(jnp.stack([c[7] for c in columns]), gy, ring(size_y, 1))  8.13 us
    all_to_all x1, starting transfers between devices, on_device(): lax.all_to_all(jnp.broadcast_to(energy[None], (plane, 1, C)), ('gx',) + o...  8.03 us
    all_to_all x1, waiting for transfers between devices, on_device(): lax.all_to_all(jnp.broadcast_to(energy[None], (plane, 1, C)), ('gx',) + o...  8 us
    pallas_call x1, Pallas kernels, main_call(): pl.pallas_call(main_kernel, out_shape=(rows, jax.ShapeDtypeStruct((3, 8,...  7.66 us
    ppermute x1, starting transfers between devices, on_device(): from_up = lax.ppermute(send_down, gy, ring(size_y, -1))  7.58 us
  transfers between devices with their start and end apart: 10, of which 5 were waited for; matrix products, arithmetic and copies ran while one was open for 2% of the time, Pallas kernels for 1%

profile of v1, /device:TPU:1, one launch (start us, length us, event | category | flops | bytes accessed | tf_op | source)
XLA Modules:
  0.0 109.7 jit_solution(3704890402435767034)
XLA Ops:
  0.6 0.8 bitcast_reduce-precision_fusion
  1.4 0.2 copy.64
  1.6 0.2 copy.67
  1.8 0.2 copy.63
  1.9 0.2 copy.66
  2.1 0.2 copy.70
  2.3 0.2 copy.69
  2.4 0.2 copy.71
  2.6 0.2 copy.72
  2.8 0.2 copy.73
  3.0 0.5 copy-done.6
  3.5 0.2 copy.74
  3.7 0.0 copy-start.4
  3.8 0.2 stack.13
  4.0 0.8 copy-done.4
  4.7 4.5 %collective-permute-start = (bf16[8,10,8,128]{3,2,1,0:T(8,128)(2,1)S(1)}, bf16[8,10,8,128]{3,2,1,0:T(8,128)(2,1)S(1)}, u32[]{:S(2)}, u32[]{:S(2)}) collective-permute-start(bf16[8,10,8,128]{3,2,1,0:T(8,128)(2,1)S(1)} %get-tuple-element.30.col_b), channel_id=1, source_target_pairs={{0,64},{64,128},{128,192},{192,256},{256,320},{320,384},{384,448},... | collective-permute-start | bytes 491528 | tf_op jit(solution)/shard_map/ppermute | solution.py:310
  9.3 13.5 %collective-permute-start.1 = (bf16[8,10,8,128]{3,2,1,0:T(8,128)(2,1)S(1)}, bf16[8,10,8,128]{3,2,1,0:T(8,128)(2,1)S(1)}, u32[]{:S(2)}, u32[]{:S(2)}) collective-permute-start(bf16[8,10,8,128]{3,2,1,0:T(8,128)(2,1)S(1)} %get-tuple-element.31.col_a), channel_id=1, source_target_pairs={{0,960},{64,0},{128,64},{192,128},{256,192},{320,256},{384,320},{4... | collective-permute-start | bytes 491528 | tf_op jit(solution)/shard_map/ppermute | solution.py:311
  22.8 0.8 count.1.counts
  23.6 0.0 collective-permute-done.col_l
  23.7 0.1 collective-permute-done.1.col_r
  23.8 13.8 %collective-permute-start.3 = (bf16[4,10,8,128]{3,2,1,0:T(8,128)(2,1)S(1)}, bf16[4,10,8,128]{3,2,1,0:T(8,128)(2,1)S(1)}, u32[]{:S(2)}, u32[]{:S(2)}) collective-permute-start(bf16[4,10,8,128]{3,2,1,0:T(8,128)(2,1)S(1)} %pad_maximum_fusion.1), channel_id=1, source_target_pairs={{0,63},{1,0},{2,1},{3,2},{4,3},{5,4},{6,5},{7,6},{8,7},{9,8},{10,9... | collective-permute-start | bytes 245768 | tf_op jit(solution)/shard_map/ppermute | solution.py:314
  37.6 0.0 copy-start.1
  37.6 0.0 copy-start.2
  37.6 1.9 %collective-permute-start.2 = (bf16[4,10,8,128]{3,2,1,0:T(8,128)(2,1)S(1)}, bf16[4,10,8,128]{3,2,1,0:T(8,128)(2,1)S(1)}, u32[]{:S(2)}, u32[]{:S(2)}) collective-permute-start(bf16[4,10,8,128]{3,2,1,0:T(8,128)(2,1)S(1)} %pad_maximum_fusion), channel_id=1, source_target_pairs={{0,1},{1,2},{2,3},{3,4},{4,5},{5,6},{6,7},{7,8},{8,9},{9,10},{10,1... | collective-permute-start | bytes 245768 | tf_op jit(solution)/shard_map/ppermute | solution.py:313
  39.6 0.0 copy-start.3
  39.6 8.1 %collective-permute-done.2.down = bf16[4,10,8,128]{3,2,1,0:T(8,128)(2,1)S(1)} collective-permute-done((bf16[4,10,8,128]{3,2,1,0:T(8,128)(2,1)S(1)}, bf16[4,10,8,128]{3,2,1,0:T(8,128)(2,1)S(1)}, u32[]{:S(2)}, u32[]{:S(2)}) %collective-permute-start.2) | collective-permute-done | bytes 81952 | tf_op jit(solution)/shard_map/ppermute | solution.py:313
  47.7 7.7 %interact.1 = (f32[8,128]{1,0:T(8,128)S(1)}, f32[3,8,128]{2,1,0:T(8,128)S(1)}, f32[8,128]{1,0:T(8,128)S(1)}, f32[8,128]{1,0:T(8,128)S(1)}) custom-call(bf16[8,10,8,128]{3,2,1,0:T(8,128)(2,1)S(1)} %get-tuple-element.31.col_a, bf16[8,10,8,128]{3,2,1,0:T(8,128)(2,1)S(1)} %get-tuple-element.30.col_b, bf16[8,10,8,128]{3,2,1,0:T(8,128)(2,1)S(1)} %collective-permute-done.col_l, ...), custom_call_target="tpu_custom_call" | custom-call | tf_op jit(solution)/shard_map/interact/pallas_call | solution.py:252
  55.4 1.9 %collective-permute-start.4 = (f32[8,128]{1,0:T(8,128)S(1)}, f32[8,128]{1,0:T(8,128)S(1)}, u32[]{:S(2)}, u32[]{:S(2)}) collective-permute-start(f32[8,128]{1,0:T(8,128)S(1)} %get-tuple-element.9), channel_id=1, source_target_pairs={{0,1},{1,2},{2,3},{3,4},{4,5},{5,6},{6,7},{7,8},{8,9},{9,10},{10,1... | collective-permute-start | bytes 12296 | tf_op jit(solution)/shard_map/ppermute | solution.py:319
  57.3 7.6 %collective-permute-start.5 = (f32[8,128]{1,0:T(8,128)S(1)}, f32[8,128]{1,0:T(8,128)S(1)}, u32[]{:S(2)}, u32[]{:S(2)}) collective-permute-start(f32[8,128]{1,0:T(8,128)S(1)} %get-tuple-element.10), channel_id=1, source_target_pairs={{0,63},{1,0},{2,1},{3,2},{4,3},{5,4},{6,5},{7,6},{8,7},{9,8},{10,9... | collective-permute-start | bytes 12296 | tf_op jit(solution)/shard_map/ppermute | solution.py:318
  64.9 0.1 broadcast_and_fusion
  65.0 0.7 collective-permute-done.5
  65.6 0.7 slice-done
  66.3 5.2 %collective-permute-start.7 = (f32[3,8,128]{2,1,0:T(8,128)S(1)}, f32[3,8,128]{2,1,0:T(8,128)S(1)}, u32[]{:S(2)}, u32[]{:S(2)}) collective-permute-start(f32[3,8,128]{2,1,0:T(8,128)S(1)} %select_add_fusion), channel_id=1, source_target_pairs={{0,960},{64,0},{128,64},{192,128},{256,192},{320,256},{384,320},{4... | collective-permute-start | bytes 36872 | tf_op jit(solution)/shard_map/ppermute | solution.py:332
  71.6 1.9 %collective-permute-start.6 = (f32[3,8,128]{2,1,0:T(8,128)S(1)}, f32[3,8,128]{2,1,0:T(8,128)S(1)}, u32[]{:S(2)}, u32[]{:S(2)}) collective-permute-start(f32[3,8,128]{2,1,0:T(8,128)S(1)} %select_add_fusion), channel_id=1, source_target_pairs={{0,64},{64,128},{128,192},{192,256},{256,320},{320,384},{384,448},... | collective-permute-start | bytes 36872 | tf_op jit(solution)/shard_map/ppermute | solution.py:331
  73.5 0.1 reshape.292
  73.6 0.6 broadcast_in_dim.64
  74.2 8.0 %all-to-all-start = ((f32[64,1,128]{2,1,0:T(1,128)}), f32[64,1,128]{2,1,0:T(1,128)S(1)}, u32[]{:S(2)}, u32[]{:S(2)}) async-start(f32[64,1,128]{2,1,0:T(1,128)} %broadcast_in_dim.64), calls=%async_computation | async-start | bytes 65536 | tf_op jit(solution)/shard_map/all_to_all | solution.py:322
  82.3 0.1 reshape_squeeze.3
  82.4 0.6 copy.81
  83.0 0.1 reshape.293
  83.1 0.1 reshape.295
  83.2 0.1 reshape.294
  83.4 8.0 %all-to-all-done = f32[64,1,128]{2,1,0:T(1,128)S(1)} async-done(((f32[64,1,128]{2,1,0:T(1,128)}), f32[64,1,128]{2,1,0:T(1,128)S(1)}, u32[]{:S(2)}, u32[]{:S(2)}) %all-to-all-start) | async-done | bytes 32800 | tf_op jit(solution)/shard_map/all_to_all | solution.py:322
  91.4 0.6 broadcast_in_dim.65
  92.0 5.8 %all-to-all-start.1 = ((f32[16,1,128]{2,1,0:T(1,128)}), f32[16,1,128]{2,1,0:T(1,128)S(1)}, u32[]{:S(2)}, u32[]{:S(2)}) async-start(f32[16,1,128]{2,1,0:T(1,128)} %broadcast_in_dim.65), calls=%async_computation.1 | async-start | bytes 16384 | tf_op jit(solution)/shard_map/all_to_all | solution.py:334
  97.8 0.6 copy.80
  98.4 10.7 %all-to-all-done.1 = f32[16,1,128]{2,1,0:T(1,128)S(1)} async-done(((f32[16,1,128]{2,1,0:T(1,128)}), f32[16,1,128]{2,1,0:T(1,128)S(1)}, u32[]{:S(2)}, u32[]{:S(2)}) %all-to-all-start.1) | async-done | bytes 8224 | tf_op jit(solution)/shard_map/all_to_all | solution.py:334
  109.1 0.6 reduce_sum.19
  (39 shorter events, 0.3 us)
Async XLA Ops:
  0.6 0.8 copy-start.5
  2.8 0.7 copy-start.6
  3.7 1.0 copy-start.4
  4.7 18.1 %copy-start = (s32[2,8,8,32]{3,2,1,0:T(8,128)S(1)}, s32[2,8,8,32]{3,2,1,0:T(8,128)}, u32[]{:S(2)}) copy-start(s32[2,8,8,32]{3,2,1,0:T(8,128)} %neighbours.1) | copy-start | bytes 49156
  4.7 18.9 %collective-permute-start = (bf16[8,10,8,128]{3,2,1,0:T(8,128)(2,1)S(1)}, bf16[8,10,8,128]{3,2,1,0:T(8,128)(2,1)S(1)}, u32[]{:S(2)}, u32[]{:S(2)}) collective-permute-start(bf16[8,10,8,128]{3,2,1,0:T(8,128)(2,1)S(1)} %get-tuple-element.30.col_b), channel_id=1, source_target_pairs={{0,64},{64,128},{128,192},{192,256},{256,320},{320,384},{384,448},... | collective-permute-start | bytes 491528 | tf_op jit(solution)/shard_map/ppermute | solution.py:310
  9.3 14.5 %collective-permute-start.1 = (bf16[8,10,8,128]{3,2,1,0:T(8,128)(2,1)S(1)}, bf16[8,10,8,128]{3,2,1,0:T(8,128)(2,1)S(1)}, u32[]{:S(2)}, u32[]{:S(2)}) collective-permute-start(bf16[8,10,8,128]{3,2,1,0:T(8,128)(2,1)S(1)} %get-tuple-element.31.col_a), channel_id=1, source_target_pairs={{0,960},{64,0},{128,64},{192,128},{256,192},{320,256},{384,320},{4... | collective-permute-start | bytes 491528 | tf_op jit(solution)/shard_map/ppermute | solution.py:311
  23.8 15.8 %collective-permute-start.3 = (bf16[4,10,8,128]{3,2,1,0:T(8,128)(2,1)S(1)}, bf16[4,10,8,128]{3,2,1,0:T(8,128)(2,1)S(1)}, u32[]{:S(2)}, u32[]{:S(2)}) collective-permute-start(bf16[4,10,8,128]{3,2,1,0:T(8,128)(2,1)S(1)} %pad_maximum_fusion.1), channel_id=1, source_target_pairs={{0,63},{1,0},{2,1},{3,2},{4,3},{5,4},{6,5},{7,6},{8,7},{9,8},{10,9... | collective-permute-start | bytes 245768 | tf_op jit(solution)/shard_map/ppermute | solution.py:314
  37.6 10.1 %copy-start.1 = (bf16[128,128]{1,0:T(8,128)(2,1)S(1)}, bf16[128,128]{1,0:T(8,128)(2,1)}, u32[]{:S(2)}) copy-start(bf16[128,128]{1,0:T(8,128)(2,1)} %mix.1) | copy-start | bytes 98308
  37.6 10.1 %copy-start.2 = (f32[7,8,128]{2,1,0:T(8,128)S(1)}, f32[7,8,128]{2,1,0:T(8,128)}, u32[]{:S(2)}) copy-start(f32[7,8,128]{2,1,0:T(8,128)} %weight.1) | copy-start | bytes 86020
  37.6 10.1 %collective-permute-start.2 = (bf16[4,10,8,128]{3,2,1,0:T(8,128)(2,1)S(1)}, bf16[4,10,8,128]{3,2,1,0:T(8,128)(2,1)S(1)}, u32[]{:S(2)}, u32[]{:S(2)}) collective-permute-start(bf16[4,10,8,128]{3,2,1,0:T(8,128)(2,1)S(1)} %pad_maximum_fusion), channel_id=1, source_target_pairs={{0,1},{1,2},{2,3},{3,4},{4,5},{5,6},{6,7},{7,8},{8,9},{9,10},{10,1... | collective-permute-start | bytes 245768 | tf_op jit(solution)/shard_map/ppermute | solution.py:313
  39.6 8.2 %copy-start.3 = (f32[128]{0:T(128)S(1)}, f32[128]{0:T(128)}, u32[]{:S(2)}) copy-start(f32[128]{0:T(128)} %param.13) | copy-start | bytes 1540
  55.4 9.6 %collective-permute-start.4 = (f32[8,128]{1,0:T(8,128)S(1)}, f32[8,128]{1,0:T(8,128)S(1)}, u32[]{:S(2)}, u32[]{:S(2)}) collective-permute-start(f32[8,128]{1,0:T(8,128)S(1)} %get-tuple-element.9), channel_id=1, source_target_pairs={{0,1},{1,2},{2,3},{3,4},{4,5},{5,6},{6,7},{7,8},{8,9},{9,10},{10,1... | collective-permute-start | bytes 12296 | tf_op jit(solution)/shard_map/ppermute | solution.py:319
  57.3 8.3 %collective-permute-start.5 = (f32[8,128]{1,0:T(8,128)S(1)}, f32[8,128]{1,0:T(8,128)S(1)}, u32[]{:S(2)}, u32[]{:S(2)}) collective-permute-start(f32[8,128]{1,0:T(8,128)S(1)} %get-tuple-element.10), channel_id=1, source_target_pairs={{0,63},{1,0},{2,1},{3,2},{4,3},{5,4},{6,5},{7,6},{8,7},{9,8},{10,9... | collective-permute-start | bytes 12296 | tf_op jit(solution)/shard_map/ppermute | solution.py:318
  65.0 0.7 copy-start.7
  65.6 0.7 slice-start
  66.3 16.8 %collective-permute-start.7 = (f32[3,8,128]{2,1,0:T(8,128)S(1)}, f32[3,8,128]{2,1,0:T(8,128)S(1)}, u32[]{:S(2)}, u32[]{:S(2)}) collective-permute-start(f32[3,8,128]{2,1,0:T(8,128)S(1)} %select_add_fusion), channel_id=1, source_target_pairs={{0,960},{64,0},{128,64},{192,128},{256,192},{320,256},{384,320},{4... | collective-permute-start | bytes 36872 | tf_op jit(solution)/shard_map/ppermute | solution.py:332
  71.6 11.6 %collective-permute-start.6 = (f32[3,8,128]{2,1,0:T(8,128)S(1)}, f32[3,8,128]{2,1,0:T(8,128)S(1)}, u32[]{:S(2)}, u32[]{:S(2)}) collective-permute-start(f32[3,8,128]{2,1,0:T(8,128)S(1)} %select_add_fusion), channel_id=1, source_target_pairs={{0,64},{64,128},{128,192},{192,256},{256,320},{320,384},{384,448},... | collective-permute-start | bytes 36872 | tf_op jit(solution)/shard_map/ppermute | solution.py:331
  74.2 17.2 %all-to-all-start = ((f32[64,1,128]{2,1,0:T(1,128)}), f32[64,1,128]{2,1,0:T(1,128)S(1)}, u32[]{:S(2)}, u32[]{:S(2)}) async-start(f32[64,1,128]{2,1,0:T(1,128)} %broadcast_in_dim.64), calls=%async_computation | async-start | bytes 65536 | tf_op jit(solution)/shard_map/all_to_all | solution.py:322
  92.0 17.1 %all-to-all-start.1 = ((f32[16,1,128]{2,1,0:T(1,128)}), f32[16,1,128]{2,1,0:T(1,128)S(1)}, u32[]{:S(2)}, u32[]{:S(2)}) async-start(f32[16,1,128]{2,1,0:T(1,128)} %broadcast_in_dim.65), calls=%async_computation.1 | async-start | bytes 16384 | tf_op jit(solution)/shard_map/all_to_all | solution.py:334

commit v2 on v1

v2 whole, which is shorter than its diff:
```python
import math

import jax
import jax.numpy as jnp
from jax import lax
from jax.experimental import pallas as pl
from jax.experimental.pallas import tpu as pltpu
from jax.sharding import Mesh, PartitionSpec as P

C = 128
NB = 8
GROUPS = 4
ROWS = 32
LEAD = (0, 3, 3, 3, 5, 5, 5, 5, 5)
PLAIN = (4, 4, 4, 6, 6, 6, 6, 6)
PAIRED = (1, 1, 1, 2, 2, 2, 2, 2)
R3 = math.sqrt(3.0)
R5 = math.sqrt(5.0)
R15 = math.sqrt(15.0)
F32 = jnp.float32
BF16 = jnp.bfloat16
NT = (((1,), (1,)), ((), ()))


def pack_kernel(features, positions, occupied, neighbours, out):
    flat = [positions[axis, x] for axis in range(3) for x in range(2)]
    flat = flat + [occupied[x].astype(F32) for x in range(2)]
    flat = jnp.concatenate(flat, axis=0)
    flat = jnp.concatenate([flat, jnp.zeros((64, C - 8), F32)], axis=1)
    flat = jnp.concatenate([flat, jnp.zeros((64, C), F32)], axis=0).T[0:8]
    high = flat.astype(BF16).astype(F32)
    rest = flat - high
    middle = rest.astype(BF16).astype(F32)
    low = pltpu.roll((rest - middle), 2, 1)
    middle = pltpu.roll(middle, 1, 1)
    lane = lax.broadcasted_iota(jnp.int32, (8, C), 1)
    kind = jnp.where(lane < 64, lane & 15, 3)
    for x in range(2):
        for y in range(8):
            out[x, y, 0:9] = features[x, y]
            back = (C - (8 * x + y)) % C
            codes = jnp.concatenate(
                [jnp.zeros((8, 64), F32), neighbours[x, y].astype(F32), jnp.zeros((8, 32), F32)], axis=1
            )
            tile = jnp.where(kind == 2, pltpu.roll(low, back, 1), codes)
            tile = jnp.where(kind == 1, pltpu.roll(middle, back, 1), tile)
            tile = jnp.where(kind == 0, pltpu.roll(high, back, 1), tile)
            out[x, y, 9] = tile.astype(BF16)


def count(codes):
    lanes = lax.broadcasted_iota(jnp.int32, (ROWS, C), 1).astype(F32)
    rows = lax.broadcasted_iota(jnp.int32, (ROWS, C), 0)
    code = codes.astype(jnp.int32)
    cell = code >> 3
    step_x = (cell * 11) >> 5
    x = ((rows >> 3) & 1) + step_x
    y = (rows >> 4) + cell - 3 * step_x
    column = jnp.where(x == 0, 2, jnp.where(x == 3, 3, x - 1))
    place = jnp.where(code < 72, (y * 4 + column) * 8 + (code & 7), -1).astype(F32)
    total = jnp.zeros((ROWS, C), F32)
    for k in range(32):
        total = total + jnp.where(lanes == place[:, 64 + k : 65 + k], 1.0, 0.0)
    return total


def block_of(q):
    return pl.ds(pl.multiple_of(q * 64, 64), C)


def weighted(products, weight, path):
    total = None
    for b in range(NB):
        term = weight[path, b : b + 1, :] * products[ROWS * b : ROWS * (b + 1)]
        total = term if total is None else total + term
    return total


def forward_kernel(
    own, right, up, weight, mix, out_weight,
    energy_out, energies, table, edge, back,
    geometry, message,
):
    for m in range(10):
        for y in range(10):
            if y < 8:
                tiles = [own[1, y, m], right[0, y, m], own[0, y, m], right[1, y, m]]
            else:
                tiles = [up[i, y - 8, m] for i in (1, 2, 0, 3)]
            rows = jnp.concatenate([tile.astype(F32) for tile in tiles], axis=0)
            table[32 * y : 32 * y + 32, C * m : C * m + C] = rows.astype(BF16)

    piece = lax.broadcasted_iota(jnp.int32, (16, C), 1)
    which = lax.broadcasted_iota(jnp.int32, (16, C), 0) * 16
    pick_rows = jnp.where((which < 64) & (piece >= which) & (piece < which + 3), 1.0, 0.0).astype(BF16)
    piece = lax.broadcasted_iota(jnp.int32, (C, 4 * C), 0)
    which = (lax.broadcasted_iota(jnp.int32, (C, 4 * C), 1) >> 7) * 16
    pick_columns = jnp.where((piece >= which) & (piece < which + 3), 1.0, 0.0).astype(BF16)
    lane = lax.broadcasted_iota(jnp.int32, (1, C), 1)
    column = (lane >> 3) & 3
    place_x = jnp.where(column == 2, 0, jnp.where(column == 3, 3, column + 1))
    shift_x = place_x.astype(F32) * 5.0
    shift_y = (lane >> 5).astype(F32) * 5.0
    row = lax.broadcasted_iota(jnp.int32, (ROWS, C), 0)
    own_shift_x = ((row >> 3) & 1).astype(F32) * 5.0 + 5.0
    own_shift_y = (row >> 4).astype(F32) * 5.0 + 5.0

    def group_values(q):
        base = pl.multiple_of(q * 64, 64)
        return jnp.concatenate(
            [
                table[pl.ds(base + 32, 16), 9 * C : 10 * C],
                table[pl.ds(base + 64, 16), 9 * C : 10 * C],
            ],
            axis=0,
        )

    def forward(q, carry):
        block = block_of(q)
        around = lax.dot_general(
            pick_rows, table[block, 9 * C : 10 * C], NT, preferred_element_type=F32
        )
        mine = group_values(q)
        own_at = jnp.dot(mine, pick_columns, preferred_element_type=F32)
        rx = (around[0:1] + shift_x) - (own_at[:, 0:C] + own_shift_x)
        ry = (around[1:2] + shift_y) - (own_at[:, C : 2 * C] + own_shift_y)
        rz = around[2:3] - own_at[:, 2 * C : 3 * C]
        times = count(mine.astype(F32))
        dist_sq = rx * rx + ry * ry + rz * rz
        inside = (times > 0.5) & (dist_sq < 25.0)
        dist_sq = jnp.where(inside, dist_sq, 25.0)
        fall = jnp.where(inside, 1.0 - dist_sq * 0.04, 0.0)
        inv = lax.rsqrt(dist_sq)
        inv = inv * (1.5 - 0.5 * dist_sq * inv * inv)
        turn = dist_sq * inv * (math.pi / 5.0) - math.pi / 2.0
        sq = turn * turn
        cosine = jnp.full_like(sq, 1.0 / math.factorial(12))
        for order in (10, 8, 6, 4, 2, 0):
            sign = 1.0 if order % 4 == 0 else -1.0
            cosine = cosine * sq + sign / math.factorial(order)
        sine = jnp.full_like(sq, 1.0 / math.factorial(13))
        for order in (11, 9, 7, 5, 3, 1):
            sign = 1.0 if order % 4 == 1 else -1.0
            sine = sine * sq + sign / math.factorial(order)
        s_now, c_now = cosine, -sine * turn
        twice = 2.0 * c_now
        s_last, c_last = jnp.zeros_like(sq), jnp.ones_like(sq)
        amount = times * around[3:4]
        base = amount * fall * fall * inv
        slope = -(amount * fall) * (fall * inv * inv + 0.16)
        ux, uy, uz = rx * inv, ry * inv, rz * inv
        harmonics = (
            None,
            R3 * ux,
            R3 * uy,
            R3 * uz,
            R15 * ux * uy,
            R15 * uy * uz,
            (0.5 * R5) * (3.0 * uz * uz - 1.0),
            R15 * ux * uz,
            (0.5 * R15) * (ux * ux - uy * uy),
        )
        edge[q, 0] = inv
        for g in range(1, 9):
            edge[q, g] = harmonics[g]
        for b in range(NB):
            radial = s_now * base
            edge[q, 9 + b] = radial
            edge[q, 17 + b] = c_now * base * ((b + 1) * math.pi / 5.0) + s_now * slope
            spot = slice(ROWS * b, ROWS * b + ROWS)
            geometry[0, spot] = radial.astype(BF16)
            for g in range(1, 9):
                geometry[g, spot] = (radial * harmonics[g]).astype(BF16)
            s_now, s_last = twice * s_now - s_last, s_now
            c_now, c_last = twice * c_now - c_last, c_now
        messages = [None] * 9
        for m in (0, 2, 4, 6, 8):
            width = 1 if m == 8 else 2
            products = jnp.dot(
                geometry[0], table[block, C * m : C * (m + width)], preferred_element_type=F32
            )
            for j in range(width):
                path = 0 if m + j == 0 else PLAIN[m + j - 1]
                messages[m + j] = weighted(products[:, C * j : C * j + C], weight, path)
        first = table[block, 0:C]
        for g in range(1, 9):
            both = jnp.concatenate([first, table[block, C * g : C * g + C]], axis=1)
            products = jnp.dot(geometry[g], both, preferred_element_type=F32)
            messages[g] = messages[g] + weighted(products[:, :C], weight, LEAD[g])
            messages[0] = messages[0] + weighted(products[:, C:], weight, PAIRED[g - 1])
        for g in range(9):
            message[g] = messages[g].astype(BF16)
        mixed = jnp.dot(message[...].reshape(9 * ROWS, C), mix[...], preferred_element_type=F32)
        mixed = mixed.reshape(9, ROWS, C)
        z = mixed[0]
        for g in range(1, 9):
            z = z + mixed[g] * mixed[g]
        gate = 1.0 / (1.0 + jnp.exp(-z))
        scale = own_at[:, 3 * C : 4 * C] * out_weight[0:1]
        spot = pl.ds(pl.multiple_of(q * ROWS, ROWS), ROWS)
        energies[spot] = scale * (z * gate)
        grad = scale * gate * (1.0 + z * (1.0 - gate))
        message[0] = grad.astype(BF16)
        grad = 2.0 * grad
        for g in range(1, 9):
            message[g] = (grad * mixed[g]).astype(BF16)
        returned = lax.dot_general(
            message[...].reshape(9 * ROWS, C), mix[...], NT, preferred_element_type=F32
        )
        back[q] = returned.reshape(9, ROWS, C)
        return carry

    lax.fori_loop(0, GROUPS, forward, 0)
    energy_out[...] = jnp.zeros_like(energy_out)
    energy_out[0:1] = jnp.sum(energies[...].T, axis=0, keepdims=True)


def backward_kernel(table, edge, back, weight, energy, near_out, send_up, values, near):
    near[...] = jnp.zeros_like(near)

    def backward(q, carry):
        block = block_of(q)
        first = table[block, 0:C]
        spot = pl.ds(pl.multiple_of(q * ROWS, ROWS), ROWS)

        def spread(g, path):
            return jnp.concatenate(
                [(weight[path, b : b + 1, :] * back[q, g]).astype(BF16) for b in range(NB)], axis=0
            )

        wide = jnp.concatenate([spread(0, 0)] + [spread(g, PLAIN[g - 1]) for g in range(1, 9)], axis=1)
        grads = lax.dot_general(wide, table[block, 0 : 9 * C], NT, preferred_element_type=F32)
        along = [None] * NB
        sums = [None] * 9
        for b in range(NB):
            along[b] = grads[ROWS * b : ROWS * b + ROWS]
        paired = {1: spread(0, 1), 2: spread(0, 2)}
        for g in range(1, 9):
            both = jnp.concatenate([first, table[block, C * g : C * g + C]], axis=1)
            wide = jnp.concatenate([spread(g, LEAD[g]), paired[PAIRED[g - 1]]], axis=1)
            grads = lax.dot_general(wide, both, NT, preferred_element_type=F32)
            harmonic = edge[q, g]
            total = None
            for b in range(NB):
                part = grads[ROWS * b : ROWS * b + ROWS]
                along[b] = along[b] + part * harmonic
                term = part * edge[q, 9 + b]
                total = term if total is None else total + term
            sums[g] = total
        radial = None
        for b in range(NB):
            term = along[b] * edge[q, 17 + b]
            radial = term if radial is None else radial + term
        inv = edge[q, 0]
        ux, uy, uz = (edge[q, g] * (1.0 / R3) for g in (1, 2, 3))
        vx = R3 * sums[1] + R15 * (uy * sums[4] + uz * sums[7] + ux * sums[8])
        vy = R3 * sums[2] + R15 * (ux * sums[4] + uz * sums[5] - uy * sums[8])
        vz = R3 * sums[3] + R15 * (uy * sums[5] + ux * sums[7]) + (3.0 * R5) * uz * sums[6]
        inward = radial - inv * (ux * vx + uy * vy + uz * vz)
        for axis, (v, unit) in enumerate(((vx, ux), (vy, uy), (vz, uz))):
            gradient = inward * unit + inv * v
            values[axis, spot] = gradient
            near[axis, pl.ds(q, 1)] = jnp.sum(gradient, axis=0, keepdims=True)
        return carry

    lax.fori_loop(0, GROUPS, backward, 0)
    send_up[...] = jnp.zeros_like(send_up)
    near_out[...] = jnp.zeros_like(near_out)
    lane = lax.broadcasted_iota(jnp.int32, (8, C), 1)
    for kind in range(4):
        if kind < 3:
            part = near[kind]
            later = pltpu.roll(pltpu.roll(part, 64, 1), 1, 0)
            pairs = -(part + later)
            own = jnp.sum(values[kind].T, axis=0, keepdims=True)
        else:
            pairs = jnp.zeros((8, C), F32)
            own = energy[0:1]
        own = jnp.concatenate(
            [own] + [pltpu.roll(own, C - 32 * q, 1) for q in range(1, 4)] + [jnp.zeros((4, C), F32)], axis=0
        )
        pairs = pairs + jnp.where((lane >= 32) & (lane < 48), pltpu.roll(own, 32, 1), 0.0)
        own = pltpu.roll(pltpu.roll(own, C - 16, 1), 1, 0)
        pairs = jnp.where(lane < 64, pairs + jnp.where(lane < 16, own, 0.0), 0.0)
        near_out[kind] = pairs
        send_up[kind : kind + 1] = pairs[4:5]


VMEM = pl.BlockSpec(memory_space=pltpu.VMEM)


def pack_call(features, positions, occupied, neighbours):
    return pl.pallas_call(
        pack_kernel,
        out_shape=jax.ShapeDtypeStruct((2, 8, 10, 8, C), BF16),
        in_specs=[VMEM] * 4,
        out_specs=VMEM,
        compiler_params=pltpu.CompilerParams(vmem_limit_bytes=8 * 1024 * 1024),
        name="pack",
    )(features, positions, occupied, neighbours)


def forward_call(*arrays):
    return pl.pallas_call(
        forward_kernel,
        out_shape=(
            jax.ShapeDtypeStruct((8, C), F32),
            jax.ShapeDtypeStruct((C, C), F32),
            jax.ShapeDtypeStruct((320, 10 * C), BF16),
            jax.ShapeDtypeStruct((GROUPS, 25, ROWS, C), F32),
            jax.ShapeDtypeStruct((GROUPS, 9, ROWS, C), F32),
        ),
        in_specs=[VMEM] * 6,
        out_specs=(VMEM,) * 5,
        scratch_shapes=[
            pltpu.VMEM((9, NB * ROWS, C), BF16),
            pltpu.VMEM((9, ROWS, C), BF16),
        ],
        compiler_params=pltpu.CompilerParams(vmem_limit_bytes=20 * 1024 * 1024),
        cost_estimate=pl.CostEstimate(flops=4_000_000_000, bytes_accessed=8_000_000, transcendentals=0),
        name="forward",
    )(*arrays)


def backward_call(*arrays):
    return pl.pallas_call(
        backward_kernel,
        out_shape=(jax.ShapeDtypeStruct((4, 8, C), F32), jax.ShapeDtypeStruct((8, C), F32)),
        in_specs=[VMEM] * 5,
        out_specs=(VMEM,) * 2,
        scratch_shapes=[pltpu.VMEM((3, C, C), F32), pltpu.VMEM((3, 8, C), F32)],
        compiler_params=pltpu.CompilerParams(vmem_limit_bytes=20 * 1024 * 1024),
        cost_estimate=pl.CostEstimate(flops=4_000_000_000, bytes_accessed=8_000_000, transcendentals=0),
        name="backward",
    )(*arrays)


def ring(size, step):
    return [(i, (i + step) % size) for i in range(size)]


def on_device(features, positions, occupied, neighbours, radial_weight, mix_weight, out_weight, *, outer, inner):
    gy = outer + inner
    size_x = lax.axis_size("gx")
    size_y = lax.axis_size(gy)
    own = pack_call(jnp.transpose(features, (0, 1, 3, 2, 4)), positions, occupied, neighbours)
    right = lax.ppermute(own, "gx", ring(size_x, -1))
    up = lax.ppermute(jnp.concatenate([own[:, :2], right[:, :2]], axis=0), gy, ring(size_y, -1))
    energy, _, table, edge, back = forward_call(
        own, right, up, radial_weight, mix_weight, out_weight[None]
    )
    plane = size_x * lax.axis_size(outer)
    gathered = lax.all_to_all(
        jnp.broadcast_to(energy[None, :1], (plane, 1, C)), ("gx",) + outer, 0, 0
    )
    near, send_up = backward_call(table, edge, back, radial_weight, energy)
    energy_plane = jnp.sum(gathered, axis=0)
    depth = lax.axis_size(inner)
    gathered = lax.all_to_all(jnp.broadcast_to(energy_plane[None], (depth, 1, C)), inner, 0, 0)
    from_down = lax.ppermute(send_up, gy, ring(size_y, 1))
    near = near.at[:, 0].add(from_down[:4])[:, :4]
    from_left = lax.ppermute(near, "gx", ring(size_x, 1))
    total_energy = jnp.sum(gathered)

    def column(block, place):
        return block[:, :, :64].reshape(4, 8, 4, 8)[:, :, place]

    first = column(near, 2) + column(from_left, 1)
    second = column(near, 0) + column(from_left, 3)
    cells = jnp.stack([first, second], axis=1)
    return cells[:3], cells[3], total_energy


def solution(mesh):
    size_x, size_y = mesh.shape["gx"], mesh.shape["gy"]
    depth = 16 if size_y % 16 == 0 else size_y // 2
    split = Mesh(mesh.devices.reshape(size_x, size_y // depth, depth), ("gx", "gya", "gyb"))
    outer, inner = ("gya",), ("gyb",)
    gy = outer + inner
    in_specs = (
        P("gx", gy, None, None, None),
        P(None, "gx", gy, None),
        P("gx", gy, None),
        P("gx", gy, None, None),
        P(),
        P(),
        P(),
    )
    out_specs = (P(None, "gx", gy, None), P("gx", gy, None), P())

    def program(*arrays):
        return on_device(*arrays, outer=outer, inner=inner)

    return jax.shard_map(
        program, mesh=split, in_specs=in_specs, out_specs=out_specs, check_vma=False
    )
```

time: 110 us -> 91.3 us (0.83)
  waiting for transfers between devices: 27.6 us -> 17.3 us
  starting transfers between devices: 64.1 us -> 54.7 us
    ppermute x6 -> x2, starting transfers between devices: 46.5 us -> 29.7 us  [the longest x1 16.1 us: on_device(): right = lax.ppermute(own, 'gx', ring(size_x, -1))]
    all_to_all x1, waiting for transfers between devices: 8 us -> 1.68 us  [on_device(): lax.all_to_all(jnp.broadcast_to(energy[None, :1], (plane, 1, C)), ('gx',)...]
    ppermute x6 -> x2, waiting for transfers between devices: 8.88 us -> 3.46 us  [the longest x1 2.24 us: on_device(): lax.ppermute(jnp.concatenate([own[:, :2], right[:, :2]], axis=0), gy, rin...]
    all_to_all x1, starting transfers between devices: 5.77 us -> 9.62 us  [on_device(): lax.all_to_all(jnp.broadcast_to(energy_plane[None], (depth, 1, C)), inner...]
    ppermute x1, starting transfers between devices: 1.92 us -> 4.93 us  [on_device(): from_left = lax.ppermute(near, 'gx', ring(size_x, 1))]
    unnamed x18 -> x16, local copies, waits for them, and re-layouts: 2.53 us -> 5.39 us
    ppermute x1, waiting for transfers between devices: 0.01 us -> 1.5 us  [on_device(): from_left = lax.ppermute(near, 'gx', ring(size_x, 1))]
    pallas_call x2 -> x3, Pallas kernels: 8.48 us -> 9.02 us  [the longest x1 5.82 us: forward_call(): pl.pallas_call(forward_kernel, out_shape=(jax.ShapeDtypeStruct((8, C), F3...]
  transfers between devices with their start and end apart: 10 -> 6, of which waited for: 5 -> 5; matrix products, arithmetic and copies ran while one was open for 2% -> 2% of each run, Pallas kernels for 1% -> 0%
where the time goes in v2:
time: 91.3 us; the launch traced here: 90.7 us
  starting transfers between devices  54.7 us (60%)
  waiting for transfers between devices  17.3 us (19%)
  Pallas kernels  9.02 us (10%)
  local copies, waits for them, and re-layouts  6.93 us (8%)
  other arithmetic  1.87 us (2%)
    ppermute x1, starting transfers between devices, on_device(): right = lax.ppermute(own, 'gx', ring(size_x, -1))  16.1 us
    ppermute x1, starting transfers between devices, on_device(): lax.ppermute(jnp.concatenate([own[:, :2], right[:, :2]], axis=0), gy, rin...  13.6 us
    all_to_all x1, waiting for transfers between devices, on_device(): lax.all_to_all(jnp.broadcast_to(energy_plane[None], (depth, 1, C)), inner...  10.7 us
    all_to_all x1, starting transfers between devices, on_device(): lax.all_to_all(jnp.broadcast_to(energy_plane[None], (depth, 1, C)), inner...  9.62 us
    all_to_all x1, starting transfers between devices, on_device(): lax.all_to_all(jnp.broadcast_to(energy[None, :1], (plane, 1, C)), ('gx',)...  8.57 us
    pallas_call x1, Pallas kernels, forward_call(): pl.pallas_call(forward_kernel, out_shape=(jax.ShapeDtypeStruct((8, C), F3...  5.82 us
    unnamed x16, local copies, waits for them, and re-layouts  5.39 us
    ppermute x1, starting transfers between devices, on_device(): from_left = lax.ppermute(near, 'gx', ring(size_x, 1))  4.93 us
  transfers between devices with their start and end apart: 6, of which 5 were waited for; matrix products, arithmetic and copies ran while one was open for 2% of the time, Pallas kernels for 0%

profile of v2, /device:TPU:1, one launch (start us, length us, event | category | flops | bytes accessed | tf_op | source)
XLA Modules:
  0.0 90.7 jit_solution(1107726174303337693)
XLA Ops:
  0.6 0.0 copy-start
  0.6 1.0 %copy-done = bf16[2,8,8,9,128]{4,2,3,1,0:T(8,128)(2,1)S(1)} copy-done((bf16[2,8,8,9,128]{4,2,3,1,0:T(8,128)(2,1)S(1)}, bf16[2,8,8,9,128]{4,2,3,1,0:T(8,128)(2,1)}, u32[]{:S(2)}) %copy-start) | copy-done | bytes 294936
  1.6 0.0 copy-start.1
  1.6 0.8 copy-done.1
  2.4 0.0 copy-start.2
  2.4 0.7 copy-done.2
  3.2 0.0 copy-start.3
  3.2 0.7 copy-done.3
  3.9 0.2 pack.1.own
  4.1 16.1 %collective-permute-start = (bf16[2,8,10,8,128]{4,3,2,1,0:T(8,128)(2,1)S(1)}, bf16[2,8,10,8,128]{4,3,2,1,0:T(8,128)(2,1)S(1)}, u32[]{:S(2)}, u32[]{:S(2)}) collective-permute-start(bf16[2,8,10,8,128]{4,3,2,1,0:T(8,128)(2,1)S(1)} %pack.1.own), channel_id=1, source_target_pairs={{0,960},{64,0},{128,64},{192,128},{256,192},{320,256},{384,320},{4... | collective-permute-start | bytes 983048 | tf_op jit(solution)/shard_map/ppermute | solution.py:347
  20.2 1.2 %collective-permute-done.right = bf16[2,8,10,8,128]{4,3,2,1,0:T(8,128)(2,1)S(1)} collective-permute-done((bf16[2,8,10,8,128]{4,3,2,1,0:T(8,128)(2,1)S(1)}, bf16[2,8,10,8,128]{4,3,2,1,0:T(8,128)(2,1)S(1)}, u32[]{:S(2)}, u32[]{:S(2)}) %collective-permute-start) | collective-permute-done | bytes 327712 | tf_op jit(solution)/shard_map/ppermute | solution.py:347
  21.4 13.6 %collective-permute-start.1 = (bf16[4,2,10,8,128]{4,3,2,1,0:T(8,128)(2,1)S(1)}, bf16[4,2,10,8,128]{4,3,2,1,0:T(8,128)(2,1)S(1)}, u32[]{:S(2)}, u32[]{:S(2)}) collective-permute-start(bf16[4,2,10,8,128]{4,3,2,1,0:T(8,128)(2,1)S(1)} %pad_maximum_fusion), channel_id=1, source_target_pairs={{0,63},{1,0},{2,1},{3,2},{4,3},{5,4},{6,5},{7,6},{8,7},{9,8},{10,9... | collective-permute-start | bytes 491528 | tf_op jit(solution)/shard_map/ppermute | solution.py:348
  35.0 2.2 %collective-permute-done.1.up = bf16[4,2,10,8,128]{4,3,2,1,0:T(8,128)(2,1)S(1)} collective-permute-done((bf16[4,2,10,8,128]{4,3,2,1,0:T(8,128)(2,1)S(1)}, bf16[4,2,10,8,128]{4,3,2,1,0:T(8,128)(2,1)S(1)}, u32[]{:S(2)}, u32[]{:S(2)}) %collective-permute-start.1) | collective-permute-done | bytes 163872 | tf_op jit(solution)/shard_map/ppermute | solution.py:348
  37.3 0.0 copy-start.4
  37.3 0.8 copy-done.4
  38.0 0.0 copy-start.5
  38.0 0.7 copy-done.5
  38.8 0.0 copy-start.7
  38.8 0.7 copy-done.7
  39.5 0.0 copy-start.6
  39.5 5.8 %forward.1 = (f32[8,128]{1,0:T(8,128)S(1)}, f32[128,128]{1,0:T(8,128)}, bf16[320,1280]{1,0:T(8,128)(2,1)S(1)}, f32[4,25,32,128]{3,2,1,0:T(8,128)S(1)}, f32[4,9,32,128]{3,2,1,0:T(8,128)S(1)}) custom-call(bf16[2,8,10,8,128]{4,3,2,1,0:T(8,128)(2,1)S(1)} %pack.1.own, bf16[2,8,10,8,128]{4,3,2,1,0:T(8,128)(2,1)S(1)} %collective-permute-done.right, ...), custom_call_target="tpu_custom_call" | custom-call | flops 4000000000 | bytes 8000000 | tf_op jit(solution)/shard_map/forward/pallas_call | solution.py:304
  45.3 0.0 copy-done.6
  45.3 3.0 %backward.1 = (f32[4,8,128]{2,1,0:T(8,128)S(1)}, f32[8,128]{1,0:T(8,128)S(1)}) custom-call(bf16[320,1280]{1,0:T(8,128)(2,1)S(1)} %get-tuple-element.21.table, f32[4,25,32,128]{3,2,1,0:T(8,128)S(1)} %get-tuple-element.22.edge, f32[4,9,32,128]{3,2,1,0:T(8,128)S(1)} %get-tuple-element.23.back, f32[7,8,128]{2,1,0:T(8,128)S(1)} %copy-done.6, ...), custom_call_target="tpu_custom_call" | custom-call | flops 4000000000 | bytes 8000000 | tf_op jit(solution)/shard_map/backward/pallas_call | solution.py:326
  48.2 1.9 %collective-permute-start.2 = (f32[8,128]{1,0:T(8,128)S(1)}, f32[8,128]{1,0:T(8,128)S(1)}, u32[]{:S(2)}, u32[]{:S(2)}) collective-permute-start(f32[8,128]{1,0:T(8,128)S(1)} %get-tuple-element.26), channel_id=1, source_target_pairs={{0,1},{1,2},{2,3},{3,4},{4,5},{5,6},{6,7},{7,8},{8,9},{9,10},{10,1... | collective-permute-start | bytes 12296 | tf_op jit(solution)/shard_map/ppermute | solution.py:360
  50.2 0.6 broadcast_in_dim.19
  50.8 8.6 %all-to-all-start = ((f32[64,1,128]{2,1,0:T(1,128)}), f32[64,1,128]{2,1,0:T(1,128)S(1)}, u32[]{:S(2)}, u32[]{:S(2)}) async-start(f32[64,1,128]{2,1,0:T(1,128)} %broadcast_in_dim.19), calls=%async_computation | async-start | bytes 65536 | tf_op jit(solution)/shard_map/all_to_all | solution.py:353
  59.4 0.0 collective-permute-done.2
  59.5 4.9 %collective-permute-start.3 = (f32[4,4,128]{2,1,0:T(4,128)S(1)}, f32[4,4,128]{2,1,0:T(4,128)S(1)}, u32[]{:S(2)}, u32[]{:S(2)}) collective-permute-start(f32[4,4,128]{2,1,0:T(4,128)S(1)} %slice.83), channel_id=1, source_target_pairs={{0,64},{64,128},{128,192},{192,256},{256,320},{320,384},{384,448},... | collective-permute-start | bytes 24584 | tf_op jit(solution)/shard_map/ppermute | solution.py:362
  64.4 0.1 reshape.92
  64.6 1.5 %collective-permute-done.3 = f32[4,4,128]{2,1,0:T(4,128)S(1)} collective-permute-done((f32[4,4,128]{2,1,0:T(4,128)S(1)}, f32[4,4,128]{2,1,0:T(4,128)S(1)}, u32[]{:S(2)}, u32[]{:S(2)}) %collective-permute-start.3) | collective-permute-done | bytes 8224 | tf_op jit(solution)/shard_map/ppermute | solution.py:362
  66.1 0.1 reshape.93
  66.2 0.6 fusion
  66.8 1.7 %all-to-all-done = f32[64,1,128]{2,1,0:T(1,128)S(1)} async-done(((f32[64,1,128]{2,1,0:T(1,128)}), f32[64,1,128]{2,1,0:T(1,128)S(1)}, u32[]{:S(2)}, u32[]{:S(2)}) %all-to-all-start) | async-done | bytes 32800 | tf_op jit(solution)/shard_map/all_to_all | solution.py:353
  68.5 0.6 broadcast_in_dim.20
  69.1 9.6 %all-to-all-start.1 = ((f32[16,1,128]{2,1,0:T(1,128)}), f32[16,1,128]{2,1,0:T(1,128)S(1)}, u32[]{:S(2)}, u32[]{:S(2)}) async-start(f32[16,1,128]{2,1,0:T(1,128)} %broadcast_in_dim.20), calls=%async_computation.1 | async-start | bytes 16384 | tf_op jit(solution)/shard_map/all_to_all | solution.py:359
  78.8 0.6 fusion.1
  79.4 10.7 %all-to-all-done.1 = f32[16,1,128]{2,1,0:T(1,128)S(1)} async-done(((f32[16,1,128]{2,1,0:T(1,128)}), f32[16,1,128]{2,1,0:T(1,128)S(1)}, u32[]{:S(2)}, u32[]{:S(2)}) %all-to-all-start.1) | async-done | bytes 8224 | tf_op jit(solution)/shard_map/all_to_all | solution.py:359
  90.1 0.6 reduce_sum.19
  (13 shorter events, 0.2 us)
Async XLA Ops:
  0.6 1.0 %copy-start = (bf16[2,8,8,9,128]{4,2,3,1,0:T(8,128)(2,1)S(1)}, bf16[2,8,8,9,128]{4,2,3,1,0:T(8,128)(2,1)}, u32[]{:S(2)}) copy-start(bf16[2,8,8,9,128]{4,2,3,1,0:T(8,128)(2,1)} %param.9) | copy-start | bytes 884740
  1.6 0.8 copy-start.1
  2.4 0.7 copy-start.2
  3.2 0.7 copy-start.3
  4.1 17.3 %collective-permute-start = (bf16[2,8,10,8,128]{4,3,2,1,0:T(8,128)(2,1)S(1)}, bf16[2,8,10,8,128]{4,3,2,1,0:T(8,128)(2,1)S(1)}, u32[]{:S(2)}, u32[]{:S(2)}) collective-permute-start(bf16[2,8,10,8,128]{4,3,2,1,0:T(8,128)(2,1)S(1)} %pack.1.own), channel_id=1, source_target_pairs={{0,960},{64,0},{128,64},{192,128},{256,192},{320,256},{384,320},{4... | collective-permute-start | bytes 983048 | tf_op jit(solution)/shard_map/ppermute | solution.py:347
  21.4 15.8 %collective-permute-start.1 = (bf16[4,2,10,8,128]{4,3,2,1,0:T(8,128)(2,1)S(1)}, bf16[4,2,10,8,128]{4,3,2,1,0:T(8,128)(2,1)S(1)}, u32[]{:S(2)}, u32[]{:S(2)}) collective-permute-start(bf16[4,2,10,8,128]{4,3,2,1,0:T(8,128)(2,1)S(1)} %pad_maximum_fusion), channel_id=1, source_target_pairs={{0,63},{1,0},{2,1},{3,2},{4,3},{5,4},{6,5},{7,6},{8,7},{9,8},{10,9... | collective-permute-start | bytes 491528 | tf_op jit(solution)/shard_map/ppermute | solution.py:348
  37.3 0.8 copy-start.4
  38.0 0.7 copy-start.5
  38.8 0.7 copy-start.7
  39.5 5.8 %copy-start.6 = (f32[7,8,128]{2,1,0:T(8,128)S(1)}, f32[7,8,128]{2,1,0:T(8,128)}, u32[]{:S(2)}) copy-start(f32[7,8,128]{2,1,0:T(8,128)} %weight.3) | copy-start | bytes 86020
  48.2 11.1 %collective-permute-start.2 = (f32[8,128]{1,0:T(8,128)S(1)}, f32[8,128]{1,0:T(8,128)S(1)}, u32[]{:S(2)}, u32[]{:S(2)}) collective-permute-start(f32[8,128]{1,0:T(8,128)S(1)} %get-tuple-element.26), channel_id=1, source_target_pairs={{0,1},{1,2},{2,3},{3,4},{4,5},{5,6},{6,7},{7,8},{8,9},{9,10},{10,1... | collective-permute-start | bytes 12296 | tf_op jit(solution)/shard_map/ppermute | solution.py:360
  50.8 17.7 %all-to-all-start = ((f32[64,1,128]{2,1,0:T(1,128)}), f32[64,1,128]{2,1,0:T(1,128)S(1)}, u32[]{:S(2)}, u32[]{:S(2)}) async-start(f32[64,1,128]{2,1,0:T(1,128)} %broadcast_in_dim.19), calls=%async_computation | async-start | bytes 65536 | tf_op jit(solution)/shard_map/all_to_all | solution.py:353
  59.5 6.6 %collective-permute-start.3 = (f32[4,4,128]{2,1,0:T(4,128)S(1)}, f32[4,4,128]{2,1,0:T(4,128)S(1)}, u32[]{:S(2)}, u32[]{:S(2)}) collective-permute-start(f32[4,4,128]{2,1,0:T(4,128)S(1)} %slice.83), channel_id=1, source_target_pairs={{0,64},{64,128},{128,192},{192,256},{256,320},{320,384},{384,448},... | collective-permute-start | bytes 24584 | tf_op jit(solution)/shard_map/ppermute | solution.py:362
  69.1 20.9 %all-to-all-start.1 = ((f32[16,1,128]{2,1,0:T(1,128)}), f32[16,1,128]{2,1,0:T(1,128)S(1)}, u32[]{:S(2)}, u32[]{:S(2)}) async-start(f32[16,1,128]{2,1,0:T(1,128)} %broadcast_in_dim.20), calls=%async_computation.1 | async-start | bytes 16384 | tf_op jit(solution)/shard_map/all_to_all | solution.py:359

commit v3 on v2

--- a/solution.py
+++ b/solution.py
@@ -22,7 +22,22 @@
 NT = (((1,), (1,)), ((), ()))
 
 
-def pack_kernel(features, positions, occupied, neighbours, out):
+def pack_kernel(features, places, present, lists, out, positions, occupied, neighbours, done):
+    moves = [
+        pltpu.make_async_copy(source, target, done.at[i])
+        for i, (source, target) in enumerate(
+            (
+                (places, positions),
+                (present, occupied),
+                (lists, neighbours),
+                (features, out.at[:, :, 0:9]),
+            )
+        )
+    ]
+    for move in moves:
+        move.start()
+    for move in moves[:3]:
+        move.wait()
     flat = [positions[axis, x] for axis in range(3) for x in range(2)]
     flat = flat + [occupied[x].astype(F32) for x in range(2)]
     flat = jnp.concatenate(flat, axis=0)
@@ -37,7 +52,6 @@
     kind = jnp.where(lane < 64, lane & 15, 3)
     for x in range(2):
         for y in range(8):
-            out[x, y, 0:9] = features[x, y]
             back = (C - (8 * x + y)) % C
             codes = jnp.concatenate(
                 [jnp.zeros((8, 64), F32), neighbours[x, y].astype(F32), jnp.zeros((8, 32), F32)], axis=1
@@ -46,6 +60,7 @@
             tile = jnp.where(kind == 1, pltpu.roll(middle, back, 1), tile)
             tile = jnp.where(kind == 0, pltpu.roll(high, back, 1), tile)
             out[x, y, 9] = tile.astype(BF16)
+    moves[3].wait()
 
 
 def count(codes):
@@ -76,20 +91,7 @@
     return total
 
 
-def forward_kernel(
-    own, right, up, weight, mix, out_weight,
-    energy_out, energies, table, edge, back,
-    geometry, message,
-):
-    for m in range(10):
-        for y in range(10):
-            if y < 8:
-                tiles = [own[1, y, m], right[0, y, m], own[0, y, m], right[1, y, m]]
-            else:
-                tiles = [up[i, y - 8, m] for i in (1, 2, 0, 3)]
-            rows = jnp.concatenate([tile.astype(F32) for tile in tiles], axis=0)
-            table[32 * y : 32 * y + 32, C * m : C * m + C] = rows.astype(BF16)
-
+def group_forward(table, weight, mix, out_weight, edge, back, energies, geometry, message):
     piece = lax.broadcasted_iota(jnp.int32, (16, C), 1)
     which = lax.broadcasted_iota(jnp.int32, (16, C), 0) * 16
     pick_rows = jnp.where((which < 64) & (piece >= which) & (piece < which + 3), 1.0, 0.0).astype(BF16)
@@ -210,18 +212,48 @@
         back[q] = returned.reshape(9, ROWS, C)
         return carry
 
-    lax.fori_loop(0, GROUPS, forward, 0)
-    energy_out[...] = jnp.zeros_like(energy_out)
-    energy_out[0:1] = jnp.sum(energies[...].T, axis=0, keepdims=True)
-
-
-def backward_kernel(table, edge, back, weight, energy, near_out, send_up, values, near):
-    near[...] = jnp.zeros_like(near)
-
+    return forward
+
+
+def fill(table, row, m, tiles):
+    rows = jnp.concatenate([tile.astype(F32) for tile in tiles], axis=0)
+    table[32 * row : 32 * row + 32, C * m : C * m + C] = rows.astype(BF16)
+
+
+def early_kernel(own, right, weight, mix, out_weight, energies, table, edge, back, geometry, message):
+    for m in range(10):
+        for y in range(8):
+            fill(table, y, m, [own[1, y, m], right[0, y, m], own[0, y, m], right[1, y, m]])
+    step = group_forward(table, weight, mix, out_weight, edge, back, energies, geometry, message)
+    lax.fori_loop(0, GROUPS - 1, step, 0)
+
+
+def late_kernel(
+    known, up, early, weight, mix, out_weight,
+    energy_out, spread_out, table, edge, back,
+    energies, geometry, message,
+):
+    table[0:64] = known[192:256]
+    for m in range(10):
+        for y in range(2):
+            fill(table, 2 + y, m, [up[i, y, m] for i in (1, 2, 0, 3)])
+    group_forward(table, weight, mix, out_weight, edge, back, energies, geometry, message)(0, 0)
+    total = jnp.concatenate([early[...], energies[...]], axis=0)
+    total = jnp.sum(total.T, axis=0, keepdims=True)
+    energy_out[...] = jnp.broadcast_to(total, energy_out.shape)
+    spread_out[...] = jnp.broadcast_to(total[None], spread_out.shape)
+
+
+def relay_kernel(gathered, out):
+    total = jnp.sum(gathered[...], axis=0, keepdims=True)
+    out[...] = jnp.broadcast_to(total, out.shape)
+
+
+def group_backward(table, edge, back, weight, values, near, ahead):
     def backward(q, carry):
         block = block_of(q)
         first = table[block, 0:C]
-        spot = pl.ds(pl.multiple_of(q * ROWS, ROWS), ROWS)
+        spot = pl.ds(pl.multiple_of((q + ahead) * ROWS, ROWS), ROWS)
 
         def spread(g, path):
             return jnp.concatenate(
@@ -260,10 +292,19 @@
         for axis, (v, unit) in enumerate(((vx, ux), (vy, uy), (vz, uz))):
             gradient = inward * unit + inv * v
             values[axis, spot] = gradient
-            near[axis, pl.ds(q, 1)] = jnp.sum(gradient, axis=0, keepdims=True)
+            near[axis, pl.ds(q + ahead, 1)] = jnp.sum(gradient, axis=0, keepdims=True)
         return carry
 
-    lax.fori_loop(0, GROUPS, backward, 0)
+    return backward
+
+
+def backward_kernel(
+    table, edge, back, late_table, late_edge, late_back, weight, energy,
+    near_out, send_up, values, near,
+):
+    near[...] = jnp.zeros_like(near)
+    lax.fori_loop(0, GROUPS - 1, group_backward(table, edge, back, weight, values, near, 0), 0)
+    group_backward(late_table, late_edge, late_back, weight, values, near, GROUPS - 1)(0, 0)
     send_up[...] = jnp.zeros_like(send_up)
     near_out[...] = jnp.zeros_like(near_out)
     lane = lax.broadcasted_iota(jnp.int32, (8, C), 1)
@@ -293,40 +334,74 @@
     return pl.pallas_call(
         pack_kernel,
         out_shape=jax.ShapeDtypeStruct((2, 8, 10, 8, C), BF16),
-        in_specs=[VMEM] * 4,
+        in_specs=[pl.BlockSpec(memory_space=pl.ANY)] * 4,
         out_specs=VMEM,
-        compiler_params=pltpu.CompilerParams(vmem_limit_bytes=8 * 1024 * 1024),
+        scratch_shapes=[
+            pltpu.VMEM(positions.shape, F32),
+            pltpu.VMEM(occupied.shape, jnp.int32),
+            pltpu.VMEM(neighbours.shape, jnp.int32),
+            pltpu.SemaphoreType.DMA((4,)),
+        ],
         name="pack",
     )(features, positions, occupied, neighbours)
 
 
-def forward_call(*arrays):
+def results(groups, rows):
+    return (
+        jax.ShapeDtypeStruct((rows, 10 * C), BF16),
+        jax.ShapeDtypeStruct((groups, 25, ROWS, C), F32),
+        jax.ShapeDtypeStruct((groups, 9, ROWS, C), F32),
+    )
+
+
+SCRATCH = [pltpu.VMEM((9, NB * ROWS, C), BF16), pltpu.VMEM((9, ROWS, C), BF16)]
+
+
+def early_call(*arrays):
     return pl.pallas_call(
-        forward_kernel,
+        early_kernel,
+        out_shape=(jax.ShapeDtypeStruct((3 * ROWS, C), F32),) + results(3, 256),
+        in_specs=[VMEM] * 5,
+        out_specs=(VMEM,) * 4,
+        scratch_shapes=SCRATCH,
+        compiler_params=pltpu.CompilerParams(vmem_limit_bytes=20 * 1024 * 1024),
+        cost_estimate=pl.CostEstimate(flops=4_000_000_000, bytes_accessed=8_000_000, transcendentals=0),
+        name="early",
+    )(*arrays)
+
+
+def late_call(plane, *arrays):
+    return pl.pallas_call(
+        late_kernel,
         out_shape=(
             jax.ShapeDtypeStruct((8, C), F32),
-            jax.ShapeDtypeStruct((C, C), F32),
-            jax.ShapeDtypeStruct((320, 10 * C), BF16),
-            jax.ShapeDtypeStruct((GROUPS, 25, ROWS, C), F32),
-            jax.ShapeDtypeStruct((GROUPS, 9, ROWS, C), F32),
-        ),
+            jax.ShapeDtypeStruct((plane, 1, C), F32),
+        ) + results(1, 128),
         in_specs=[VMEM] * 6,
         out_specs=(VMEM,) * 5,
-        scratch_shapes=[
-            pltpu.VMEM((9, NB * ROWS, C), BF16),
-            pltpu.VMEM((9, ROWS, C), BF16),
-        ],
+        scratch_shapes=[pltpu.VMEM((ROWS, C), F32)] + SCRATCH,
         compiler_params=pltpu.CompilerParams(vmem_limit_bytes=20 * 1024 * 1024),
-        cost_estimate=pl.CostEstimate(flops=4_000_000_000, bytes_accessed=8_000_000, transcendentals=0),
-        name="forward",
+        cost_estimate=pl.CostEstimate(flops=1_000_000_000, bytes_accessed=2_000_000, transcendentals=0),
+        name="late",
     )(*arrays)
+
+
+def relay_call(gathered, depth):
+    return pl.pallas_call(
+        relay_kernel,
+        out_shape=jax.ShapeDtypeStruct((depth, 1, C), F32),
+        in_specs=[VMEM],
+        out_specs=VMEM,
+        compiler_params=pltpu.CompilerParams(vmem_limit_bytes=4 * 1024 * 1024),
+        name="relay",
+    )(gathered)
 
 
 def backward_call(*arrays):
     return pl.pallas_call(
         backward_kernel,
         out_shape=(jax.ShapeDtypeStruct((4, 8, C), F32), jax.ShapeDtypeStruct((8, C), F32)),
-        in_specs=[VMEM] * 5,
+        in_specs=[VMEM] * 8,
         out_specs=(VMEM,) * 2,
         scratch_shapes=[pltpu.VMEM((3, C, C), F32), pltpu.VMEM((3, 8, C), F32)],
         compiler_params=pltpu.CompilerParams(vmem_limit_bytes=20 * 1024 * 1024),
@@ -346,17 +421,14 @@
     own = pack_call(jnp.transpose(features, (0, 1, 3, 2, 4)), positions, occupied, neighbours)
     right = lax.ppermute(own, "gx", ring(size_x, -1))
     up = lax.ppermute(jnp.concatenate([own[:, :2], right[:, :2]], axis=0), gy, ring(size_y, -1))
-    energy, _, table, edge, back = forward_call(
-        own, right, up, radial_weight, mix_weight, out_weight[None]
-    )
+    shared = (radial_weight, mix_weight, out_weight[None])
+    early, *first = early_call(own, right, *shared)
     plane = size_x * lax.axis_size(outer)
-    gathered = lax.all_to_all(
-        jnp.broadcast_to(energy[None, :1], (plane, 1, C)), ("gx",) + outer, 0, 0
-    )
-    near, send_up = backward_call(table, edge, back, radial_weight, energy)
-    energy_plane = jnp.sum(gathered, axis=0)
-    depth = lax.axis_size(inner)
-    gathered = lax.all_to_all(jnp.broadcast_to(energy_plane[None], (depth, 1, C)), inner, 0, 0)
+    energy, spread, *last = late_call(plane, first[0], up, early, *shared)
+    gathered = lax.all_to_all(spread, ("gx",) + outer, 0, 0)
+    near, send_up = backward_call(*first, *last, radial_weight, energy)
+    gathered, near = lax.optimization_barrier((gathered, near))
+    gathered = lax.all_to_all(relay_call(gathered, lax.axis_size(inner)), inner, 0, 0)
     from_down = lax.ppermute(send_up, gy, ring(size_y, 1))
     near = near.at[:, 0].add(from_down[:4])[:, :4]
     from_left = lax.ppermute(near, "gx", ring(size_x, 1))

time: 91.3 us -> 79.7 us (0.87)
  starting transfers between devices: 54.7 us -> 47.6 us
  local copies, waits for them, and re-layouts: 6.93 us -> 2.18 us
  waiting for transfers between devices: 17.3 us -> 14.8 us
  Pallas kernels: 9.02 us -> 11.2 us
    all_to_all x2, starting transfers between devices: 18.2 us -> 11.8 us  [the longest x1 8.35 us: on_device(): gathered = lax.all_to_all(spread, ('gx',) + outer, 0, 0)]
    unnamed x16 -> x8, local copies, waits for them, and re-layouts: 5.39 us -> 0.98 us
    ppermute x1, waiting for transfers between devices: 0.01 us -> 4.4 us  [on_device(): from_down = lax.ppermute(send_up, gy, ring(size_y, 1))]
    all_to_all x2, waiting for transfers between devices: 12.4 us -> 9.21 us  [the longest x1 4.84 us: on_device(): lax.all_to_all(relay_call(gathered, lax.axis_size(inner)), inner, 0, 0)]
    ppermute x1, waiting for transfers between devices: 2.24 us -> 0.01 us  [on_device(): lax.ppermute(jnp.concatenate([own[:, :2], right[:, :2]], axis=0), gy, rin...]
    pallas_call x1, Pallas kernels: 0.24 us -> 1.89 us  [pack_call(): pl.pallas_call(pack_kernel, out_shape=jax.ShapeDtypeStruct((2, 8, 10, 8,...]
    broadcast_in_dim x3 -> x0, local copies, waits for them, and re-layouts: 1.22 us -> none  [the longest x2 0.62 us: on_device(): jnp.broadcast_to(energy[None, :1], (plane, 1, C))]
    pallas_call x1 -> x3, Pallas kernels: 5.82 us -> 6.5 us  [the longest x1 4.01 us: early_call(): pl.pallas_call(early_kernel, out_shape=(jax.ShapeDtypeStruct((3 * ROWS, C...]
  transfers between devices with their start and end apart: 6 -> 6, of which waited for: 5 -> 5; matrix products, arithmetic and copies ran while one was open for 2% -> 3% of each run, Pallas kernels for 0% -> 9%
where the time goes in v3:
time: 79.7 us; the launch traced here: 78.5 us
  starting transfers between devices  47.6 us (60%)
  waiting for transfers between devices  14.8 us (19%)
  Pallas kernels  11.2 us (14%)
  local copies, waits for them, and re-layouts  2.18 us (3%)
  other arithmetic  1.86 us (2%)
  between operations  0.82 us (1%)
    ppermute x1, starting transfers between devices, on_device(): right = lax.ppermute(own, 'gx', ring(size_x, -1))  16.1 us
    ppermute x1, starting transfers between devices, on_device(): lax.ppermute(jnp.concatenate([own[:, :2], right[:, :2]], axis=0), gy, rin...  13.6 us
    all_to_all x1, starting transfers between devices, on_device(): gathered = lax.all_to_all(spread, ('gx',) + outer, 0, 0)  8.35 us
    all_to_all x1, waiting for transfers between devices, on_device(): lax.all_to_all(relay_call(gathered, lax.axis_size(inner)), inner, 0, 0)  4.84 us
    ppermute x1, waiting for transfers between devices, on_device(): from_down = lax.ppermute(send_up, gy, ring(size_y, 1))  4.4 us
    all_to_all x1, waiting for transfers between devices, on_device(): gathered = lax.all_to_all(spread, ('gx',) + outer, 0, 0)  4.37 us
    ppermute x1, starting transfers between devices, on_device(): from_left = lax.ppermute(near, 'gx', ring(size_x, 1))  4.23 us
    pallas_call x1, Pallas kernels, early_call(): pl.pallas_call(early_kernel, out_shape=(jax.ShapeDtypeStruct((3 * ROWS, C...  4.01 us
  transfers between devices with their start and end apart: 6, of which 5 were waited for; matrix products, arithmetic and copies ran while one was open for 3% of the time, Pallas kernels for 9%

profile of v3, /device:TPU:1, one launch (start us, length us, event | category | flops | bytes accessed | tf_op | source)
XLA Modules:
  0.0 78.5 jit_solution(14141131630512619386)
XLA Ops:
  0.6 0.0 copy-start.2
  0.6 0.0 copy-start.1
  0.7 0.0 copy-start.3
  0.7 1.9 %pack.1.own = bf16[2,8,10,8,128]{4,3,2,1,0:T(8,128)(2,1)} custom-call(bf16[2,8,9,8,128]{4,3,2,1,0:T(8,128)(2,1)} %bitcast.18, f32[3,2,8,8]{3,2,1,0:T(8,128)} %places.1, s32[2,8,8]{2,1,0:T(8,128)} %present.1, s32[2,8,8,32]{3,2,1,0:T(8,128)} %lists.1), custom_call_target="tpu_custom_call" | custom-call | tf_op jit(solution)/shard_map/pack/pallas_call | solution.py:334
  2.6 16.1 %collective-permute-start = (bf16[2,8,10,8,128]{4,3,2,1,0:T(8,128)(2,1)}, bf16[2,8,10,8,128]{4,3,2,1,0:T(8,128)(2,1)S(1)}, u32[]{:S(2)}, u32[]{:S(2)}) collective-permute-start(bf16[2,8,10,8,128]{4,3,2,1,0:T(8,128)(2,1)} %pack.1.own), channel_id=1, source_target_pairs={{0,960},{64,0},{128,64},{192,128},{256,192},{320,256},{384,320},{4... | collective-permute-start | bytes 983048 | tf_op jit(solution)/shard_map/ppermute | solution.py:422
  18.6 0.9 %slice.74 = bf16[2,2,10,8,128]{4,3,2,1,0:T(8,128)(2,1)S(1)} slice(bf16[2,8,10,8,128]{4,3,2,1,0:T(8,128)(2,1)} %pack.1.own), slice={[0:2], [0:2], [0:10], [0:8], [0:128]} | slice | bytes 163840 | tf_op jit(solution)/shard_map/slice | solution.py:423
  19.5 0.5 collective-permute-done.right
  20.1 13.6 %collective-permute-start.1 = (bf16[4,2,10,8,128]{4,3,2,1,0:T(8,128)(2,1)S(1)}, bf16[4,2,10,8,128]{4,3,2,1,0:T(8,128)(2,1)S(1)}, u32[]{:S(2)}, u32[]{:S(2)}) collective-permute-start(bf16[4,2,10,8,128]{4,3,2,1,0:T(8,128)(2,1)S(1)} %pad_maximum_fusion), channel_id=1, source_target_pairs={{0,63},{1,0},{2,1},{3,2},{4,3},{5,4},{6,5},{7,6},{8,7},{9,8},{10,9... | collective-permute-start | bytes 491528 | tf_op jit(solution)/shard_map/ppermute | solution.py:423
  33.7 0.0 copy-done.2
  33.7 0.0 copy-done.1
  33.7 0.0 copy-done.3
  33.7 0.0 copy-start
  33.7 1.0 %copy-done = bf16[2,8,10,8,128]{4,3,2,1,0:T(8,128)(2,1)S(1)} copy-done((bf16[2,8,10,8,128]{4,3,2,1,0:T(8,128)(2,1)S(1)}, bf16[2,8,10,8,128]{4,3,2,1,0:T(8,128)(2,1)}, u32[]{:S(2)}) %copy-start) | copy-done | bytes 327704
  34.7 4.0 %early.1 = (f32[96,128]{1,0:T(8,128)S(1)}, bf16[256,1280]{1,0:T(8,128)(2,1)S(1)}, f32[3,25,32,128]{3,2,1,0:T(8,128)S(1)}, f32[3,9,32,128]{3,2,1,0:T(8,128)S(1)}) custom-call(bf16[2,8,10,8,128]{4,3,2,1,0:T(8,128)(2,1)S(1)} %copy-done, bf16[2,8,10,8,128]{4,3,2,1,0:T(8,128)(2,1)S(1)} %collective-permute-done.right, f32[7,8,128]{2,1,0:T(8,128)S(1)} %copy-done.2, ...), custom_call_target="tpu_custom_call" | custom-call | flops 4000000000 | bytes 8000000 | tf_op jit(solution)/shard_map/early/pallas_call | solution.py:361
  38.7 0.0 collective-permute-done.1.up
  38.7 1.8 %late.1 = (f32[8,128]{1,0:T(8,128)S(1)}, f32[64,1,128]{2,1,0:T(1,128)}, bf16[128,1280]{1,0:T(8,128)(2,1)S(1)}, f32[1,25,32,128]{3,2,1,0:T(8,128)S(1)}, f32[1,9,32,128]{3,2,1,0:T(8,128)S(1)}) custom-call(bf16[256,1280]{1,0:T(8,128)(2,1)S(1)} %get-tuple-element.28.known.table, bf16[4,2,10,8,128]{4,3,2,1,0:T(8,128)(2,1)S(1)} %collective-permute-done.1.up, ...), custom_call_target="tpu_custom_call" | custom-call | flops 1000000000 | bytes 2000000 | tf_op jit(solution)/shard_map/late/pallas_call | solution.py:374
  40.6 8.3 %all-to-all-start = ((f32[64,1,128]{2,1,0:T(1,128)}), f32[64,1,128]{2,1,0:T(1,128)S(1)}, u32[]{:S(2)}, u32[]{:S(2)}) async-start(f32[64,1,128]{2,1,0:T(1,128)} %get-tuple-element.30), calls=%async_computation | async-start | bytes 65536 | tf_op jit(solution)/shard_map/all_to_all | solution.py:428
  48.9 2.8 %backward.1 = (f32[4,8,128]{2,1,0:T(8,128)S(1)}, f32[8,128]{1,0:T(8,128)S(1)}) custom-call(bf16[256,1280]{1,0:T(8,128)(2,1)S(1)} %get-tuple-element.28.known.table, f32[3,25,32,128]{3,2,1,0:T(8,128)S(1)} %get-tuple-element.31.edge, f32[3,9,32,128]{3,2,1,0:T(8,128)S(1)} %get-tuple-element.32.back, bf16[128,1280]{1,0:T(8,128)(2,1)S(1)} %get-tuple-element.33.late_table, ...), custom_call_target="tpu_custom_call" | custom-call | flops 4000000000 | bytes 8000000 | tf_op jit(solution)/shard_map/backward/pallas_call | solution.py:401
  51.7 1.9 %collective-permute-start.2 = (f32[8,128]{1,0:T(8,128)S(1)}, f32[8,128]{1,0:T(8,128)S(1)}, u32[]{:S(2)}, u32[]{:S(2)}) collective-permute-start(f32[8,128]{1,0:T(8,128)S(1)} %get-tuple-element.39), channel_id=1, source_target_pairs={{0,1},{1,2},{2,3},{3,4},{4,5},{5,6},{6,7},{7,8},{8,9},{9,10},{10,1... | collective-permute-start | bytes 12296 | tf_op jit(solution)/shard_map/ppermute | solution.py:432
  53.7 4.4 %all-to-all-done.gathered = f32[64,1,128]{2,1,0:T(1,128)S(1)} async-done(((f32[64,1,128]{2,1,0:T(1,128)}), f32[64,1,128]{2,1,0:T(1,128)S(1)}, u32[]{:S(2)}, u32[]{:S(2)}) %all-to-all-start) | async-done | bytes 32800 | tf_op jit(solution)/shard_map/all_to_all | solution.py:428
  58.0 4.4 %collective-permute-done.2 = f32[8,128]{1,0:T(8,128)S(1)} collective-permute-done((f32[8,128]{1,0:T(8,128)S(1)}, f32[8,128]{1,0:T(8,128)S(1)}, u32[]{:S(2)}, u32[]{:S(2)}) %collective-permute-start.2) | collective-permute-done | bytes 4128 | tf_op jit(solution)/shard_map/ppermute | solution.py:432
  62.5 0.7 relay.1
  63.2 3.5 %all-to-all-start.1 = ((f32[16,1,128]{2,1,0:T(1,128)}), f32[16,1,128]{2,1,0:T(1,128)S(1)}, u32[]{:S(2)}, u32[]{:S(2)}) async-start(f32[16,1,128]{2,1,0:T(1,128)} %relay.1), calls=%async_computation.1 | async-start | bytes 16384 | tf_op jit(solution)/shard_map/all_to_all | solution.py:431
  66.6 4.2 %collective-permute-start.3 = (f32[4,4,128]{2,1,0:T(4,128)S(1)}, f32[4,4,128]{2,1,0:T(4,128)S(1)}, u32[]{:S(2)}, u32[]{:S(2)}) collective-permute-start(f32[4,4,128]{2,1,0:T(4,128)S(1)} %slice.79), channel_id=1, source_target_pairs={{0,64},{64,128},{128,192},{192,256},{256,320},{320,384},{384,448},... | collective-permute-start | bytes 24584 | tf_op jit(solution)/shard_map/ppermute | solution.py:434
  70.9 0.1 reshape.84
  71.0 0.6 collective-permute-done.3
  71.6 0.1 reshape.85
  71.8 0.6 fusion
  72.4 0.6 fusion.1
  73.0 4.8 %all-to-all-done.1 = f32[16,1,128]{2,1,0:T(1,128)S(1)} async-done(((f32[16,1,128]{2,1,0:T(1,128)}), f32[16,1,128]{2,1,0:T(1,128)S(1)}, u32[]{:S(2)}, u32[]{:S(2)}) %all-to-all-start.1) | async-done | bytes 8224 | tf_op jit(solution)/shard_map/all_to_all | solution.py:431
  77.9 0.6 reduce_sum.9
  (10 shorter events, 0.1 us)
Async XLA Ops:
  0.6 33.1 %copy-start.2 = (f32[7,8,128]{2,1,0:T(8,128)S(1)}, f32[7,8,128]{2,1,0:T(8,128)}, u32[]{:S(2)}) copy-start(f32[7,8,128]{2,1,0:T(8,128)} %weight.5) | copy-start | bytes 86020
  0.6 33.1 %copy-start.1 = (bf16[128,128]{1,0:T(8,128)(2,1)S(1)}, bf16[128,128]{1,0:T(8,128)(2,1)}, u32[]{:S(2)}) copy-start(bf16[128,128]{1,0:T(8,128)(2,1)} %mix.3) | copy-start | bytes 98308
  0.7 33.1 %copy-start.3 = (f32[128]{0:T(128)S(1)}, f32[128]{0:T(128)}, u32[]{:S(2)}) copy-start(f32[128]{0:T(128)} %param.15) | copy-start | bytes 1540
  2.6 17.5 %collective-permute-start = (bf16[2,8,10,8,128]{4,3,2,1,0:T(8,128)(2,1)}, bf16[2,8,10,8,128]{4,3,2,1,0:T(8,128)(2,1)S(1)}, u32[]{:S(2)}, u32[]{:S(2)}) collective-permute-start(bf16[2,8,10,8,128]{4,3,2,1,0:T(8,128)(2,1)} %pack.1.own), channel_id=1, source_target_pairs={{0,960},{64,0},{128,64},{192,128},{256,192},{320,256},{384,320},{4... | collective-permute-start | bytes 983048 | tf_op jit(solution)/shard_map/ppermute | solution.py:422
  20.1 18.6 %collective-permute-start.1 = (bf16[4,2,10,8,128]{4,3,2,1,0:T(8,128)(2,1)S(1)}, bf16[4,2,10,8,128]{4,3,2,1,0:T(8,128)(2,1)S(1)}, u32[]{:S(2)}, u32[]{:S(2)}) collective-permute-start(bf16[4,2,10,8,128]{4,3,2,1,0:T(8,128)(2,1)S(1)} %pad_maximum_fusion), channel_id=1, source_target_pairs={{0,63},{1,0},{2,1},{3,2},{4,3},{5,4},{6,5},{7,6},{8,7},{9,8},{10,9... | collective-permute-start | bytes 491528 | tf_op jit(solution)/shard_map/ppermute | solution.py:423
  33.7 1.0 %copy-start = (bf16[2,8,10,8,128]{4,3,2,1,0:T(8,128)(2,1)S(1)}, bf16[2,8,10,8,128]{4,3,2,1,0:T(8,128)(2,1)}, u32[]{:S(2)}) copy-start(bf16[2,8,10,8,128]{4,3,2,1,0:T(8,128)(2,1)} %pack.1.own) | copy-start | bytes 983044
  40.6 17.5 %all-to-all-start = ((f32[64,1,128]{2,1,0:T(1,128)}), f32[64,1,128]{2,1,0:T(1,128)S(1)}, u32[]{:S(2)}, u32[]{:S(2)}) async-start(f32[64,1,128]{2,1,0:T(1,128)} %get-tuple-element.30), calls=%async_computation | async-start | bytes 65536 | tf_op jit(solution)/shard_map/all_to_all | solution.py:428
  51.7 10.7 %collective-permute-start.2 = (f32[8,128]{1,0:T(8,128)S(1)}, f32[8,128]{1,0:T(8,128)S(1)}, u32[]{:S(2)}, u32[]{:S(2)}) collective-permute-start(f32[8,128]{1,0:T(8,128)S(1)} %get-tuple-element.39), channel_id=1, source_target_pairs={{0,1},{1,2},{2,3},{3,4},{4,5},{5,6},{6,7},{7,8},{8,9},{9,10},{10,1... | collective-permute-start | bytes 12296 | tf_op jit(solution)/shard_map/ppermute | solution.py:432
  63.2 14.7 %all-to-all-start.1 = ((f32[16,1,128]{2,1,0:T(1,128)}), f32[16,1,128]{2,1,0:T(1,128)S(1)}, u32[]{:S(2)}, u32[]{:S(2)}) async-start(f32[16,1,128]{2,1,0:T(1,128)} %relay.1), calls=%async_computation.1 | async-start | bytes 16384 | tf_op jit(solution)/shard_map/all_to_all | solution.py:431
  66.6 5.0 %collective-permute-start.3 = (f32[4,4,128]{2,1,0:T(4,128)S(1)}, f32[4,4,128]{2,1,0:T(4,128)S(1)}, u32[]{:S(2)}, u32[]{:S(2)}) collective-permute-start(f32[4,4,128]{2,1,0:T(4,128)S(1)} %slice.79), channel_id=1, source_target_pairs={{0,64},{64,128},{128,192},{192,256},{256,320},{320,384},{384,448},... | collective-permute-start | bytes 24584 | tf_op jit(solution)/shard_map/ppermute | solution.py:434

commit v4 on v3

--- a/solution.py
+++ b/solution.py
@@ -22,7 +22,7 @@
 NT = (((1,), (1,)), ((), ()))
 
 
-def pack_kernel(features, places, present, lists, out, positions, occupied, neighbours, done):
+def pack_kernel(features, places, present, lists, out, low_out, positions, occupied, neighbours, done):
     moves = [
         pltpu.make_async_copy(source, target, done.at[i])
         for i, (source, target) in enumerate(
@@ -61,6 +61,7 @@
             tile = jnp.where(kind == 0, pltpu.roll(high, back, 1), tile)
             out[x, y, 9] = tile.astype(BF16)
     moves[3].wait()
+    low_out[...] = out[:, 0:2]
 
 
 def count(codes):
@@ -229,19 +230,26 @@
 
 
 def late_kernel(
-    known, up, early, weight, mix, out_weight,
+    known, up, across, early, weight, mix, out_weight,
     energy_out, spread_out, table, edge, back,
     energies, geometry, message,
 ):
     table[0:64] = known[192:256]
     for m in range(10):
         for y in range(2):
-            fill(table, 2 + y, m, [up[i, y, m] for i in (1, 2, 0, 3)])
+            fill(table, 2 + y, m, [up[1, y, m], across[0, y, m], up[0, y, m], across[1, y, m]])
     group_forward(table, weight, mix, out_weight, edge, back, energies, geometry, message)(0, 0)
     total = jnp.concatenate([early[...], energies[...]], axis=0)
     total = jnp.sum(total.T, axis=0, keepdims=True)
     energy_out[...] = jnp.broadcast_to(total, energy_out.shape)
     spread_out[...] = jnp.broadcast_to(total[None], spread_out.shape)
+
+
+def stage_kernel(own, weight, mix, out_weight, own_copy, weight_copy, mix_copy, out_weight_copy):
+    own_copy[...] = own[...]
+    weight_copy[...] = weight[...]
+    mix_copy[...] = mix[...]
+    out_weight_copy[...] = out_weight[...]
 
 
 def relay_kernel(gathered, out):
@@ -333,9 +341,12 @@
 def pack_call(features, positions, occupied, neighbours):
     return pl.pallas_call(
         pack_kernel,
-        out_shape=jax.ShapeDtypeStruct((2, 8, 10, 8, C), BF16),
+        out_shape=(
+            jax.ShapeDtypeStruct((2, 8, 10, 8, C), BF16),
+            jax.ShapeDtypeStruct((2, 2, 10, 8, C), BF16),
+        ),
         in_specs=[pl.BlockSpec(memory_space=pl.ANY)] * 4,
-        out_specs=VMEM,
+        out_specs=(VMEM, VMEM),
         scratch_shapes=[
             pltpu.VMEM(positions.shape, F32),
             pltpu.VMEM(occupied.shape, jnp.int32),
@@ -344,6 +355,18 @@
         ],
         name="pack",
     )(features, positions, occupied, neighbours)
+
+
+def stage_call(*arrays):
+    return pl.pallas_call(
+        stage_kernel,
+        out_shape=tuple(jax.ShapeDtypeStruct(a.shape, a.dtype) for a in arrays),
+        in_specs=[VMEM] * 4,
+        out_specs=(VMEM,) * 4,
+        compiler_params=pltpu.CompilerParams(vmem_limit_bytes=8 * 1024 * 1024),
+        cost_estimate=pl.CostEstimate(flops=2_000_000, bytes_accessed=2_000_000, transcendentals=0),
+        name="stage",
+    )(*arrays)
 
 
 def results(groups, rows):
@@ -377,7 +400,7 @@
             jax.ShapeDtypeStruct((8, C), F32),
             jax.ShapeDtypeStruct((plane, 1, C), F32),
         ) + results(1, 128),
-        in_specs=[VMEM] * 6,
+        in_specs=[VMEM] * 7,
         out_specs=(VMEM,) * 5,
         scratch_shapes=[pltpu.VMEM((ROWS, C), F32)] + SCRATCH,
         compiler_params=pltpu.CompilerParams(vmem_limit_bytes=20 * 1024 * 1024),
@@ -418,17 +441,23 @@
     gy = outer + inner
     size_x = lax.axis_size("gx")
     size_y = lax.axis_size(gy)
-    own = pack_call(jnp.transpose(features, (0, 1, 3, 2, 4)), positions, occupied, neighbours)
+    own, low = pack_call(jnp.transpose(features, (0, 1, 3, 2, 4)), positions, occupied, neighbours)
     right = lax.ppermute(own, "gx", ring(size_x, -1))
-    up = lax.ppermute(jnp.concatenate([own[:, :2], right[:, :2]], axis=0), gy, ring(size_y, -1))
-    shared = (radial_weight, mix_weight, out_weight[None])
+    up = lax.ppermute(low, gy, ring(size_y, -1))
+    corner = [
+        (x * size_y + y, (x - 1) % size_x * size_y + (y - 1) % size_y)
+        for x in range(size_x)
+        for y in range(size_y)
+    ]
+    across = lax.ppermute(low, ("gx",) + gy, corner)
+    own, *shared = stage_call(own, radial_weight, mix_weight, out_weight[None])
     early, *first = early_call(own, right, *shared)
     plane = size_x * lax.axis_size(outer)
-    energy, spread, *last = late_call(plane, first[0], up, early, *shared)
+    energy, spread, *last = late_call(plane, first[0], up, across, early, *shared)
     gathered = lax.all_to_all(spread, ("gx",) + outer, 0, 0)
-    near, send_up = backward_call(*first, *last, radial_weight, energy)
-    gathered, near = lax.optimization_barrier((gathered, near))
-    gathered = lax.all_to_all(relay_call(gathered, lax.axis_size(inner)), inner, 0, 0)
+    near, send_up = backward_call(*first, *last, shared[0], energy)
+    spread, send_up = lax.optimization_barrier((relay_call(gathered, lax.axis_size(inner)), send_up))
+    gathered = lax.all_to_all(spread, inner, 0, 0)
     from_down = lax.ppermute(send_up, gy, ring(size_y, 1))
     near = near.at[:, 0].add(from_down[:4])[:, :4]
     from_left = lax.ppermute(near, "gx", ring(size_x, 1))

time: 79.7 us -> 75.5 us (0.947)
  waiting for transfers between devices: 14.8 us -> 12.1 us
  starting transfers between devices: 47.6 us -> 45.5 us
  local copies, waits for them, and re-layouts: 2.18 us -> 3.43 us
    all_to_all x1, starting transfers between devices: 8.35 us -> 5.42 us  [on_device(): gathered = lax.all_to_all(spread, ('gx',) + outer, 0, 0)]
    ppermute x1, waiting for transfers between devices: 4.4 us -> 1.78 us  [on_device(): from_down = lax.ppermute(send_up, gy, ring(size_y, 1))]
    unnamed x8, local copies, waits for them, and re-layouts: 0.98 us -> 3.13 us
    all_to_all x1, waiting for transfers between devices: 4.37 us -> 6.27 us  [on_device(): gathered = lax.all_to_all(spread, ('gx',) + outer, 0, 0)]
    all_to_all x1, waiting for transfers between devices: 4.84 us -> 3.39 us  [on_device(): gathered = lax.all_to_all(spread, inner, 0, 0)]
    slice x2 -> x0, local copies, waits for them, and re-layouts: 0.9 us -> none  [the longest x1 0.9 us: on_device(): own[:, :2]]
    ppermute x1 -> x2, starting transfers between devices: 13.6 us -> 13.4 us  [the longest x1 11.2 us: on_device(): across = lax.ppermute(low, ('gx',) + gy, corner)]
    pallas_call x1 -> x2, Pallas kernels: 1.89 us -> 1.93 us  [the longest x1 1.9 us: pack_call(): pl.pallas_call(pack_kernel, out_shape=(jax.ShapeDtypeStruct((2, 8, 10, 8,...]
  transfers between devices with their start and end apart: 6 -> 7, of which waited for: 5 -> 4; matrix products, arithmetic and copies ran while one was open for 3% -> 2% of each run, Pallas kernels for 9% -> 9%
where the time goes in v4:
time: 75.5 us; the launch traced here: 75 us
  starting transfers between devices  45.5 us (60%)
  waiting for transfers between devices  12.1 us (16%)
  Pallas kernels  11.3 us (15%)
  local copies, waits for them, and re-layouts  3.43 us (5%)
  other arithmetic  1.84 us (2%)
  between operations  0.81 us (1%)
    ppermute x1, starting transfers between devices, on_device(): right = lax.ppermute(own, 'gx', ring(size_x, -1))  16.1 us
    ppermute x1, starting transfers between devices, on_device(): across = lax.ppermute(low, ('gx',) + gy, corner)  11.2 us
    all_to_all x1, waiting for transfers between devices, on_device(): gathered = lax.all_to_all(spread, ('gx',) + outer, 0, 0)  6.27 us
    all_to_all x1, starting transfers between devices, on_device(): gathered = lax.all_to_all(spread, ('gx',) + outer, 0, 0)  5.42 us
    all_to_all x1, starting transfers between devices, on_device(): gathered = lax.all_to_all(spread, inner, 0, 0)  4.18 us
    pallas_call x1, Pallas kernels, early_call(): pl.pallas_call(early_kernel, out_shape=(jax.ShapeDtypeStruct((3 * ROWS, C...  4.02 us
    ppermute x1, starting transfers between devices, on_device(): from_left = lax.ppermute(near, 'gx', ring(size_x, 1))  3.93 us
    all_to_all x1, waiting for transfers between devices, on_device(): gathered = lax.all_to_all(spread, inner, 0, 0)  3.39 us
  transfers between devices with their start and end apart: 7, of which 4 were waited for; matrix products, arithmetic and copies ran while one was open for 2% of the time, Pallas kernels for 9%

profile of v4, /device:TPU:1, one launch (start us, length us, event | category | flops | bytes accessed | tf_op | source)
XLA Modules:
  0.0 75.0 jit_solution(15846378359902033910)
XLA Ops:
  0.6 1.9 %pack.1 = (bf16[2,8,10,8,128]{4,3,2,1,0:T(8,128)(2,1)}, bf16[2,2,10,8,128]{4,3,2,1,0:T(8,128)(2,1)}) custom-call(bf16[2,8,9,8,128]{4,3,2,1,0:T(8,128)(2,1)} %bitcast.17, f32[3,2,8,8]{3,2,1,0:T(8,128)} %places.1, s32[2,8,8]{2,1,0:T(8,128)} %present.1, s32[2,8,8,32]{3,2,1,0:T(8,128)} %lists.1), custom_call_target="tpu_custom_call" | custom-call | tf_op jit(solution)/shard_map/pack/pallas_call | solution.py:342
  2.5 16.1 %collective-permute-start = (bf16[2,8,10,8,128]{4,3,2,1,0:T(8,128)(2,1)}, bf16[2,8,10,8,128]{4,3,2,1,0:T(8,128)(2,1)S(1)}, u32[]{:S(2)}, u32[]{:S(2)}) collective-permute-start(bf16[2,8,10,8,128]{4,3,2,1,0:T(8,128)(2,1)} %get-tuple-element.34.own), channel_id=1, source_target_pairs={{0,960},{64,0},{128,64},{192,128},{256,192},{320,256},{384,320},{4... | collective-permute-start | bytes 983048 | tf_op jit(solution)/shard_map/ppermute | solution.py:445
  18.6 11.2 %collective-permute-start.2 = (bf16[2,2,10,8,128]{4,3,2,1,0:T(8,128)(2,1)}, bf16[2,2,10,8,128]{4,3,2,1,0:T(8,128)(2,1)S(1)}, u32[]{:S(2)}, u32[]{:S(2)}) collective-permute-start(bf16[2,2,10,8,128]{4,3,2,1,0:T(8,128)(2,1)} %get-tuple-element.42), channel_id=1, source_target_pairs={{0,1023},{1,960},{2,961},{3,962},{4,963},{5,964},{6,965},{7,966},{... | collective-permute-start | bytes 245768 | tf_op jit(solution)/shard_map/ppermute | solution.py:452
  29.8 2.2 %collective-permute-start.1 = (bf16[2,2,10,8,128]{4,3,2,1,0:T(8,128)(2,1)}, bf16[2,2,10,8,128]{4,3,2,1,0:T(8,128)(2,1)S(1)}, u32[]{:S(2)}, u32[]{:S(2)}) collective-permute-start(bf16[2,2,10,8,128]{4,3,2,1,0:T(8,128)(2,1)} %get-tuple-element.42), channel_id=1, source_target_pairs={{0,63},{1,0},{2,1},{3,2},{4,3},{5,4},{6,5},{7,6},{8,7},{9,8},{10,9... | collective-permute-start | bytes 245768 | tf_op jit(solution)/shard_map/ppermute | solution.py:446
  32.0 0.0 copy-start
  32.0 1.0 %copy-done = bf16[2,8,10,8,128]{4,3,2,1,0:T(8,128)(2,1)S(1)} copy-done((bf16[2,8,10,8,128]{4,3,2,1,0:T(8,128)(2,1)S(1)}, bf16[2,8,10,8,128]{4,3,2,1,0:T(8,128)(2,1)}, u32[]{:S(2)}) %copy-start) | copy-done | bytes 327704
  33.0 0.0 copy-start.1
  33.0 0.8 %copy-done.1 = bf16[128,128]{1,0:T(8,128)(2,1)S(1)} copy-done((bf16[128,128]{1,0:T(8,128)(2,1)S(1)}, bf16[128,128]{1,0:T(8,128)(2,1)}, u32[]{:S(2)}) %copy-start.1) | copy-done | bytes 32792
  33.7 0.0 copy-start.2
  33.7 0.7 copy-done.2
  34.5 0.0 copy-start.3
  34.5 0.7 copy-done.3
  35.2 0.0 collective-permute-done.right
  35.2 4.0 %early.1 = (f32[96,128]{1,0:T(8,128)S(1)}, bf16[256,1280]{1,0:T(8,128)(2,1)S(1)}, f32[3,25,32,128]{3,2,1,0:T(8,128)S(1)}, f32[3,9,32,128]{3,2,1,0:T(8,128)S(1)}) custom-call(bf16[2,8,10,8,128]{4,3,2,1,0:T(8,128)(2,1)S(1)} %get-tuple-element.35.own, bf16[2,8,10,8,128]{4,3,2,1,0:T(8,128)(2,1)S(1)} %collective-permute-done.right, ...), custom_call_target="tpu_custom_call" | custom-call | flops 4000000000 | bytes 8000000 | tf_op jit(solution)/shard_map/early/pallas_call | solution.py:384
  39.2 0.0 collective-permute-done.2.across
  39.2 0.0 collective-permute-done.1.up
  39.2 1.8 %late.1 = (f32[8,128]{1,0:T(8,128)S(1)}, f32[64,1,128]{2,1,0:T(1,128)}, bf16[128,1280]{1,0:T(8,128)(2,1)S(1)}, f32[1,25,32,128]{3,2,1,0:T(8,128)S(1)}, f32[1,9,32,128]{3,2,1,0:T(8,128)S(1)}) custom-call(bf16[256,1280]{1,0:T(8,128)(2,1)S(1)} %get-tuple-element.39.known.table, bf16[2,2,10,8,128]{4,3,2,1,0:T(8,128)(2,1)S(1)} %collective-permute-done.1.up, ...), custom_call_target="tpu_custom_call" | custom-call | flops 1000000000 | bytes 2000000 | tf_op jit(solution)/shard_map/late/pallas_call | solution.py:397
  41.1 5.4 %all-to-all-start = ((f32[64,1,128]{2,1,0:T(1,128)}), f32[64,1,128]{2,1,0:T(1,128)S(1)}, u32[]{:S(2)}, u32[]{:S(2)}) async-start(f32[64,1,128]{2,1,0:T(1,128)} %get-tuple-element.49), calls=%async_computation | async-start | bytes 65536 | tf_op jit(solution)/shard_map/all_to_all | solution.py:457
  46.5 2.8 %backward.1 = (f32[4,8,128]{2,1,0:T(8,128)S(1)}, f32[8,128]{1,0:T(8,128)S(1)}) custom-call(bf16[256,1280]{1,0:T(8,128)(2,1)S(1)} %get-tuple-element.39.known.table, f32[3,25,32,128]{3,2,1,0:T(8,128)S(1)} %get-tuple-element.40.edge, f32[3,9,32,128]{3,2,1,0:T(8,128)S(1)} %get-tuple-element.41.back, bf16[128,1280]{1,0:T(8,128)(2,1)S(1)} %get-tuple-element.44.late_table, ...), custom_call_target="tpu_custom_call" | custom-call | flops 4000000000 | bytes 8000000 | tf_op jit(solution)/shard_map/backward/pallas_call | solution.py:424
  49.3 6.3 %all-to-all-done.gathered = f32[64,1,128]{2,1,0:T(1,128)S(1)} async-done(((f32[64,1,128]{2,1,0:T(1,128)}), f32[64,1,128]{2,1,0:T(1,128)S(1)}, u32[]{:S(2)}, u32[]{:S(2)}) %all-to-all-start) | async-done | bytes 32800 | tf_op jit(solution)/shard_map/all_to_all | solution.py:457
  55.6 0.7 relay.1
  56.3 2.6 %collective-permute-start.3 = (f32[8,128]{1,0:T(8,128)S(1)}, f32[8,128]{1,0:T(8,128)S(1)}, u32[]{:S(2)}, u32[]{:S(2)}) collective-permute-start(f32[8,128]{1,0:T(8,128)S(1)} %get-tuple-element.51), channel_id=1, source_target_pairs={{0,1},{1,2},{2,3},{3,4},{4,5},{5,6},{6,7},{7,8},{8,9},{9,10},{10,1... | collective-permute-start | bytes 12296 | tf_op jit(solution)/shard_map/ppermute | solution.py:461
  58.9 4.2 %all-to-all-start.1 = ((f32[16,1,128]{2,1,0:T(1,128)}), f32[16,1,128]{2,1,0:T(1,128)S(1)}, u32[]{:S(2)}, u32[]{:S(2)}) async-start(f32[16,1,128]{2,1,0:T(1,128)} %relay.1), calls=%async_computation.1 | async-start | bytes 16384 | tf_op jit(solution)/shard_map/all_to_all | solution.py:460
  63.0 1.8 %collective-permute-done.3 = f32[8,128]{1,0:T(8,128)S(1)} collective-permute-done((f32[8,128]{1,0:T(8,128)S(1)}, f32[8,128]{1,0:T(8,128)S(1)}, u32[]{:S(2)}, u32[]{:S(2)}) %collective-permute-start.3) | collective-permute-done | bytes 4128 | tf_op jit(solution)/shard_map/ppermute | solution.py:461
  64.9 3.9 %collective-permute-start.4 = (f32[4,4,128]{2,1,0:T(4,128)S(1)}, f32[4,4,128]{2,1,0:T(4,128)S(1)}, u32[]{:S(2)}, u32[]{:S(2)}) collective-permute-start(f32[4,4,128]{2,1,0:T(4,128)S(1)} %slice.69), channel_id=1, source_target_pairs={{0,64},{64,128},{128,192},{192,256},{256,320},{320,384},{384,448},... | collective-permute-start | bytes 24584 | tf_op jit(solution)/shard_map/ppermute | solution.py:463
  68.8 0.1 reshape.84
  69.0 0.6 collective-permute-done.4
  69.6 0.1 reshape.85
  69.7 0.6 fusion
  70.4 0.6 fusion.1
  71.0 3.4 %all-to-all-done.1 = f32[16,1,128]{2,1,0:T(1,128)S(1)} async-done(((f32[16,1,128]{2,1,0:T(1,128)}), f32[16,1,128]{2,1,0:T(1,128)S(1)}, u32[]{:S(2)}, u32[]{:S(2)}) %all-to-all-start.1) | async-done | bytes 8224 | tf_op jit(solution)/shard_map/all_to_all | solution.py:460
  74.3 0.6 reduce_sum.9
  (9 shorter events, 0.1 us)
Async XLA Ops:
  2.5 32.6 %collective-permute-start = (bf16[2,8,10,8,128]{4,3,2,1,0:T(8,128)(2,1)}, bf16[2,8,10,8,128]{4,3,2,1,0:T(8,128)(2,1)S(1)}, u32[]{:S(2)}, u32[]{:S(2)}) collective-permute-start(bf16[2,8,10,8,128]{4,3,2,1,0:T(8,128)(2,1)} %get-tuple-element.34.own), channel_id=1, source_target_pairs={{0,960},{64,0},{128,64},{192,128},{256,192},{320,256},{384,320},{4... | collective-permute-start | bytes 983048 | tf_op jit(solution)/shard_map/ppermute | solution.py:445
  18.6 20.6 %collective-permute-start.2 = (bf16[2,2,10,8,128]{4,3,2,1,0:T(8,128)(2,1)}, bf16[2,2,10,8,128]{4,3,2,1,0:T(8,128)(2,1)S(1)}, u32[]{:S(2)}, u32[]{:S(2)}) collective-permute-start(bf16[2,2,10,8,128]{4,3,2,1,0:T(8,128)(2,1)} %get-tuple-element.42), channel_id=1, source_target_pairs={{0,1023},{1,960},{2,961},{3,962},{4,963},{5,964},{6,965},{7,966},{... | collective-permute-start | bytes 245768 | tf_op jit(solution)/shard_map/ppermute | solution.py:452
  29.8 9.4 %collective-permute-start.1 = (bf16[2,2,10,8,128]{4,3,2,1,0:T(8,128)(2,1)}, bf16[2,2,10,8,128]{4,3,2,1,0:T(8,128)(2,1)S(1)}, u32[]{:S(2)}, u32[]{:S(2)}) collective-permute-start(bf16[2,2,10,8,128]{4,3,2,1,0:T(8,128)(2,1)} %get-tuple-element.42), channel_id=1, source_target_pairs={{0,63},{1,0},{2,1},{3,2},{4,3},{5,4},{6,5},{7,6},{8,7},{9,8},{10,9... | collective-permute-start | bytes 245768 | tf_op jit(solution)/shard_map/ppermute | solution.py:446
  32.0 1.0 %copy-start = (bf16[2,8,10,8,128]{4,3,2,1,0:T(8,128)(2,1)S(1)}, bf16[2,8,10,8,128]{4,3,2,1,0:T(8,128)(2,1)}, u32[]{:S(2)}) copy-start(bf16[2,8,10,8,128]{4,3,2,1,0:T(8,128)(2,1)} %get-tuple-element.34.own) | copy-start | bytes 983044
  33.0 0.8 %copy-start.1 = (bf16[128,128]{1,0:T(8,128)(2,1)S(1)}, bf16[128,128]{1,0:T(8,128)(2,1)}, u32[]{:S(2)}) copy-start(bf16[128,128]{1,0:T(8,128)(2,1)} %mix.1) | copy-start | bytes 98308
  33.7 0.7 copy-start.2
  34.5 0.7 copy-start.3
  41.1 14.5 %all-to-all-start = ((f32[64,1,128]{2,1,0:T(1,128)}), f32[64,1,128]{2,1,0:T(1,128)S(1)}, u32[]{:S(2)}, u32[]{:S(2)}) async-start(f32[64,1,128]{2,1,0:T(1,128)} %get-tuple-element.49), calls=%async_computation | async-start | bytes 65536 | tf_op jit(solution)/shard_map/all_to_all | solution.py:457
  56.3 8.6 %collective-permute-start.3 = (f32[8,128]{1,0:T(8,128)S(1)}, f32[8,128]{1,0:T(8,128)S(1)}, u32[]{:S(2)}, u32[]{:S(2)}) collective-permute-start(f32[8,128]{1,0:T(8,128)S(1)} %get-tuple-element.51), channel_id=1, source_target_pairs={{0,1},{1,2},{2,3},{3,4},{4,5},{5,6},{6,7},{7,8},{8,9},{9,10},{10,1... | collective-permute-start | bytes 12296 | tf_op jit(solution)/shard_map/ppermute | solution.py:461
  58.9 15.5 %all-to-all-start.1 = ((f32[16,1,128]{2,1,0:T(1,128)}), f32[16,1,128]{2,1,0:T(1,128)S(1)}, u32[]{:S(2)}, u32[]{:S(2)}) async-start(f32[16,1,128]{2,1,0:T(1,128)} %relay.1), calls=%async_computation.1 | async-start | bytes 16384 | tf_op jit(solution)/shard_map/all_to_all | solution.py:460
  64.9 4.7 %collective-permute-start.4 = (f32[4,4,128]{2,1,0:T(4,128)S(1)}, f32[4,4,128]{2,1,0:T(4,128)S(1)}, u32[]{:S(2)}, u32[]{:S(2)}) collective-permute-start(f32[4,4,128]{2,1,0:T(4,128)S(1)} %slice.69), channel_id=1, source_target_pairs={{0,64},{64,128},{128,192},{192,256},{256,320},{320,384},{384,448},... | collective-permute-start | bytes 24584 | tf_op jit(solution)/shard_map/ppermute | solution.py:463

commit v5 on v4

--- a/solution.py
+++ b/solution.py
@@ -22,7 +22,10 @@
 NT = (((1,), (1,)), ((), ()))
 
 
-def pack_kernel(features, places, present, lists, out, low_out, positions, occupied, neighbours, done):
+def pack_kernel(
+    features, places, present, lists, weight, out_weight, mix,
+    out, low_out, shared, positions, occupied, neighbours, mix_copy, done,
+):
     moves = [
         pltpu.make_async_copy(source, target, done.at[i])
         for i, (source, target) in enumerate(
@@ -31,6 +34,9 @@
                 (present, occupied),
                 (lists, neighbours),
                 (features, out.at[:, :, 0:9]),
+                (weight, shared.at[0:7]),
+                (out_weight, shared.at[7, 0:1]),
+                (mix, mix_copy),
             )
         )
     ]
@@ -60,7 +66,9 @@
             tile = jnp.where(kind == 1, pltpu.roll(middle, back, 1), tile)
             tile = jnp.where(kind == 0, pltpu.roll(high, back, 1), tile)
             out[x, y, 9] = tile.astype(BF16)
-    moves[3].wait()
+    for move in moves[3:]:
+        move.wait()
+    shared[8:24] = mix_copy[...].astype(F32).reshape(16, 8, C)
     low_out[...] = out[:, 0:2]
 
 
@@ -245,11 +253,11 @@
     spread_out[...] = jnp.broadcast_to(total[None], spread_out.shape)
 
 
-def stage_kernel(own, weight, mix, out_weight, own_copy, weight_copy, mix_copy, out_weight_copy):
+def stage_kernel(own, shared, own_copy, weight, mix, out_weight):
     own_copy[...] = own[...]
-    weight_copy[...] = weight[...]
-    mix_copy[...] = mix[...]
-    out_weight_copy[...] = out_weight[...]
+    weight[...] = shared[0:7]
+    out_weight[...] = shared[7, 0:1]
+    mix[...] = shared[8:24].reshape(C, C).astype(BF16)
 
 
 def relay_kernel(gathered, out):
@@ -335,38 +343,65 @@
         send_up[kind : kind + 1] = pairs[4:5]
 
 
+def finish_kernel(near, from_left, from_down, from_across, forces, energies):
+    row = lax.broadcasted_iota(jnp.int32, (8, C), 0)
+    for kind in range(4):
+        mine = near[kind] + jnp.where(row == 0, from_down[kind : kind + 1], 0.0)
+        theirs = from_left[kind] + jnp.where(row == 0, from_across[kind : kind + 1], 0.0)
+        columns = (
+            pltpu.roll(mine, C - 16, 1) + pltpu.roll(theirs, C - 8, 1),
+            mine + pltpu.roll(theirs, C - 24, 1),
+        )
+        for x in range(2):
+            for odd in range(2):
+                cells = columns[x] if odd == 0 else pltpu.roll(columns[x], C - 32, 1)
+                for p in range(4):
+                    y = 2 * p + odd
+                    if kind < 3:
+                        forces[kind, x, y : y + 1] = cells[p : p + 1, 0:8]
+                    else:
+                        energies[x, y : y + 1] = cells[p : p + 1, 0:8]
+
+
 VMEM = pl.BlockSpec(memory_space=pltpu.VMEM)
 
 
-def pack_call(features, positions, occupied, neighbours):
+def pack_call(features, positions, occupied, neighbours, *weights):
     return pl.pallas_call(
         pack_kernel,
         out_shape=(
             jax.ShapeDtypeStruct((2, 8, 10, 8, C), BF16),
             jax.ShapeDtypeStruct((2, 2, 10, 8, C), BF16),
+            jax.ShapeDtypeStruct((24, 8, C), F32),
         ),
-        in_specs=[pl.BlockSpec(memory_space=pl.ANY)] * 4,
-        out_specs=(VMEM, VMEM),
+        in_specs=[pl.BlockSpec(memory_space=pl.ANY)] * 7,
+        out_specs=(VMEM,) * 3,
         scratch_shapes=[
             pltpu.VMEM(positions.shape, F32),
             pltpu.VMEM(occupied.shape, jnp.int32),
             pltpu.VMEM(neighbours.shape, jnp.int32),
-            pltpu.SemaphoreType.DMA((4,)),
+            pltpu.VMEM((C, C), BF16),
+            pltpu.SemaphoreType.DMA((7,)),
         ],
         name="pack",
-    )(features, positions, occupied, neighbours)
-
-
-def stage_call(*arrays):
+    )(features, positions, occupied, neighbours, *weights)
+
+
+def stage_call(own, shared):
     return pl.pallas_call(
         stage_kernel,
-        out_shape=tuple(jax.ShapeDtypeStruct(a.shape, a.dtype) for a in arrays),
-        in_specs=[VMEM] * 4,
+        out_shape=(
+            jax.ShapeDtypeStruct(own.shape, BF16),
+            jax.ShapeDtypeStruct((7, NB, C), F32),
+            jax.ShapeDtypeStruct((C, C), BF16),
+            jax.ShapeDtypeStruct((1, C), F32),
+        ),
+        in_specs=[VMEM] * 2,
         out_specs=(VMEM,) * 4,
         compiler_params=pltpu.CompilerParams(vmem_limit_bytes=8 * 1024 * 1024),
         cost_estimate=pl.CostEstimate(flops=2_000_000, bytes_accessed=2_000_000, transcendentals=0),
         name="stage",
-    )(*arrays)
+    )(own, shared)
 
 
 def results(groups, rows):
@@ -433,6 +468,21 @@
     )(*arrays)
 
 
+def finish_call(*arrays):
+    return pl.pallas_call(
+        finish_kernel,
+        out_shape=(
+            jax.ShapeDtypeStruct((3, 2, 8, 8), F32),
+            jax.ShapeDtypeStruct((2, 8, 8), F32),
+        ),
+        in_specs=[VMEM] * 4,
+        out_specs=(VMEM,) * 2,
+        compiler_params=pltpu.CompilerParams(vmem_limit_bytes=4 * 1024 * 1024),
+        cost_estimate=pl.CostEstimate(flops=1000, bytes_accessed=1000, transcendentals=0),
+        name="finish",
+    )(*arrays)
+
+
 def ring(size, step):
     return [(i, (i + step) % size) for i in range(size)]
 
@@ -441,7 +491,10 @@
     gy = outer + inner
     size_x = lax.axis_size("gx")
     size_y = lax.axis_size(gy)
-    own, low = pack_call(jnp.transpose(features, (0, 1, 3, 2, 4)), positions, occupied, neighbours)
+    own, low, shared = pack_call(
+        jnp.transpose(features, (0, 1, 3, 2, 4)), positions, occupied, neighbours,
+        radial_weight, out_weight[None], mix_weight,
+    )
     right = lax.ppermute(own, "gx", ring(size_x, -1))
     up = lax.ppermute(low, gy, ring(size_y, -1))
     corner = [
@@ -450,26 +503,20 @@
         for y in range(size_y)
     ]
     across = lax.ppermute(low, ("gx",) + gy, corner)
-    own, *shared = stage_call(own, radial_weight, mix_weight, out_weight[None])
+    own, *shared = stage_call(own, shared)
     early, *first = early_call(own, right, *shared)
     plane = size_x * lax.axis_size(outer)
     energy, spread, *last = late_call(plane, first[0], up, across, early, *shared)
     gathered = lax.all_to_all(spread, ("gx",) + outer, 0, 0)
     near, send_up = backward_call(*first, *last, shared[0], energy)
-    spread, send_up = lax.optimization_barrier((relay_call(gathered, lax.axis_size(inner)), send_up))
+    spread = relay_call(gathered, lax.axis_size(inner))
+    spread, near, send_up = lax.optimization_barrier((spread, near, send_up))
     gathered = lax.all_to_all(spread, inner, 0, 0)
+    from_left = lax.ppermute(near, "gx", ring(size_x, 1))
     from_down = lax.ppermute(send_up, gy, ring(size_y, 1))
-    near = near.at[:, 0].add(from_down[:4])[:, :4]
-    from_left = lax.ppermute(near, "gx", ring(size_x, 1))
-    total_energy = jnp.sum(gathered)
-
-    def column(block, place):
-        return block[:, :, :64].reshape(4, 8, 4, 8)[:, :, place]
-
-    first = column(near, 2) + column(from_left, 1)
-    second = column(near, 0) + column(from_left, 3)
-    cells = jnp.stack([first, second], axis=1)
-    return cells[:3], cells[3], total_energy
+    from_across = lax.ppermute(send_up, ("gx",) + gy, [(j, i) for i, j in corner])
+    forces, slot_energy_values = finish_call(near, from_left, from_down, from_across)
+    return forces, slot_energy_values, jnp.sum(gathered)
 
 
 def solution(mesh):

time: 75.5 us -> 77.1 us (1.021)
  starting transfers between devices: 45.5 us -> 49.2 us
  local copies, waits for them, and re-layouts: 3.43 us -> 1.86 us
  other arithmetic: 1.84 us -> 0.62 us
  Pallas kernels: 11.3 us -> 12.1 us
    all_to_all x1, waiting for transfers between devices: 3.39 us -> 0.01 us  [on_device(): gathered = lax.all_to_all(spread, inner, 0, 0)]
    ppermute x0 -> x1, starting transfers between devices: none -> 3.27 us  [on_device(): lax.ppermute(send_up, ('gx',) + gy, [(j, i) for i, j in corner])]
    ppermute x0 -> x1, waiting for transfers between devices: none -> 3.07 us  [on_device(): lax.ppermute(send_up, ('gx',) + gy, [(j, i) for i, j in corner])]
    unnamed x8 -> x4, local copies, waits for them, and re-layouts: 3.13 us -> 1.86 us
    ppermute x1, starting transfers between devices: 3.93 us -> 3.05 us  [on_device(): from_left = lax.ppermute(near, 'gx', ring(size_x, 1))]
  transfers between devices with their start and end apart: 7 -> 8, of which waited for: 4 -> 3; matrix products, arithmetic and copies ran while one was open for 2% -> 0% of each run, Pallas kernels for 9% -> 10%
where the time goes in v5:
time: 77.1 us; the launch traced here: 76.3 us
  starting transfers between devices  49.2 us (64%)
  Pallas kernels  12.1 us (16%)
  waiting for transfers between devices  11.8 us (15%)
  local copies, waits for them, and re-layouts  1.86 us (2%)
    ppermute x1, starting transfers between devices, on_device(): right = lax.ppermute(own, 'gx', ring(size_x, -1))  16.1 us
    ppermute x1, starting transfers between devices, on_device(): across = lax.ppermute(low, ('gx',) + gy, corner)  11.2 us
    all_to_all x1, waiting for transfers between devices, on_device(): gathered = lax.all_to_all(spread, ('gx',) + outer, 0, 0)  6.3 us
    all_to_all x1, starting transfers between devices, on_device(): gathered = lax.all_to_all(spread, ('gx',) + outer, 0, 0)  5.42 us
    all_to_all x1, starting transfers between devices, on_device(): gathered = lax.all_to_all(spread, inner, 0, 0)  4.93 us
    pallas_call x1, Pallas kernels, early_call(): pl.pallas_call(early_kernel, out_shape=(jax.ShapeDtypeStruct((3 * ROWS, C...  4.02 us
    ppermute x1, starting transfers between devices, on_device(): lax.ppermute(send_up, ('gx',) + gy, [(j, i) for i, j in corner])  3.27 us
    ppermute x1, starting transfers between devices, on_device(): from_down = lax.ppermute(send_up, gy, ring(size_y, 1))  3.09 us
  transfers between devices with their start and end apart: 8, of which 3 were waited for; matrix products, arithmetic and copies ran while one was open for 0% of the time, Pallas kernels for 10%

profile of v5, /device:TPU:1, one launch (start us, length us, event | category | flops | bytes accessed | tf_op | source)
XLA Modules:
  0.0 76.3 jit_solution(7850644781990729764)
XLA Ops:
  0.6 2.0 %pack.1 = (bf16[2,8,10,8,128]{4,3,2,1,0:T(8,128)(2,1)}, bf16[2,2,10,8,128]{4,3,2,1,0:T(8,128)(2,1)}, f32[24,8,128]{2,1,0:T(8,128)}) custom-call(bf16[2,8,9,8,128]{4,3,2,1,0:T(8,128)(2,1)} %bitcast.2, f32[3,2,8,8]{3,2,1,0:T(8,128)} %places.1, s32[2,8,8]{2,1,0:T(8,128)} %present.1, s32[2,8,8,32]{3,2,1,0:T(8,128)} %lists.1, f32[7,8,128]{2,1,0:T(8,128)} %weight.1, ...), custom_call_target="tpu_custom_call" | custom-call | tf_op jit(solution)/shard_map/pack/pallas_call | solution.py:370
  2.6 16.1 %collective-permute-start = (bf16[2,8,10,8,128]{4,3,2,1,0:T(8,128)(2,1)}, bf16[2,8,10,8,128]{4,3,2,1,0:T(8,128)(2,1)S(1)}, u32[]{:S(2)}, u32[]{:S(2)}) collective-permute-start(bf16[2,8,10,8,128]{4,3,2,1,0:T(8,128)(2,1)} %get-tuple-element.26.own), channel_id=1, source_target_pairs={{0,960},{64,0},{128,64},{192,128},{256,192},{320,256},{384,320},{4... | collective-permute-start | bytes 983048 | tf_op jit(solution)/shard_map/ppermute | solution.py:498
  18.7 11.2 %collective-permute-start.2 = (bf16[2,2,10,8,128]{4,3,2,1,0:T(8,128)(2,1)}, bf16[2,2,10,8,128]{4,3,2,1,0:T(8,128)(2,1)S(1)}, u32[]{:S(2)}, u32[]{:S(2)}) collective-permute-start(bf16[2,2,10,8,128]{4,3,2,1,0:T(8,128)(2,1)} %get-tuple-element.33), channel_id=1, source_target_pairs={{0,1023},{1,960},{2,961},{3,962},{4,963},{5,964},{6,965},{7,966},{... | collective-permute-start | bytes 245768 | tf_op jit(solution)/shard_map/ppermute | solution.py:505
  29.9 2.2 %collective-permute-start.1 = (bf16[2,2,10,8,128]{4,3,2,1,0:T(8,128)(2,1)}, bf16[2,2,10,8,128]{4,3,2,1,0:T(8,128)(2,1)S(1)}, u32[]{:S(2)}, u32[]{:S(2)}) collective-permute-start(bf16[2,2,10,8,128]{4,3,2,1,0:T(8,128)(2,1)} %get-tuple-element.33), channel_id=1, source_target_pairs={{0,63},{1,0},{2,1},{3,2},{4,3},{5,4},{6,5},{7,6},{8,7},{9,8},{10,9... | collective-permute-start | bytes 245768 | tf_op jit(solution)/shard_map/ppermute | solution.py:499
  32.1 0.0 copy-start
  32.1 1.0 %copy-done = bf16[2,8,10,8,128]{4,3,2,1,0:T(8,128)(2,1)S(1)} copy-done((bf16[2,8,10,8,128]{4,3,2,1,0:T(8,128)(2,1)S(1)}, bf16[2,8,10,8,128]{4,3,2,1,0:T(8,128)(2,1)}, u32[]{:S(2)}) %copy-start) | copy-done | bytes 327704
  33.0 0.0 copy-start.1
  33.0 0.9 %copy-done.1 = f32[24,8,128]{2,1,0:T(8,128)S(1)} copy-done((f32[24,8,128]{2,1,0:T(8,128)S(1)}, f32[24,8,128]{2,1,0:T(8,128)}, u32[]{:S(2)}) %copy-start.1) | copy-done | bytes 98328
  34.0 0.0 collective-permute-done.right
  34.0 4.0 %early.1 = (f32[96,128]{1,0:T(8,128)S(1)}, bf16[256,1280]{1,0:T(8,128)(2,1)S(1)}, f32[3,25,32,128]{3,2,1,0:T(8,128)S(1)}, f32[3,9,32,128]{3,2,1,0:T(8,128)S(1)}) custom-call(bf16[2,8,10,8,128]{4,3,2,1,0:T(8,128)(2,1)S(1)} %get-tuple-element.28.own, bf16[2,8,10,8,128]{4,3,2,1,0:T(8,128)(2,1)S(1)} %collective-permute-done.right, ...), custom_call_target="tpu_custom_call" | custom-call | flops 4000000000 | bytes 8000000 | tf_op jit(solution)/shard_map/early/pallas_call | solution.py:419
  38.0 0.0 collective-permute-done.2.across
  38.0 0.0 collective-permute-done.1.up
  38.0 1.8 %late.1 = (f32[8,128]{1,0:T(8,128)S(1)}, f32[64,1,128]{2,1,0:T(1,128)}, bf16[128,1280]{1,0:T(8,128)(2,1)S(1)}, f32[1,25,32,128]{3,2,1,0:T(8,128)S(1)}, f32[1,9,32,128]{3,2,1,0:T(8,128)S(1)}) custom-call(bf16[256,1280]{1,0:T(8,128)(2,1)S(1)} %get-tuple-element.32.known.table, bf16[2,2,10,8,128]{4,3,2,1,0:T(8,128)(2,1)S(1)} %collective-permute-done.1.up, ...), custom_call_target="tpu_custom_call" | custom-call | flops 1000000000 | bytes 2000000 | tf_op jit(solution)/shard_map/late/pallas_call | solution.py:432
  39.8 5.4 %all-to-all-start = ((f32[64,1,128]{2,1,0:T(1,128)}), f32[64,1,128]{2,1,0:T(1,128)S(1)}, u32[]{:S(2)}, u32[]{:S(2)}) async-start(f32[64,1,128]{2,1,0:T(1,128)} %get-tuple-element.35), calls=%async_computation | async-start | bytes 65536 | tf_op jit(solution)/shard_map/all_to_all | solution.py:510
  45.3 2.8 %backward.1 = (f32[4,8,128]{2,1,0:T(8,128)S(1)}, f32[8,128]{1,0:T(8,128)S(1)}) custom-call(bf16[256,1280]{1,0:T(8,128)(2,1)S(1)} %get-tuple-element.32.known.table, f32[3,25,32,128]{3,2,1,0:T(8,128)S(1)} %get-tuple-element.36.edge, f32[3,9,32,128]{3,2,1,0:T(8,128)S(1)} %get-tuple-element.37.back, bf16[128,1280]{1,0:T(8,128)(2,1)S(1)} %get-tuple-element.38.late_table, ...), custom_call_target="tpu_custom_call" | custom-call | flops 4000000000 | bytes 8000000 | tf_op jit(solution)/shard_map/backward/pallas_call | solution.py:459
  48.1 6.3 %all-to-all-done.gathered = f32[64,1,128]{2,1,0:T(1,128)S(1)} async-done(((f32[64,1,128]{2,1,0:T(1,128)}), f32[64,1,128]{2,1,0:T(1,128)S(1)}, u32[]{:S(2)}, u32[]{:S(2)}) %all-to-all-start) | async-done | bytes 32800 | tf_op jit(solution)/shard_map/all_to_all | solution.py:510
  54.4 0.7 relay.1
  55.1 4.9 %all-to-all-start.1 = ((f32[16,1,128]{2,1,0:T(1,128)}), f32[16,1,128]{2,1,0:T(1,128)S(1)}, u32[]{:S(2)}, u32[]{:S(2)}) async-start(f32[16,1,128]{2,1,0:T(1,128)} %relay.1), calls=%async_computation.1 | async-start | bytes 16384 | tf_op jit(solution)/shard_map/all_to_all | solution.py:514
  60.0 3.0 %collective-permute-start.3 = (f32[4,8,128]{2,1,0:T(8,128)S(1)}, f32[4,8,128]{2,1,0:T(8,128)S(1)}, u32[]{:S(2)}, u32[]{:S(2)}) collective-permute-start(f32[4,8,128]{2,1,0:T(8,128)S(1)} %get-tuple-element.44.near), channel_id=1, source_target_pairs={{0,64},{64,128},{128,192},{192,256},{256,320},{320,384},{384,448},... | collective-permute-start | bytes 49160 | tf_op jit(solution)/shard_map/ppermute | solution.py:515
  63.0 3.3 %collective-permute-start.5 = (f32[8,128]{1,0:T(8,128)S(1)}, f32[8,128]{1,0:T(8,128)S(1)}, u32[]{:S(2)}, u32[]{:S(2)}) collective-permute-start(f32[8,128]{1,0:T(8,128)S(1)} %get-tuple-element.45), channel_id=1, source_target_pairs={{1023,0},{960,1},{961,2},{962,3},{963,4},{964,5},{965,6},{966,7},{... | collective-permute-start | bytes 12296 | tf_op jit(solution)/shard_map/ppermute | solution.py:517
  66.3 3.1 %collective-permute-start.4 = (f32[8,128]{1,0:T(8,128)S(1)}, f32[8,128]{1,0:T(8,128)S(1)}, u32[]{:S(2)}, u32[]{:S(2)}) collective-permute-start(f32[8,128]{1,0:T(8,128)S(1)} %get-tuple-element.45), channel_id=1, source_target_pairs={{0,1},{1,2},{2,3},{3,4},{4,5},{5,6},{6,7},{7,8},{8,9},{9,10},{10,1... | collective-permute-start | bytes 12296 | tf_op jit(solution)/shard_map/ppermute | solution.py:516
  69.4 3.1 %collective-permute-done.5.from_across = f32[8,128]{1,0:T(8,128)S(1)} collective-permute-done((f32[8,128]{1,0:T(8,128)S(1)}, f32[8,128]{1,0:T(8,128)S(1)}, u32[]{:S(2)}, u32[]{:S(2)}) %collective-permute-start.5) | collective-permute-done | bytes 4128 | tf_op jit(solution)/shard_map/ppermute | solution.py:517
  72.5 2.4 %collective-permute-done.4.from_down = f32[8,128]{1,0:T(8,128)S(1)} collective-permute-done((f32[8,128]{1,0:T(8,128)S(1)}, f32[8,128]{1,0:T(8,128)S(1)}, u32[]{:S(2)}, u32[]{:S(2)}) %collective-permute-start.4) | collective-permute-done | bytes 4128 | tf_op jit(solution)/shard_map/ppermute | solution.py:516
  74.9 0.0 collective-permute-done.3.from_left
  74.9 0.8 finish.1
  75.7 0.0 all-to-all-done.1
  75.7 0.6 reduce_sum.9
  (1 shorter events, 0.0 us)
Async XLA Ops:
  2.6 31.3 %collective-permute-start = (bf16[2,8,10,8,128]{4,3,2,1,0:T(8,128)(2,1)}, bf16[2,8,10,8,128]{4,3,2,1,0:T(8,128)(2,1)S(1)}, u32[]{:S(2)}, u32[]{:S(2)}) collective-permute-start(bf16[2,8,10,8,128]{4,3,2,1,0:T(8,128)(2,1)} %get-tuple-element.26.own), channel_id=1, source_target_pairs={{0,960},{64,0},{128,64},{192,128},{256,192},{320,256},{384,320},{4... | collective-permute-start | bytes 983048 | tf_op jit(solution)/shard_map/ppermute | solution.py:498
  18.7 19.3 %collective-permute-start.2 = (bf16[2,2,10,8,128]{4,3,2,1,0:T(8,128)(2,1)}, bf16[2,2,10,8,128]{4,3,2,1,0:T(8,128)(2,1)S(1)}, u32[]{:S(2)}, u32[]{:S(2)}) collective-permute-start(bf16[2,2,10,8,128]{4,3,2,1,0:T(8,128)(2,1)} %get-tuple-element.33), channel_id=1, source_target_pairs={{0,1023},{1,960},{2,961},{3,962},{4,963},{5,964},{6,965},{7,966},{... | collective-permute-start | bytes 245768 | tf_op jit(solution)/shard_map/ppermute | solution.py:505
  29.9 8.1 %collective-permute-start.1 = (bf16[2,2,10,8,128]{4,3,2,1,0:T(8,128)(2,1)}, bf16[2,2,10,8,128]{4,3,2,1,0:T(8,128)(2,1)S(1)}, u32[]{:S(2)}, u32[]{:S(2)}) collective-permute-start(bf16[2,2,10,8,128]{4,3,2,1,0:T(8,128)(2,1)} %get-tuple-element.33), channel_id=1, source_target_pairs={{0,63},{1,0},{2,1},{3,2},{4,3},{5,4},{6,5},{7,6},{8,7},{9,8},{10,9... | collective-permute-start | bytes 245768 | tf_op jit(solution)/shard_map/ppermute | solution.py:499
  32.1 1.0 %copy-start = (bf16[2,8,10,8,128]{4,3,2,1,0:T(8,128)(2,1)S(1)}, bf16[2,8,10,8,128]{4,3,2,1,0:T(8,128)(2,1)}, u32[]{:S(2)}) copy-start(bf16[2,8,10,8,128]{4,3,2,1,0:T(8,128)(2,1)} %get-tuple-element.26.own) | copy-start | bytes 983044
  33.0 0.9 %copy-start.1 = (f32[24,8,128]{2,1,0:T(8,128)S(1)}, f32[24,8,128]{2,1,0:T(8,128)}, u32[]{:S(2)}) copy-start(f32[24,8,128]{2,1,0:T(8,128)} %get-tuple-element.27.shared) | copy-start | bytes 294916
  39.8 14.5 %all-to-all-start = ((f32[64,1,128]{2,1,0:T(1,128)}), f32[64,1,128]{2,1,0:T(1,128)S(1)}, u32[]{:S(2)}, u32[]{:S(2)}) async-start(f32[64,1,128]{2,1,0:T(1,128)} %get-tuple-element.35), calls=%async_computation | async-start | bytes 65536 | tf_op jit(solution)/shard_map/all_to_all | solution.py:510
  55.1 20.6 %all-to-all-start.1 = ((f32[16,1,128]{2,1,0:T(1,128)}), f32[16,1,128]{2,1,0:T(1,128)S(1)}, u32[]{:S(2)}, u32[]{:S(2)}) async-start(f32[16,1,128]{2,1,0:T(1,128)} %relay.1), calls=%async_computation.1 | async-start | bytes 16384 | tf_op jit(solution)/shard_map/all_to_all | solution.py:514
  60.0 14.9 %collective-permute-start.3 = (f32[4,8,128]{2,1,0:T(8,128)S(1)}, f32[4,8,128]{2,1,0:T(8,128)S(1)}, u32[]{:S(2)}, u32[]{:S(2)}) collective-permute-start(f32[4,8,128]{2,1,0:T(8,128)S(1)} %get-tuple-element.44.near), channel_id=1, source_target_pairs={{0,64},{64,128},{128,192},{192,256},{256,320},{320,384},{384,448},... | collective-permute-start | bytes 49160 | tf_op jit(solution)/shard_map/ppermute | solution.py:515
  63.0 9.4 %collective-permute-start.5 = (f32[8,128]{1,0:T(8,128)S(1)}, f32[8,128]{1,0:T(8,128)S(1)}, u32[]{:S(2)}, u32[]{:S(2)}) collective-permute-start(f32[8,128]{1,0:T(8,128)S(1)} %get-tuple-element.45), channel_id=1, source_target_pairs={{1023,0},{960,1},{961,2},{962,3},{963,4},{964,5},{965,6},{966,7},{... | collective-permute-start | bytes 12296 | tf_op jit(solution)/shard_map/ppermute | solution.py:517
  66.3 8.6 %collective-permute-start.4 = (f32[8,128]{1,0:T(8,128)S(1)}, f32[8,128]{1,0:T(8,128)S(1)}, u32[]{:S(2)}, u32[]{:S(2)}) collective-permute-start(f32[8,128]{1,0:T(8,128)S(1)} %get-tuple-element.45), channel_id=1, source_target_pairs={{0,1},{1,2},{2,3},{3,4},{4,5},{5,6},{6,7},{7,8},{8,9},{9,10},{10,1... | collective-permute-start | bytes 12296 | tf_op jit(solution)/shard_map/ppermute | solution.py:516

commit v6 on v5

--- a/solution.py
+++ b/solution.py
@@ -343,11 +343,15 @@
         send_up[kind : kind + 1] = pairs[4:5]
 
 
-def finish_kernel(near, from_left, from_down, from_across, forces, energies):
+def fold_kernel(near, from_down, out):
     row = lax.broadcasted_iota(jnp.int32, (8, C), 0)
     for kind in range(4):
-        mine = near[kind] + jnp.where(row == 0, from_down[kind : kind + 1], 0.0)
-        theirs = from_left[kind] + jnp.where(row == 0, from_across[kind : kind + 1], 0.0)
+        out[kind] = near[kind] + jnp.where(row == 0, from_down[kind : kind + 1], 0.0)
+
+
+def finish_kernel(near, from_left, forces, energies):
+    for kind in range(4):
+        mine, theirs = near[kind], from_left[kind]
         columns = (
             pltpu.roll(mine, C - 16, 1) + pltpu.roll(theirs, C - 8, 1),
             mine + pltpu.roll(theirs, C - 24, 1),
@@ -468,6 +472,18 @@
     )(*arrays)
 
 
+def fold_call(near, from_down):
+    return pl.pallas_call(
+        fold_kernel,
+        out_shape=jax.ShapeDtypeStruct(near.shape, F32),
+        in_specs=[VMEM] * 2,
+        out_specs=VMEM,
+        compiler_params=pltpu.CompilerParams(vmem_limit_bytes=4 * 1024 * 1024),
+        cost_estimate=pl.CostEstimate(flops=1_000_000_000, bytes_accessed=1000, transcendentals=0),
+        name="fold",
+    )(near, from_down)
+
+
 def finish_call(*arrays):
     return pl.pallas_call(
         finish_kernel,
@@ -475,7 +491,7 @@
             jax.ShapeDtypeStruct((3, 2, 8, 8), F32),
             jax.ShapeDtypeStruct((2, 8, 8), F32),
         ),
-        in_specs=[VMEM] * 4,
+        in_specs=[VMEM] * 2,
         out_specs=(VMEM,) * 2,
         compiler_params=pltpu.CompilerParams(vmem_limit_bytes=4 * 1024 * 1024),
         cost_estimate=pl.CostEstimate(flops=1000, bytes_accessed=1000, transcendentals=0),
@@ -509,13 +525,13 @@
     energy, spread, *last = late_call(plane, first[0], up, across, early, *shared)
     gathered = lax.all_to_all(spread, ("gx",) + outer, 0, 0)
     near, send_up = backward_call(*first, *last, shared[0], energy)
+    from_down = lax.ppermute(send_up, gy, ring(size_y, 1))
     spread = relay_call(gathered, lax.axis_size(inner))
-    spread, near, send_up = lax.optimization_barrier((spread, near, send_up))
+    spread, near = lax.optimization_barrier((spread, near))
     gathered = lax.all_to_all(spread, inner, 0, 0)
+    near = fold_call(near, from_down)
     from_left = lax.ppermute(near, "gx", ring(size_x, 1))
-    from_down = lax.ppermute(send_up, gy, ring(size_y, 1))
-    from_across = lax.ppermute(send_up, ("gx",) + gy, [(j, i) for i, j in corner])
-    forces, slot_energy_values = finish_call(near, from_left, from_down, from_across)
+    forces, slot_energy_values = finish_call(near, from_left)
     return forces, slot_energy_values, jnp.sum(gathered)
 
 

time: 77.1 us -> 72.3 us (0.938)
  starting transfers between devices: 49.2 us -> 45.4 us
    all_to_all x1, waiting for transfers between devices: 0.01 us -> 6.58 us  [on_device(): gathered = lax.all_to_all(spread, inner, 0, 0)]
    ppermute x1 -> x0, starting transfers between devices: 3.27 us -> none  [on_device(): lax.ppermute(send_up, ('gx',) + gy, [(j, i) for i, j in corner])]
    ppermute x1 -> x0, waiting for transfers between devices: 3.07 us -> none  [on_device(): lax.ppermute(send_up, ('gx',) + gy, [(j, i) for i, j in corner])]
    all_to_all x1, waiting for transfers between devices: 6.3 us -> 3.68 us  [on_device(): gathered = lax.all_to_all(spread, ('gx',) + outer, 0, 0)]
    ppermute x1, waiting for transfers between devices: 2.4 us -> 0.01 us  [on_device(): from_down = lax.ppermute(send_up, gy, ring(size_y, 1))]
    ppermute x1, waiting for transfers between devices: 0.01 us -> 0.85 us  [on_device(): from_left = lax.ppermute(near, 'gx', ring(size_x, 1))]
  transfers between devices with their start and end apart: 8 -> 7, of which waited for: 3 -> 3; matrix products, arithmetic and copies ran while one was open for 0% -> 0% of each run, Pallas kernels for 10% -> 12%
where the time goes in v6:
time: 72.3 us; the launch traced here: 71.9 us
  starting transfers between devices  45.4 us (63%)
  Pallas kernels  12.1 us (17%)
  waiting for transfers between devices  11.1 us (15%)
  local copies, waits for them, and re-layouts  1.86 us (3%)
  between operations  0.77 us (1%)
    ppermute x1, starting transfers between devices, on_device(): right = lax.ppermute(own, 'gx', ring(size_x, -1))  16.1 us
    ppermute x1, starting transfers between devices, on_device(): across = lax.ppermute(low, ('gx',) + gy, corner)  11.2 us
    all_to_all x1, waiting for transfers between devices, on_device(): gathered = lax.all_to_all(spread, inner, 0, 0)  6.58 us
    all_to_all x1, starting transfers between devices, on_device(): gathered = lax.all_to_all(spread, ('gx',) + outer, 0, 0)  5.42 us
    all_to_all x1, starting transfers between devices, on_device(): gathered = lax.all_to_all(spread, inner, 0, 0)  4.93 us
    pallas_call x1, Pallas kernels, early_call(): pl.pallas_call(early_kernel, out_shape=(jax.ShapeDtypeStruct((3 * ROWS, C...  4.02 us
    all_to_all x1, waiting for transfers between devices, on_device(): gathered = lax.all_to_all(spread, ('gx',) + outer, 0, 0)  3.68 us
    ppermute x1, starting transfers between devices, on_device(): from_left = lax.ppermute(near, 'gx', ring(size_x, 1))  3.07 us
  transfers between devices with their start and end apart: 7, of which 3 were waited for; matrix products, arithmetic and copies ran while one was open for 0% of the time, Pallas kernels for 12%

profile of v6, /device:TPU:1, one launch (start us, length us, event | category | flops | bytes accessed | tf_op | source)
XLA Modules:
  0.0 71.9 jit_solution(10394126102178148553)
XLA Ops:
  0.6 2.0 %pack.1 = (bf16[2,8,10,8,128]{4,3,2,1,0:T(8,128)(2,1)}, bf16[2,2,10,8,128]{4,3,2,1,0:T(8,128)(2,1)}, f32[24,8,128]{2,1,0:T(8,128)}) custom-call(bf16[2,8,9,8,128]{4,3,2,1,0:T(8,128)(2,1)} %bitcast.2, f32[3,2,8,8]{3,2,1,0:T(8,128)} %places.1, s32[2,8,8]{2,1,0:T(8,128)} %present.1, s32[2,8,8,32]{3,2,1,0:T(8,128)} %lists.1, f32[7,8,128]{2,1,0:T(8,128)} %weight.1, ...), custom_call_target="tpu_custom_call" | custom-call | tf_op jit(solution)/shard_map/pack/pallas_call | solution.py:374
  2.6 16.1 %collective-permute-start = (bf16[2,8,10,8,128]{4,3,2,1,0:T(8,128)(2,1)}, bf16[2,8,10,8,128]{4,3,2,1,0:T(8,128)(2,1)S(1)}, u32[]{:S(2)}, u32[]{:S(2)}) collective-permute-start(bf16[2,8,10,8,128]{4,3,2,1,0:T(8,128)(2,1)} %get-tuple-element.25.own), channel_id=1, source_target_pairs={{0,960},{64,0},{128,64},{192,128},{256,192},{320,256},{384,320},{4... | collective-permute-start | bytes 983048 | tf_op jit(solution)/shard_map/ppermute | solution.py:514
  18.7 11.2 %collective-permute-start.2 = (bf16[2,2,10,8,128]{4,3,2,1,0:T(8,128)(2,1)}, bf16[2,2,10,8,128]{4,3,2,1,0:T(8,128)(2,1)S(1)}, u32[]{:S(2)}, u32[]{:S(2)}) collective-permute-start(bf16[2,2,10,8,128]{4,3,2,1,0:T(8,128)(2,1)} %get-tuple-element.32), channel_id=1, source_target_pairs={{0,1023},{1,960},{2,961},{3,962},{4,963},{5,964},{6,965},{7,966},{... | collective-permute-start | bytes 245768 | tf_op jit(solution)/shard_map/ppermute | solution.py:521
  29.9 2.2 %collective-permute-start.1 = (bf16[2,2,10,8,128]{4,3,2,1,0:T(8,128)(2,1)}, bf16[2,2,10,8,128]{4,3,2,1,0:T(8,128)(2,1)S(1)}, u32[]{:S(2)}, u32[]{:S(2)}) collective-permute-start(bf16[2,2,10,8,128]{4,3,2,1,0:T(8,128)(2,1)} %get-tuple-element.32), channel_id=1, source_target_pairs={{0,63},{1,0},{2,1},{3,2},{4,3},{5,4},{6,5},{7,6},{8,7},{9,8},{10,9... | collective-permute-start | bytes 245768 | tf_op jit(solution)/shard_map/ppermute | solution.py:515
  32.1 0.0 copy-start
  32.1 1.0 %copy-done = bf16[2,8,10,8,128]{4,3,2,1,0:T(8,128)(2,1)S(1)} copy-done((bf16[2,8,10,8,128]{4,3,2,1,0:T(8,128)(2,1)S(1)}, bf16[2,8,10,8,128]{4,3,2,1,0:T(8,128)(2,1)}, u32[]{:S(2)}) %copy-start) | copy-done | bytes 327704
  33.0 0.0 copy-start.1
  33.0 0.9 %copy-done.1 = f32[24,8,128]{2,1,0:T(8,128)S(1)} copy-done((f32[24,8,128]{2,1,0:T(8,128)S(1)}, f32[24,8,128]{2,1,0:T(8,128)}, u32[]{:S(2)}) %copy-start.1) | copy-done | bytes 98328
  34.0 0.0 collective-permute-done.right
  34.0 4.0 %early.1 = (f32[96,128]{1,0:T(8,128)S(1)}, bf16[256,1280]{1,0:T(8,128)(2,1)S(1)}, f32[3,25,32,128]{3,2,1,0:T(8,128)S(1)}, f32[3,9,32,128]{3,2,1,0:T(8,128)S(1)}) custom-call(bf16[2,8,10,8,128]{4,3,2,1,0:T(8,128)(2,1)S(1)} %get-tuple-element.27.own, bf16[2,8,10,8,128]{4,3,2,1,0:T(8,128)(2,1)S(1)} %collective-permute-done.right, ...), custom_call_target="tpu_custom_call" | custom-call | flops 4000000000 | bytes 8000000 | tf_op jit(solution)/shard_map/early/pallas_call | solution.py:423
  38.0 0.0 collective-permute-done.2.across
  38.0 0.0 collective-permute-done.1.up
  38.0 1.8 %late.1 = (f32[8,128]{1,0:T(8,128)S(1)}, f32[64,1,128]{2,1,0:T(1,128)}, bf16[128,1280]{1,0:T(8,128)(2,1)S(1)}, f32[1,25,32,128]{3,2,1,0:T(8,128)S(1)}, f32[1,9,32,128]{3,2,1,0:T(8,128)S(1)}) custom-call(bf16[256,1280]{1,0:T(8,128)(2,1)S(1)} %get-tuple-element.31.known.table, bf16[2,2,10,8,128]{4,3,2,1,0:T(8,128)(2,1)S(1)} %collective-permute-done.1.up, ...), custom_call_target="tpu_custom_call" | custom-call | flops 1000000000 | bytes 2000000 | tf_op jit(solution)/shard_map/late/pallas_call | solution.py:436
  39.9 5.4 %all-to-all-start = ((f32[64,1,128]{2,1,0:T(1,128)}), f32[64,1,128]{2,1,0:T(1,128)S(1)}, u32[]{:S(2)}, u32[]{:S(2)}) async-start(f32[64,1,128]{2,1,0:T(1,128)} %get-tuple-element.34), calls=%async_computation | async-start | bytes 65536 | tf_op jit(solution)/shard_map/all_to_all | solution.py:526
  45.3 2.8 %backward.1 = (f32[4,8,128]{2,1,0:T(8,128)S(1)}, f32[8,128]{1,0:T(8,128)S(1)}) custom-call(bf16[256,1280]{1,0:T(8,128)(2,1)S(1)} %get-tuple-element.31.known.table, f32[3,25,32,128]{3,2,1,0:T(8,128)S(1)} %get-tuple-element.35.edge, f32[3,9,32,128]{3,2,1,0:T(8,128)S(1)} %get-tuple-element.36.back, bf16[128,1280]{1,0:T(8,128)(2,1)S(1)} %get-tuple-element.37.late_table, ...), custom_call_target="tpu_custom_call" | custom-call | flops 4000000000 | bytes 8000000 | tf_op jit(solution)/shard_map/backward/pallas_call | solution.py:463
  48.1 2.6 %collective-permute-start.3 = (f32[8,128]{1,0:T(8,128)S(1)}, f32[8,128]{1,0:T(8,128)S(1)}, u32[]{:S(2)}, u32[]{:S(2)}) collective-permute-start(f32[8,128]{1,0:T(8,128)S(1)} %get-tuple-element.43), channel_id=1, source_target_pairs={{0,1},{1,2},{2,3},{3,4},{4,5},{5,6},{6,7},{7,8},{8,9},{9,10},{10,1... | collective-permute-start | bytes 12296 | tf_op jit(solution)/shard_map/ppermute | solution.py:528
  50.7 3.7 %all-to-all-done.gathered = f32[64,1,128]{2,1,0:T(1,128)S(1)} async-done(((f32[64,1,128]{2,1,0:T(1,128)}), f32[64,1,128]{2,1,0:T(1,128)S(1)}, u32[]{:S(2)}, u32[]{:S(2)}) %all-to-all-start) | async-done | bytes 32800 | tf_op jit(solution)/shard_map/all_to_all | solution.py:526
  54.4 0.7 relay.1
  55.1 4.9 %all-to-all-start.1 = ((f32[16,1,128]{2,1,0:T(1,128)}), f32[16,1,128]{2,1,0:T(1,128)S(1)}, u32[]{:S(2)}, u32[]{:S(2)}) async-start(f32[16,1,128]{2,1,0:T(1,128)} %relay.1), calls=%async_computation.1 | async-start | bytes 16384 | tf_op jit(solution)/shard_map/all_to_all | solution.py:531
  60.0 0.0 collective-permute-done.3.from_down
  60.0 3.1 %collective-permute-start.4 = (f32[4,8,128]{2,1,0:T(8,128)S(1)}, f32[4,8,128]{2,1,0:T(8,128)S(1)}, u32[]{:S(2)}, u32[]{:S(2)}) collective-permute-start(f32[4,8,128]{2,1,0:T(8,128)S(1)} %fold.1.near), channel_id=1, source_target_pairs={{0,64},{64,128},{128,192},{192,256},{256,320},{320,384},{384,448},... | collective-permute-start | bytes 49160 | tf_op jit(solution)/shard_map/ppermute | solution.py:533
  63.1 0.8 %collective-permute-done.4.from_left = f32[4,8,128]{2,1,0:T(8,128)S(1)} collective-permute-done((f32[4,8,128]{2,1,0:T(8,128)S(1)}, f32[4,8,128]{2,1,0:T(8,128)S(1)}, u32[]{:S(2)}, u32[]{:S(2)}) %collective-permute-start.4) | collective-permute-done | bytes 16416 | tf_op jit(solution)/shard_map/ppermute | solution.py:533
  63.9 0.8 %finish.1 = (f32[3,2,8,8]{3,2,1,0:T(8,128)}, f32[2,8,8]{2,1,0:T(8,128)}) custom-call(f32[4,8,128]{2,1,0:T(8,128)S(1)} %fold.1.near, f32[4,8,128]{2,1,0:T(8,128)S(1)} %collective-permute-done.4.from_left), custom_call_target="tpu_custom_call" | custom-call | flops 1000 | bytes 1000 | tf_op jit(solution)/shard_map/finish/pallas_call | solution.py:488
  64.7 6.6 %all-to-all-done.1 = f32[16,1,128]{2,1,0:T(1,128)S(1)} async-done(((f32[16,1,128]{2,1,0:T(1,128)}), f32[16,1,128]{2,1,0:T(1,128)S(1)}, u32[]{:S(2)}, u32[]{:S(2)}) %all-to-all-start.1) | async-done | bytes 8224 | tf_op jit(solution)/shard_map/all_to_all | solution.py:531
  71.3 0.6 reduce_sum.9
  (2 shorter events, 0.0 us)
Async XLA Ops:
  2.6 31.3 %collective-permute-start = (bf16[2,8,10,8,128]{4,3,2,1,0:T(8,128)(2,1)}, bf16[2,8,10,8,128]{4,3,2,1,0:T(8,128)(2,1)S(1)}, u32[]{:S(2)}, u32[]{:S(2)}) collective-permute-start(bf16[2,8,10,8,128]{4,3,2,1,0:T(8,128)(2,1)} %get-tuple-element.25.own), channel_id=1, source_target_pairs={{0,960},{64,0},{128,64},{192,128},{256,192},{320,256},{384,320},{4... | collective-permute-start | bytes 983048 | tf_op jit(solution)/shard_map/ppermute | solution.py:514
  18.7 19.3 %collective-permute-start.2 = (bf16[2,2,10,8,128]{4,3,2,1,0:T(8,128)(2,1)}, bf16[2,2,10,8,128]{4,3,2,1,0:T(8,128)(2,1)S(1)}, u32[]{:S(2)}, u32[]{:S(2)}) collective-permute-start(bf16[2,2,10,8,128]{4,3,2,1,0:T(8,128)(2,1)} %get-tuple-element.32), channel_id=1, source_target_pairs={{0,1023},{1,960},{2,961},{3,962},{4,963},{5,964},{6,965},{7,966},{... | collective-permute-start | bytes 245768 | tf_op jit(solution)/shard_map/ppermute | solution.py:521
  29.9 8.1 %collective-permute-start.1 = (bf16[2,2,10,8,128]{4,3,2,1,0:T(8,128)(2,1)}, bf16[2,2,10,8,128]{4,3,2,1,0:T(8,128)(2,1)S(1)}, u32[]{:S(2)}, u32[]{:S(2)}) collective-permute-start(bf16[2,2,10,8,128]{4,3,2,1,0:T(8,128)(2,1)} %get-tuple-element.32), channel_id=1, source_target_pairs={{0,63},{1,0},{2,1},{3,2},{4,3},{5,4},{6,5},{7,6},{8,7},{9,8},{10,9... | collective-permute-start | bytes 245768 | tf_op jit(solution)/shard_map/ppermute | solution.py:515
  32.1 1.0 %copy-start = (bf16[2,8,10,8,128]{4,3,2,1,0:T(8,128)(2,1)S(1)}, bf16[2,8,10,8,128]{4,3,2,1,0:T(8,128)(2,1)}, u32[]{:S(2)}) copy-start(bf16[2,8,10,8,128]{4,3,2,1,0:T(8,128)(2,1)} %get-tuple-element.25.own) | copy-start | bytes 983044
  33.0 0.9 %copy-start.1 = (f32[24,8,128]{2,1,0:T(8,128)S(1)}, f32[24,8,128]{2,1,0:T(8,128)}, u32[]{:S(2)}) copy-start(f32[24,8,128]{2,1,0:T(8,128)} %get-tuple-element.26.shared) | copy-start | bytes 294916
  39.9 14.5 %all-to-all-start = ((f32[64,1,128]{2,1,0:T(1,128)}), f32[64,1,128]{2,1,0:T(1,128)S(1)}, u32[]{:S(2)}, u32[]{:S(2)}) async-start(f32[64,1,128]{2,1,0:T(1,128)} %get-tuple-element.34), calls=%async_computation | async-start | bytes 65536 | tf_op jit(solution)/shard_map/all_to_all | solution.py:526
  48.1 11.9 %collective-permute-start.3 = (f32[8,128]{1,0:T(8,128)S(1)}, f32[8,128]{1,0:T(8,128)S(1)}, u32[]{:S(2)}, u32[]{:S(2)}) collective-permute-start(f32[8,128]{1,0:T(8,128)S(1)} %get-tuple-element.43), channel_id=1, source_target_pairs={{0,1},{1,2},{2,3},{3,4},{4,5},{5,6},{6,7},{7,8},{8,9},{9,10},{10,1... | collective-permute-start | bytes 12296 | tf_op jit(solution)/shard_map/ppermute | solution.py:528
  55.1 16.2 %all-to-all-start.1 = ((f32[16,1,128]{2,1,0:T(1,128)}), f32[16,1,128]{2,1,0:T(1,128)S(1)}, u32[]{:S(2)}, u32[]{:S(2)}) async-start(f32[16,1,128]{2,1,0:T(1,128)} %relay.1), calls=%async_computation.1 | async-start | bytes 16384 | tf_op jit(solution)/shard_map/all_to_all | solution.py:531
  60.0 3.9 %collective-permute-start.4 = (f32[4,8,128]{2,1,0:T(8,128)S(1)}, f32[4,8,128]{2,1,0:T(8,128)S(1)}, u32[]{:S(2)}, u32[]{:S(2)}) collective-permute-start(f32[4,8,128]{2,1,0:T(8,128)S(1)} %fold.1.near), channel_id=1, source_target_pairs={{0,64},{64,128},{128,192},{192,256},{256,320},{320,384},{384,448},... | collective-permute-start | bytes 49160 | tf_op jit(solution)/shard_map/ppermute | solution.py:533

commit v7 on v6

--- a/solution.py
+++ b/solution.py
@@ -238,7 +238,7 @@
 
 
 def late_kernel(
-    known, up, across, early, weight, mix, out_weight,
+    known, across, up, early, weight, mix, out_weight,
     energy_out, spread_out, table, edge, back,
     energies, geometry, message,
 ):
@@ -522,7 +522,7 @@
     own, *shared = stage_call(own, shared)
     early, *first = early_call(own, right, *shared)
     plane = size_x * lax.axis_size(outer)
-    energy, spread, *last = late_call(plane, first[0], up, across, early, *shared)
+    energy, spread, *last = late_call(plane, first[0], across, up, early, *shared)
     gathered = lax.all_to_all(spread, ("gx",) + outer, 0, 0)
     near, send_up = backward_call(*first, *last, shared[0], energy)
     from_down = lax.ppermute(send_up, gy, ring(size_y, 1))

time: 72.3 us -> 75.8 us (1.048)
  starting transfers between devices: 45.4 us -> 49.2 us
    ppermute x1, starting transfers between devices: 2.18 us -> 8.98 us  [on_device(): up = lax.ppermute(low, gy, ring(size_y, -1))]
    ppermute x1, starting transfers between devices: 11.2 us -> 4.66 us  [on_device(): across = lax.ppermute(low, ('gx',) + gy, corner)]
    all_to_all x1, starting transfers between devices: 4.93 us -> 8.44 us  [on_device(): gathered = lax.all_to_all(spread, inner, 0, 0)]
  transfers between devices with their start and end apart: 7 -> 7, of which waited for: 3 -> 3; matrix products, arithmetic and copies ran while one was open for 0% -> 0% of each run, Pallas kernels for 12% -> 11%
where the time goes in v7:
time: 75.8 us; the launch traced here: 75.4 us
  starting transfers between devices  49.2 us (65%)
  Pallas kernels  12.1 us (16%)
  waiting for transfers between devices  10.9 us (14%)
  local copies, waits for them, and re-layouts  1.86 us (2%)
  between operations  0.77 us (1%)
    ppermute x1, starting transfers between devices, on_device(): right = lax.ppermute(own, 'gx', ring(size_x, -1))  16.1 us
    ppermute x1, starting transfers between devices, on_device(): up = lax.ppermute(low, gy, ring(size_y, -1))  8.98 us
    all_to_all x1, starting transfers between devices, on_device(): gathered = lax.all_to_all(spread, inner, 0, 0)  8.44 us
    all_to_all x1, waiting for transfers between devices, on_device(): gathered = lax.all_to_all(spread, inner, 0, 0)  6.58 us
    all_to_all x1, starting transfers between devices, on_device(): gathered = lax.all_to_all(spread, ('gx',) + outer, 0, 0)  5.1 us
    ppermute x1, starting transfers between devices, on_device(): across = lax.ppermute(low, ('gx',) + gy, corner)  4.66 us
    pallas_call x1, Pallas kernels, early_call(): pl.pallas_call(early_kernel, out_shape=(jax.ShapeDtypeStruct((3 * ROWS, C...  4.02 us
    all_to_all x1, waiting for transfers between devices, on_device(): gathered = lax.all_to_all(spread, ('gx',) + outer, 0, 0)  3.42 us
  transfers between devices with their start and end apart: 7, of which 3 were waited for; matrix products, arithmetic and copies ran while one was open for 0% of the time, Pallas kernels for 11%

profile of v7, /device:TPU:1, one launch (start us, length us, event | category | flops | bytes accessed | tf_op | source)
XLA Modules:
  0.0 75.4 jit_solution(16671271543528952775)
XLA Ops:
  0.6 2.0 %pack.1 = (bf16[2,8,10,8,128]{4,3,2,1,0:T(8,128)(2,1)}, bf16[2,2,10,8,128]{4,3,2,1,0:T(8,128)(2,1)}, f32[24,8,128]{2,1,0:T(8,128)}) custom-call(bf16[2,8,9,8,128]{4,3,2,1,0:T(8,128)(2,1)} %bitcast.2, f32[3,2,8,8]{3,2,1,0:T(8,128)} %places.1, s32[2,8,8]{2,1,0:T(8,128)} %present.1, s32[2,8,8,32]{3,2,1,0:T(8,128)} %lists.1, f32[7,8,128]{2,1,0:T(8,128)} %weight.1, ...), custom_call_target="tpu_custom_call" | custom-call | tf_op jit(solution)/shard_map/pack/pallas_call | solution.py:374
  2.6 16.1 %collective-permute-start = (bf16[2,8,10,8,128]{4,3,2,1,0:T(8,128)(2,1)}, bf16[2,8,10,8,128]{4,3,2,1,0:T(8,128)(2,1)S(1)}, u32[]{:S(2)}, u32[]{:S(2)}) collective-permute-start(bf16[2,8,10,8,128]{4,3,2,1,0:T(8,128)(2,1)} %get-tuple-element.25.own), channel_id=1, source_target_pairs={{0,960},{64,0},{128,64},{192,128},{256,192},{320,256},{384,320},{4... | collective-permute-start | bytes 983048 | tf_op jit(solution)/shard_map/ppermute | solution.py:514
  18.7 9.0 %collective-permute-start.2 = (bf16[2,2,10,8,128]{4,3,2,1,0:T(8,128)(2,1)}, bf16[2,2,10,8,128]{4,3,2,1,0:T(8,128)(2,1)S(1)}, u32[]{:S(2)}, u32[]{:S(2)}) collective-permute-start(bf16[2,2,10,8,128]{4,3,2,1,0:T(8,128)(2,1)} %get-tuple-element.32), channel_id=1, source_target_pairs={{0,63},{1,0},{2,1},{3,2},{4,3},{5,4},{6,5},{7,6},{8,7},{9,8},{10,9... | collective-permute-start | bytes 245768 | tf_op jit(solution)/shard_map/ppermute | solution.py:515
  27.7 4.7 %collective-permute-start.1 = (bf16[2,2,10,8,128]{4,3,2,1,0:T(8,128)(2,1)}, bf16[2,2,10,8,128]{4,3,2,1,0:T(8,128)(2,1)S(1)}, u32[]{:S(2)}, u32[]{:S(2)}) collective-permute-start(bf16[2,2,10,8,128]{4,3,2,1,0:T(8,128)(2,1)} %get-tuple-element.32), channel_id=1, source_target_pairs={{0,1023},{1,960},{2,961},{3,962},{4,963},{5,964},{6,965},{7,966},{... | collective-permute-start | bytes 245768 | tf_op jit(solution)/shard_map/ppermute | solution.py:521
  32.3 0.0 copy-start
  32.3 1.0 %copy-done = bf16[2,8,10,8,128]{4,3,2,1,0:T(8,128)(2,1)S(1)} copy-done((bf16[2,8,10,8,128]{4,3,2,1,0:T(8,128)(2,1)S(1)}, bf16[2,8,10,8,128]{4,3,2,1,0:T(8,128)(2,1)}, u32[]{:S(2)}) %copy-start) | copy-done | bytes 327704
  33.3 0.0 copy-start.1
  33.3 0.9 %copy-done.1 = f32[24,8,128]{2,1,0:T(8,128)S(1)} copy-done((f32[24,8,128]{2,1,0:T(8,128)S(1)}, f32[24,8,128]{2,1,0:T(8,128)}, u32[]{:S(2)}) %copy-start.1) | copy-done | bytes 98328
  34.2 0.0 collective-permute-done.right
  34.2 4.0 %early.1 = (f32[96,128]{1,0:T(8,128)S(1)}, bf16[256,1280]{1,0:T(8,128)(2,1)S(1)}, f32[3,25,32,128]{3,2,1,0:T(8,128)S(1)}, f32[3,9,32,128]{3,2,1,0:T(8,128)S(1)}) custom-call(bf16[2,8,10,8,128]{4,3,2,1,0:T(8,128)(2,1)S(1)} %get-tuple-element.27.own, bf16[2,8,10,8,128]{4,3,2,1,0:T(8,128)(2,1)S(1)} %collective-permute-done.right, ...), custom_call_target="tpu_custom_call" | custom-call | flops 4000000000 | bytes 8000000 | tf_op jit(solution)/shard_map/early/pallas_call | solution.py:423
  38.3 0.0 collective-permute-done.2.up
  38.3 0.0 collective-permute-done.1.across
  38.3 1.8 %late.1 = (f32[8,128]{1,0:T(8,128)S(1)}, f32[64,1,128]{2,1,0:T(1,128)}, bf16[128,1280]{1,0:T(8,128)(2,1)S(1)}, f32[1,25,32,128]{3,2,1,0:T(8,128)S(1)}, f32[1,9,32,128]{3,2,1,0:T(8,128)S(1)}) custom-call(bf16[256,1280]{1,0:T(8,128)(2,1)S(1)} %get-tuple-element.31.known.table, bf16[2,2,10,8,128]{4,3,2,1,0:T(8,128)(2,1)S(1)} %collective-permute-done.1.across, ...), custom_call_target="tpu_custom_call" | custom-call | flops 1000000000 | bytes 2000000 | tf_op jit(solution)/shard_map/late/pallas_call | solution.py:436
  40.1 5.1 %all-to-all-start = ((f32[64,1,128]{2,1,0:T(1,128)}), f32[64,1,128]{2,1,0:T(1,128)S(1)}, u32[]{:S(2)}, u32[]{:S(2)}) async-start(f32[64,1,128]{2,1,0:T(1,128)} %get-tuple-element.34), calls=%async_computation | async-start | bytes 65536 | tf_op jit(solution)/shard_map/all_to_all | solution.py:526
  45.2 2.8 %backward.1 = (f32[4,8,128]{2,1,0:T(8,128)S(1)}, f32[8,128]{1,0:T(8,128)S(1)}) custom-call(bf16[256,1280]{1,0:T(8,128)(2,1)S(1)} %get-tuple-element.31.known.table, f32[3,25,32,128]{3,2,1,0:T(8,128)S(1)} %get-tuple-element.35.edge, f32[3,9,32,128]{3,2,1,0:T(8,128)S(1)} %get-tuple-element.36.back, bf16[128,1280]{1,0:T(8,128)(2,1)S(1)} %get-tuple-element.37.late_table, ...), custom_call_target="tpu_custom_call" | custom-call | flops 4000000000 | bytes 8000000 | tf_op jit(solution)/shard_map/backward/pallas_call | solution.py:463
  48.1 2.9 %collective-permute-start.3 = (f32[8,128]{1,0:T(8,128)S(1)}, f32[8,128]{1,0:T(8,128)S(1)}, u32[]{:S(2)}, u32[]{:S(2)}) collective-permute-start(f32[8,128]{1,0:T(8,128)S(1)} %get-tuple-element.43), channel_id=1, source_target_pairs={{0,1},{1,2},{2,3},{3,4},{4,5},{5,6},{6,7},{7,8},{8,9},{9,10},{10,1... | collective-permute-start | bytes 12296 | tf_op jit(solution)/shard_map/ppermute | solution.py:528
  50.9 3.4 %all-to-all-done.gathered = f32[64,1,128]{2,1,0:T(1,128)S(1)} async-done(((f32[64,1,128]{2,1,0:T(1,128)}), f32[64,1,128]{2,1,0:T(1,128)S(1)}, u32[]{:S(2)}, u32[]{:S(2)}) %all-to-all-start) | async-done | bytes 32800 | tf_op jit(solution)/shard_map/all_to_all | solution.py:526
  54.4 0.7 relay.1
  55.0 8.4 %all-to-all-start.1 = ((f32[16,1,128]{2,1,0:T(1,128)}), f32[16,1,128]{2,1,0:T(1,128)S(1)}, u32[]{:S(2)}, u32[]{:S(2)}) async-start(f32[16,1,128]{2,1,0:T(1,128)} %relay.1), calls=%async_computation.1 | async-start | bytes 16384 | tf_op jit(solution)/shard_map/all_to_all | solution.py:531
  63.5 0.0 collective-permute-done.3.from_down
  63.5 3.1 %collective-permute-start.4 = (f32[4,8,128]{2,1,0:T(8,128)S(1)}, f32[4,8,128]{2,1,0:T(8,128)S(1)}, u32[]{:S(2)}, u32[]{:S(2)}) collective-permute-start(f32[4,8,128]{2,1,0:T(8,128)S(1)} %fold.1.near), channel_id=1, source_target_pairs={{0,64},{64,128},{128,192},{192,256},{256,320},{320,384},{384,448},... | collective-permute-start | bytes 49160 | tf_op jit(solution)/shard_map/ppermute | solution.py:533
  66.6 0.8 %collective-permute-done.4.from_left = f32[4,8,128]{2,1,0:T(8,128)S(1)} collective-permute-done((f32[4,8,128]{2,1,0:T(8,128)S(1)}, f32[4,8,128]{2,1,0:T(8,128)S(1)}, u32[]{:S(2)}, u32[]{:S(2)}) %collective-permute-start.4) | collective-permute-done | bytes 16416 | tf_op jit(solution)/shard_map/ppermute | solution.py:533
  67.4 0.8 %finish.1 = (f32[3,2,8,8]{3,2,1,0:T(8,128)}, f32[2,8,8]{2,1,0:T(8,128)}) custom-call(f32[4,8,128]{2,1,0:T(8,128)S(1)} %fold.1.near, f32[4,8,128]{2,1,0:T(8,128)S(1)} %collective-permute-done.4.from_left), custom_call_target="tpu_custom_call" | custom-call | flops 1000 | bytes 1000 | tf_op jit(solution)/shard_map/finish/pallas_call | solution.py:488
  68.2 6.6 %all-to-all-done.1 = f32[16,1,128]{2,1,0:T(1,128)S(1)} async-done(((f32[16,1,128]{2,1,0:T(1,128)}), f32[16,1,128]{2,1,0:T(1,128)S(1)}, u32[]{:S(2)}, u32[]{:S(2)}) %all-to-all-start.1) | async-done | bytes 8224 | tf_op jit(solution)/shard_map/all_to_all | solution.py:531
  74.8 0.6 reduce_sum.9
  (2 shorter events, 0.0 us)
Async XLA Ops:
  2.6 31.6 %collective-permute-start = (bf16[2,8,10,8,128]{4,3,2,1,0:T(8,128)(2,1)}, bf16[2,8,10,8,128]{4,3,2,1,0:T(8,128)(2,1)S(1)}, u32[]{:S(2)}, u32[]{:S(2)}) collective-permute-start(bf16[2,8,10,8,128]{4,3,2,1,0:T(8,128)(2,1)} %get-tuple-element.25.own), channel_id=1, source_target_pairs={{0,960},{64,0},{128,64},{192,128},{256,192},{320,256},{384,320},{4... | collective-permute-start | bytes 983048 | tf_op jit(solution)/shard_map/ppermute | solution.py:514
  18.7 19.6 %collective-permute-start.2 = (bf16[2,2,10,8,128]{4,3,2,1,0:T(8,128)(2,1)}, bf16[2,2,10,8,128]{4,3,2,1,0:T(8,128)(2,1)S(1)}, u32[]{:S(2)}, u32[]{:S(2)}) collective-permute-start(bf16[2,2,10,8,128]{4,3,2,1,0:T(8,128)(2,1)} %get-tuple-element.32), channel_id=1, source_target_pairs={{0,63},{1,0},{2,1},{3,2},{4,3},{5,4},{6,5},{7,6},{8,7},{9,8},{10,9... | collective-permute-start | bytes 245768 | tf_op jit(solution)/shard_map/ppermute | solution.py:515
  27.7 10.6 %collective-permute-start.1 = (bf16[2,2,10,8,128]{4,3,2,1,0:T(8,128)(2,1)}, bf16[2,2,10,8,128]{4,3,2,1,0:T(8,128)(2,1)S(1)}, u32[]{:S(2)}, u32[]{:S(2)}) collective-permute-start(bf16[2,2,10,8,128]{4,3,2,1,0:T(8,128)(2,1)} %get-tuple-element.32), channel_id=1, source_target_pairs={{0,1023},{1,960},{2,961},{3,962},{4,963},{5,964},{6,965},{7,966},{... | collective-permute-start | bytes 245768 | tf_op jit(solution)/shard_map/ppermute | solution.py:521
  32.3 1.0 %copy-start = (bf16[2,8,10,8,128]{4,3,2,1,0:T(8,128)(2,1)S(1)}, bf16[2,8,10,8,128]{4,3,2,1,0:T(8,128)(2,1)}, u32[]{:S(2)}) copy-start(bf16[2,8,10,8,128]{4,3,2,1,0:T(8,128)(2,1)} %get-tuple-element.25.own) | copy-start | bytes 983044
  33.3 0.9 %copy-start.1 = (f32[24,8,128]{2,1,0:T(8,128)S(1)}, f32[24,8,128]{2,1,0:T(8,128)}, u32[]{:S(2)}) copy-start(f32[24,8,128]{2,1,0:T(8,128)} %get-tuple-element.26.shared) | copy-start | bytes 294916
  40.1 14.2 %all-to-all-start = ((f32[64,1,128]{2,1,0:T(1,128)}), f32[64,1,128]{2,1,0:T(1,128)S(1)}, u32[]{:S(2)}, u32[]{:S(2)}) async-start(f32[64,1,128]{2,1,0:T(1,128)} %get-tuple-element.34), calls=%async_computation | async-start | bytes 65536 | tf_op jit(solution)/shard_map/all_to_all | solution.py:526
  48.1 15.4 %collective-permute-start.3 = (f32[8,128]{1,0:T(8,128)S(1)}, f32[8,128]{1,0:T(8,128)S(1)}, u32[]{:S(2)}, u32[]{:S(2)}) collective-permute-start(f32[8,128]{1,0:T(8,128)S(1)} %get-tuple-element.43), channel_id=1, source_target_pairs={{0,1},{1,2},{2,3},{3,4},{4,5},{5,6},{6,7},{7,8},{8,9},{9,10},{10,1... | collective-permute-start | bytes 12296 | tf_op jit(solution)/shard_map/ppermute | solution.py:528
  55.0 19.7 %all-to-all-start.1 = ((f32[16,1,128]{2,1,0:T(1,128)}), f32[16,1,128]{2,1,0:T(1,128)S(1)}, u32[]{:S(2)}, u32[]{:S(2)}) async-start(f32[16,1,128]{2,1,0:T(1,128)} %relay.1), calls=%async_computation.1 | async-start | bytes 16384 | tf_op jit(solution)/shard_map/all_to_all | solution.py:531
  63.5 3.9 %collective-permute-start.4 = (f32[4,8,128]{2,1,0:T(8,128)S(1)}, f32[4,8,128]{2,1,0:T(8,128)S(1)}, u32[]{:S(2)}, u32[]{:S(2)}) collective-permute-start(f32[4,8,128]{2,1,0:T(8,128)S(1)} %fold.1.near), channel_id=1, source_target_pairs={{0,64},{64,128},{128,192},{192,256},{256,320},{320,384},{384,448},... | collective-permute-start | bytes 49160 | tf_op jit(solution)/shard_map/ppermute | solution.py:533

commit v8 on v6

--- a/solution.py
+++ b/solution.py
@@ -233,8 +233,10 @@
     for m in range(10):
         for y in range(8):
             fill(table, y, m, [own[1, y, m], right[0, y, m], own[0, y, m], right[1, y, m]])
-    step = group_forward(table, weight, mix, out_weight, edge, back, energies, geometry, message)
-    lax.fori_loop(0, GROUPS - 1, step, 0)
+    for q in range(GROUPS - 1):
+        group_forward(
+            table, weight, mix, out_weight, edge, back, energies, geometry.at[q], message.at[q]
+        )(q, 0)
 
 
 def late_kernel(
@@ -425,7 +427,10 @@
         out_shape=(jax.ShapeDtypeStruct((3 * ROWS, C), F32),) + results(3, 256),
         in_specs=[VMEM] * 5,
         out_specs=(VMEM,) * 4,
-        scratch_shapes=SCRATCH,
+        scratch_shapes=[
+            pltpu.VMEM((3, 9, NB * ROWS, C), BF16),
+            pltpu.VMEM((3, 9, ROWS, C), BF16),
+        ],
         compiler_params=pltpu.CompilerParams(vmem_limit_bytes=20 * 1024 * 1024),
         cost_estimate=pl.CostEstimate(flops=4_000_000_000, bytes_accessed=8_000_000, transcendentals=0),
         name="early",

time: 72.3 us -> 72.3 us (level)
  transfers between devices with their start and end apart: 7 -> 7, of which waited for: 3 -> 3; matrix products, arithmetic and copies ran while one was open for 0% -> 0% of each run, Pallas kernels for 12% -> 11%
where the time goes in v8:
time: 72.3 us; the launch traced here: 71.9 us
  starting transfers between devices  46 us (64%)
  Pallas kernels  11.5 us (16%)
  waiting for transfers between devices  11.1 us (15%)
  local copies, waits for them, and re-layouts  1.86 us (3%)
  between operations  0.77 us (1%)
    ppermute x1, starting transfers between devices, on_device(): right = lax.ppermute(own, 'gx', ring(size_x, -1))  16.1 us
    ppermute x1, starting transfers between devices, on_device(): across = lax.ppermute(low, ('gx',) + gy, corner)  11.2 us
    all_to_all x1, waiting for transfers between devices, on_device(): gathered = lax.all_to_all(spread, inner, 0, 0)  6.58 us
    all_to_all x1, starting transfers between devices, on_device(): gathered = lax.all_to_all(spread, inner, 0, 0)  5.54 us
    all_to_all x1, starting transfers between devices, on_device(): gathered = lax.all_to_all(spread, ('gx',) + outer, 0, 0)  5.42 us
    all_to_all x1, waiting for transfers between devices, on_device(): gathered = lax.all_to_all(spread, ('gx',) + outer, 0, 0)  3.7 us
    pallas_call x1, Pallas kernels, early_call(): pl.pallas_call(early_kernel, out_shape=(jax.ShapeDtypeStruct((3 * ROWS, C...  3.41 us
    ppermute x1, starting transfers between devices, on_device(): from_left = lax.ppermute(near, 'gx', ring(size_x, 1))  3.07 us
  transfers between devices with their start and end apart: 7, of which 3 were waited for; matrix products, arithmetic and copies ran while one was open for 0% of the time, Pallas kernels for 11%

profile of v8, /device:TPU:1, one launch (start us, length us, event | category | flops | bytes accessed | tf_op | source)
XLA Modules:
  0.0 71.9 jit_solution(2841608212065929945)
XLA Ops:
  0.6 2.0 %pack.1 = (bf16[2,8,10,8,128]{4,3,2,1,0:T(8,128)(2,1)}, bf16[2,2,10,8,128]{4,3,2,1,0:T(8,128)(2,1)}, f32[24,8,128]{2,1,0:T(8,128)}) custom-call(bf16[2,8,9,8,128]{4,3,2,1,0:T(8,128)(2,1)} %bitcast.2, f32[3,2,8,8]{3,2,1,0:T(8,128)} %places.1, s32[2,8,8]{2,1,0:T(8,128)} %present.1, s32[2,8,8,32]{3,2,1,0:T(8,128)} %lists.1, f32[7,8,128]{2,1,0:T(8,128)} %weight.1, ...), custom_call_target="tpu_custom_call" | custom-call | tf_op jit(solution)/shard_map/pack/pallas_call | solution.py:376
  2.6 16.1 %collective-permute-start = (bf16[2,8,10,8,128]{4,3,2,1,0:T(8,128)(2,1)}, bf16[2,8,10,8,128]{4,3,2,1,0:T(8,128)(2,1)S(1)}, u32[]{:S(2)}, u32[]{:S(2)}) collective-permute-start(bf16[2,8,10,8,128]{4,3,2,1,0:T(8,128)(2,1)} %get-tuple-element.25.own), channel_id=1, source_target_pairs={{0,960},{64,0},{128,64},{192,128},{256,192},{320,256},{384,320},{4... | collective-permute-start | bytes 983048 | tf_op jit(solution)/shard_map/ppermute | solution.py:519
  18.7 11.2 %collective-permute-start.2 = (bf16[2,2,10,8,128]{4,3,2,1,0:T(8,128)(2,1)}, bf16[2,2,10,8,128]{4,3,2,1,0:T(8,128)(2,1)S(1)}, u32[]{:S(2)}, u32[]{:S(2)}) collective-permute-start(bf16[2,2,10,8,128]{4,3,2,1,0:T(8,128)(2,1)} %get-tuple-element.32), channel_id=1, source_target_pairs={{0,1023},{1,960},{2,961},{3,962},{4,963},{5,964},{6,965},{7,966},{... | collective-permute-start | bytes 245768 | tf_op jit(solution)/shard_map/ppermute | solution.py:526
  29.9 2.2 %collective-permute-start.1 = (bf16[2,2,10,8,128]{4,3,2,1,0:T(8,128)(2,1)}, bf16[2,2,10,8,128]{4,3,2,1,0:T(8,128)(2,1)S(1)}, u32[]{:S(2)}, u32[]{:S(2)}) collective-permute-start(bf16[2,2,10,8,128]{4,3,2,1,0:T(8,128)(2,1)} %get-tuple-element.32), channel_id=1, source_target_pairs={{0,63},{1,0},{2,1},{3,2},{4,3},{5,4},{6,5},{7,6},{8,7},{9,8},{10,9... | collective-permute-start | bytes 245768 | tf_op jit(solution)/shard_map/ppermute | solution.py:520
  32.1 0.0 copy-start
  32.1 1.0 %copy-done = bf16[2,8,10,8,128]{4,3,2,1,0:T(8,128)(2,1)S(1)} copy-done((bf16[2,8,10,8,128]{4,3,2,1,0:T(8,128)(2,1)S(1)}, bf16[2,8,10,8,128]{4,3,2,1,0:T(8,128)(2,1)}, u32[]{:S(2)}) %copy-start) | copy-done | bytes 327704
  33.0 0.0 copy-start.1
  33.0 0.9 %copy-done.1 = f32[24,8,128]{2,1,0:T(8,128)S(1)} copy-done((f32[24,8,128]{2,1,0:T(8,128)S(1)}, f32[24,8,128]{2,1,0:T(8,128)}, u32[]{:S(2)}) %copy-start.1) | copy-done | bytes 98328
  34.0 0.0 collective-permute-done.right
  34.0 3.4 %early.1 = (f32[96,128]{1,0:T(8,128)S(1)}, bf16[256,1280]{1,0:T(8,128)(2,1)S(1)}, f32[3,25,32,128]{3,2,1,0:T(8,128)S(1)}, f32[3,9,32,128]{3,2,1,0:T(8,128)S(1)}) custom-call(bf16[2,8,10,8,128]{4,3,2,1,0:T(8,128)(2,1)S(1)} %get-tuple-element.27.own, bf16[2,8,10,8,128]{4,3,2,1,0:T(8,128)(2,1)S(1)} %collective-permute-done.right, ...), custom_call_target="tpu_custom_call" | custom-call | flops 4000000000 | bytes 8000000 | tf_op jit(solution)/shard_map/early/pallas_call | solution.py:425
  37.4 0.0 collective-permute-done.2.across
  37.4 0.0 collective-permute-done.1.up
  37.4 1.8 %late.1 = (f32[8,128]{1,0:T(8,128)S(1)}, f32[64,1,128]{2,1,0:T(1,128)}, bf16[128,1280]{1,0:T(8,128)(2,1)S(1)}, f32[1,25,32,128]{3,2,1,0:T(8,128)S(1)}, f32[1,9,32,128]{3,2,1,0:T(8,128)S(1)}) custom-call(bf16[256,1280]{1,0:T(8,128)(2,1)S(1)} %get-tuple-element.31.known.table, bf16[2,2,10,8,128]{4,3,2,1,0:T(8,128)(2,1)S(1)} %collective-permute-done.1.up, ...), custom_call_target="tpu_custom_call" | custom-call | flops 1000000000 | bytes 2000000 | tf_op jit(solution)/shard_map/late/pallas_call | solution.py:441
  39.2 5.4 %all-to-all-start = ((f32[64,1,128]{2,1,0:T(1,128)}), f32[64,1,128]{2,1,0:T(1,128)S(1)}, u32[]{:S(2)}, u32[]{:S(2)}) async-start(f32[64,1,128]{2,1,0:T(1,128)} %get-tuple-element.34), calls=%async_computation | async-start | bytes 65536 | tf_op jit(solution)/shard_map/all_to_all | solution.py:531
  44.7 2.8 %backward.1 = (f32[4,8,128]{2,1,0:T(8,128)S(1)}, f32[8,128]{1,0:T(8,128)S(1)}) custom-call(bf16[256,1280]{1,0:T(8,128)(2,1)S(1)} %get-tuple-element.31.known.table, f32[3,25,32,128]{3,2,1,0:T(8,128)S(1)} %get-tuple-element.35.edge, f32[3,9,32,128]{3,2,1,0:T(8,128)S(1)} %get-tuple-element.36.back, bf16[128,1280]{1,0:T(8,128)(2,1)S(1)} %get-tuple-element.37.late_table, ...), custom_call_target="tpu_custom_call" | custom-call | flops 4000000000 | bytes 8000000 | tf_op jit(solution)/shard_map/backward/pallas_call | solution.py:468
  47.5 2.6 %collective-permute-start.3 = (f32[8,128]{1,0:T(8,128)S(1)}, f32[8,128]{1,0:T(8,128)S(1)}, u32[]{:S(2)}, u32[]{:S(2)}) collective-permute-start(f32[8,128]{1,0:T(8,128)S(1)} %get-tuple-element.43), channel_id=1, source_target_pairs={{0,1},{1,2},{2,3},{3,4},{4,5},{5,6},{6,7},{7,8},{8,9},{9,10},{10,1... | collective-permute-start | bytes 12296 | tf_op jit(solution)/shard_map/ppermute | solution.py:533
  50.1 3.7 %all-to-all-done.gathered = f32[64,1,128]{2,1,0:T(1,128)S(1)} async-done(((f32[64,1,128]{2,1,0:T(1,128)}), f32[64,1,128]{2,1,0:T(1,128)S(1)}, u32[]{:S(2)}, u32[]{:S(2)}) %all-to-all-start) | async-done | bytes 32800 | tf_op jit(solution)/shard_map/all_to_all | solution.py:531
  53.8 0.7 relay.1
  54.5 5.5 %all-to-all-start.1 = ((f32[16,1,128]{2,1,0:T(1,128)}), f32[16,1,128]{2,1,0:T(1,128)S(1)}, u32[]{:S(2)}, u32[]{:S(2)}) async-start(f32[16,1,128]{2,1,0:T(1,128)} %relay.1), calls=%async_computation.1 | async-start | bytes 16384 | tf_op jit(solution)/shard_map/all_to_all | solution.py:536
  60.0 0.0 collective-permute-done.3.from_down
  60.0 3.1 %collective-permute-start.4 = (f32[4,8,128]{2,1,0:T(8,128)S(1)}, f32[4,8,128]{2,1,0:T(8,128)S(1)}, u32[]{:S(2)}, u32[]{:S(2)}) collective-permute-start(f32[4,8,128]{2,1,0:T(8,128)S(1)} %fold.1.near), channel_id=1, source_target_pairs={{0,64},{64,128},{128,192},{192,256},{256,320},{320,384},{384,448},... | collective-permute-start | bytes 49160 | tf_op jit(solution)/shard_map/ppermute | solution.py:538
  63.1 0.8 %collective-permute-done.4.from_left = f32[4,8,128]{2,1,0:T(8,128)S(1)} collective-permute-done((f32[4,8,128]{2,1,0:T(8,128)S(1)}, f32[4,8,128]{2,1,0:T(8,128)S(1)}, u32[]{:S(2)}, u32[]{:S(2)}) %collective-permute-start.4) | collective-permute-done | bytes 16416 | tf_op jit(solution)/shard_map/ppermute | solution.py:538
  63.9 0.8 %finish.1 = (f32[3,2,8,8]{3,2,1,0:T(8,128)}, f32[2,8,8]{2,1,0:T(8,128)}) custom-call(f32[4,8,128]{2,1,0:T(8,128)S(1)} %fold.1.near, f32[4,8,128]{2,1,0:T(8,128)S(1)} %collective-permute-done.4.from_left), custom_call_target="tpu_custom_call" | custom-call | flops 1000 | bytes 1000 | tf_op jit(solution)/shard_map/finish/pallas_call | solution.py:493
  64.7 6.6 %all-to-all-done.1 = f32[16,1,128]{2,1,0:T(1,128)S(1)} async-done(((f32[16,1,128]{2,1,0:T(1,128)}), f32[16,1,128]{2,1,0:T(1,128)S(1)}, u32[]{:S(2)}, u32[]{:S(2)}) %all-to-all-start.1) | async-done | bytes 8224 | tf_op jit(solution)/shard_map/all_to_all | solution.py:536
  71.3 0.6 reduce_sum.9
  (2 shorter events, 0.0 us)
Async XLA Ops:
  2.6 31.3 %collective-permute-start = (bf16[2,8,10,8,128]{4,3,2,1,0:T(8,128)(2,1)}, bf16[2,8,10,8,128]{4,3,2,1,0:T(8,128)(2,1)S(1)}, u32[]{:S(2)}, u32[]{:S(2)}) collective-permute-start(bf16[2,8,10,8,128]{4,3,2,1,0:T(8,128)(2,1)} %get-tuple-element.25.own), channel_id=1, source_target_pairs={{0,960},{64,0},{128,64},{192,128},{256,192},{320,256},{384,320},{4... | collective-permute-start | bytes 983048 | tf_op jit(solution)/shard_map/ppermute | solution.py:519
  18.7 18.7 %collective-permute-start.2 = (bf16[2,2,10,8,128]{4,3,2,1,0:T(8,128)(2,1)}, bf16[2,2,10,8,128]{4,3,2,1,0:T(8,128)(2,1)S(1)}, u32[]{:S(2)}, u32[]{:S(2)}) collective-permute-start(bf16[2,2,10,8,128]{4,3,2,1,0:T(8,128)(2,1)} %get-tuple-element.32), channel_id=1, source_target_pairs={{0,1023},{1,960},{2,961},{3,962},{4,963},{5,964},{6,965},{7,966},{... | collective-permute-start | bytes 245768 | tf_op jit(solution)/shard_map/ppermute | solution.py:526
  29.9 7.5 %collective-permute-start.1 = (bf16[2,2,10,8,128]{4,3,2,1,0:T(8,128)(2,1)}, bf16[2,2,10,8,128]{4,3,2,1,0:T(8,128)(2,1)S(1)}, u32[]{:S(2)}, u32[]{:S(2)}) collective-permute-start(bf16[2,2,10,8,128]{4,3,2,1,0:T(8,128)(2,1)} %get-tuple-element.32), channel_id=1, source_target_pairs={{0,63},{1,0},{2,1},{3,2},{4,3},{5,4},{6,5},{7,6},{8,7},{9,8},{10,9... | collective-permute-start | bytes 245768 | tf_op jit(solution)/shard_map/ppermute | solution.py:520
  32.1 1.0 %copy-start = (bf16[2,8,10,8,128]{4,3,2,1,0:T(8,128)(2,1)S(1)}, bf16[2,8,10,8,128]{4,3,2,1,0:T(8,128)(2,1)}, u32[]{:S(2)}) copy-start(bf16[2,8,10,8,128]{4,3,2,1,0:T(8,128)(2,1)} %get-tuple-element.25.own) | copy-start | bytes 983044
  33.0 0.9 %copy-start.1 = (f32[24,8,128]{2,1,0:T(8,128)S(1)}, f32[24,8,128]{2,1,0:T(8,128)}, u32[]{:S(2)}) copy-start(f32[24,8,128]{2,1,0:T(8,128)} %get-tuple-element.26.shared) | copy-start | bytes 294916
  39.2 14.5 %all-to-all-start = ((f32[64,1,128]{2,1,0:T(1,128)}), f32[64,1,128]{2,1,0:T(1,128)S(1)}, u32[]{:S(2)}, u32[]{:S(2)}) async-start(f32[64,1,128]{2,1,0:T(1,128)} %get-tuple-element.34), calls=%async_computation | async-start | bytes 65536 | tf_op jit(solution)/shard_map/all_to_all | solution.py:531
  47.5 12.5 %collective-permute-start.3 = (f32[8,128]{1,0:T(8,128)S(1)}, f32[8,128]{1,0:T(8,128)S(1)}, u32[]{:S(2)}, u32[]{:S(2)}) collective-permute-start(f32[8,128]{1,0:T(8,128)S(1)} %get-tuple-element.43), channel_id=1, source_target_pairs={{0,1},{1,2},{2,3},{3,4},{4,5},{5,6},{6,7},{7,8},{8,9},{9,10},{10,1... | collective-permute-start | bytes 12296 | tf_op jit(solution)/shard_map/ppermute | solution.py:533
  54.5 16.8 %all-to-all-start.1 = ((f32[16,1,128]{2,1,0:T(1,128)}), f32[16,1,128]{2,1,0:T(1,128)S(1)}, u32[]{:S(2)}, u32[]{:S(2)}) async-start(f32[16,1,128]{2,1,0:T(1,128)} %relay.1), calls=%async_computation.1 | async-start | bytes 16384 | tf_op jit(solution)/shard_map/all_to_all | solution.py:536
  60.0 3.9 %collective-permute-start.4 = (f32[4,8,128]{2,1,0:T(8,128)S(1)}, f32[4,8,128]{2,1,0:T(8,128)S(1)}, u32[]{:S(2)}, u32[]{:S(2)}) collective-permute-start(f32[4,8,128]{2,1,0:T(8,128)S(1)} %fold.1.near), channel_id=1, source_target_pairs={{0,64},{64,128},{128,192},{192,256},{256,320},{320,384},{384,448},... | collective-permute-start | bytes 49160 | tf_op jit(solution)/shard_map/ppermute | solution.py:538
